TPU v7x, 32 devices: a whole 2x2x4 slice. The times are simulated.
32 devices in a mesh: rows: 8 (over z, x), sub: 4 (over y, core).
Axes of the slice: x: 2, y: 2, z: 4, core: 2. Of those that a mesh axis runs over, the one named last changes fastest.
Arguments:
- diag_blocks: bfloat16 [512, 128, 128], P(('rows', 'sub')), may hold values from -1 to 4
- off_blocks: bfloat16 [512, 8, 128, 128], P(('rows', 'sub')), may hold values from -0.5 to 0.5
- col_blocks: int32 [512, 8], P(('rows', 'sub')), may hold values from 0 to 511, as said below
- sketch: bfloat16 [65536, 256], P(('rows', 'sub')), may hold values from -6 to 6
Outputs:
- basis: float32 [65536, 256], P(('rows', 'sub'))
- factor: float32 [256, 256], replicated
Inputs may be any that keep to these rules, and one draw needn't show every extreme that they name: `col_blocks`: in the 128 entries of the rows of one device (16 block rows), at most 8 lie in the range of any one device's 16 block rows; in every draw the range of some device receives exactly 8 from every device.
All inputs are finite; a program needn't handle non-finite values.
Results may differ from a plain program's by a relative error of at most 0.002.
Values may be sent and summed in bfloat16 or wider, within the bound.
No kernel may reach another device: no remote copies, remote signals or barrier semaphores. Data moves between devices by JAX's collectives and lax.ppermute only.
A program may use at most 256 MiB of HBM per device.

v0:
```python
import jax
import jax.numpy as jnp
from jax import lax
from jax.sharding import PartitionSpec as P


def send_out(outgoing, labels):
    received, tags = (
        lax.all_to_all(outgoing, ("rows", "sub"), split_axis=0, concat_axis=0, tiled=True),
        lax.all_to_all(labels, ("rows", "sub"), split_axis=0, concat_axis=0, tiled=True),
    )
    return (received, tags)


def send_back(reply):
    answered = lax.all_to_all(reply, ("rows", "sub"), split_axis=0, concat_axis=0, tiled=True)
    return answered


def on_device(diag_blocks, off_blocks, col_blocks, sketch):
    block_rows, per_row = col_blocks.shape
    edge = diag_blocks.shape[1]
    columns = sketch.shape[1]
    peers = lax.axis_size(("rows", "sub"))
    most = max(2, (2 * block_rows * per_row + peers - 1) // peers)
    requests = block_rows * per_row
    target_positions = peers * most
    flat = col_blocks.reshape(requests)
    owners = flat // block_rows
    local_id = flat % block_rows
    order = jnp.arange(requests)
    earlier = (owners[:, None] == owners[None, :]) & (order[None, :] < order[:, None])
    ranks = jnp.sum(earlier.astype(jnp.int32), axis=1)
    where_to = owners * most + ranks
    omega = sketch.reshape(block_rows, edge, columns)
    mirror = jnp.einsum("bkji,bjc->bkic", off_blocks, omega, preferred_element_type=jnp.float32)
    mirror = mirror.astype(jnp.bfloat16).reshape(requests, edge, columns)
    outgoing = jnp.zeros((target_positions, edge, columns), jnp.bfloat16).at[where_to].set(mirror)
    labels = (
        jnp.full((target_positions,), -1.0, jnp.float32)
        .at[where_to]
        .set(local_id.astype(jnp.float32))
    )
    labels = labels.astype(jnp.bfloat16)
    received, tags = send_out(
        outgoing.reshape(peers, most, edge, columns), labels.reshape(peers, most)
    )
    near = jnp.einsum("bij,bjc->bic", diag_blocks, omega, preferred_element_type=jnp.float32)
    selector = (
        tags.reshape(target_positions).astype(jnp.int32)[None, :] == jnp.arange(block_rows)[:, None]
    ).astype(jnp.bfloat16)
    returned = jnp.dot(
        selector,
        received.reshape(target_positions, edge * columns),
        preferred_element_type=jnp.float32,
    )
    returned = returned.reshape(block_rows, edge, columns)
    reply = jnp.einsum(
        "rs,rk->sk",
        selector,
        omega.reshape(block_rows, edge * columns),
        preferred_element_type=jnp.float32,
    )
    reply = reply.astype(jnp.bfloat16).reshape(peers, most, edge, columns)
    answered = send_back(reply).reshape(target_positions, edge, columns)
    fetched = answered[where_to]
    far = jnp.einsum(
        "nij,njc->nic",
        off_blocks.reshape(requests, edge, edge),
        fetched,
        preferred_element_type=jnp.float32,
    )
    far = far.reshape(block_rows, per_row, edge, columns).sum(axis=1)
    image = (near + far + returned).reshape(block_rows * edge, columns)
    total_rows = block_rows * edge * peers
    gram_local = (
        jnp.dot(image.T, image, precision=lax.Precision.HIGHEST, preferred_element_type=jnp.float32)
        / total_rows
    )
    gram = lax.psum(gram_local, ("rows", "sub"))
    lower = jnp.linalg.cholesky(gram)
    upper = lower.T
    basis = lax.linalg.triangular_solve(lower, image, left_side=False, lower=True, transpose_a=True)
    return (basis, upper)


def solution(mesh):
    placed = (
        P(("rows", "sub"), None, None),
        P(("rows", "sub"), None, None, None),
        P(("rows", "sub"), None),
        P(("rows", "sub"), None),
    )
    return jax.shard_map(
        on_device,
        mesh=mesh,
        in_specs=placed,
        out_specs=(P(("rows", "sub"), None), P()),
        check_vma=False,
    )
```

profile of v0, /device:TPU:0, one launch (start us, length us, event | category | flops | bytes accessed | tf_op | source)
XLA Modules:
  0.0 1053.3 jit_solution(9912018516112709183)
XLA Ops:
  10.1 7.3 all-to-all-start
  17.4 8.1 convolution_convert_fusion.1
  25.5 6.0 broadcast_in_dim.6
  31.4 23.3 %scatter_fusion = bf16[256,128,256]{2,1,0:T(8,128)(2,1)} fusion(bf16[256,128,256]{2,1,0:T(8,128)(2,1)} %broadcast_in_dim.6, s32[128]{0:T(128)S(1)} %fusion.18, bf16[128,128,256]{2,1,0:T(8,128)(2,1)} %bitcast.81), kind=kCustom, calls=%fused_computation.2 | custom fusion | bytes 25166336 | tf_op jit(solution)/shard_map/scatter | solution.py:38
  54.8 6.0 all-to-all-start.2
  61.5 4.8 convolution_convert_fusion
  66.3 7.9 copy.44
  74.2 352.3 %all-to-all-done.2 = bf16[32,8,128,256]{3,2,1,0:T(8,128)(2,1)} async-done(((bf16[32,8,128,256]{3,2,1,0:T(8,128)(2,1)}), bf16[32,8,128,256]{3,2,1,0:T(8,128)(2,1)}, u32[]{:S(2)}, u32[]{:S(2)}) %all-to-all-start.2) | async-done | bytes 16777248 | tf_op jit(solution)/shard_map/all_to_all | solution.py:9
  426.5 16.1 %all-to-all-start.1 = ((bf16[32,8,128,256]{3,2,1,0:T(8,128)(2,1)}), bf16[32,8,128,256]{3,2,1,0:T(8,128)(2,1)}, u32[]{:S(2)}, u32[]{:S(2)}) async-start(bf16[32,8,128,256]{3,2,1,0:T(8,128)(2,1)} %copy.44), calls=%async_computation.1 | async-start | bytes 33554432 | tf_op jit(solution)/shard_map/all_to_all | solution.py:16
  442.9 17.8 %copy.61 = bf16[32,8,128,256]{3,1,2,0:T(8,128)(2,1)} copy(bf16[32,8,128,256]{3,2,1,0:T(8,128)(2,1)} %all-to-all-done.2) | data formatting | bytes 33554432
  460.7 22.4 %copy.48 = bf16[32768,256]{1,0:T(8,128)(2,1)} copy(bf16[32768,256]{0,1:T(8,128)(2,1)} %bitcast.80) | data formatting | bytes 33554432 | tf_op jit(solution)/shard_map/dot_general | solution.py:52
  483.1 11.5 %fusion.13 = f32[16,128,256]{2,0,1:T(8,128)} fusion(bf16[128,256,256]{2,1,0:T(8,128)(2,1)} %bitcast.78, s32[256]{0:T(256)S(1)} %reshape.224), kind=kOutput, calls=%fused_computation.40 | convolution fusion | flops 268439552 | bytes 18875392 | tf_op jit(solution)/shard_map/dot_general | solution.py:52
  494.6 313.7 %all-to-all-done.1 = bf16[32,8,128,256]{3,2,1,0:T(8,128)(2,1)} async-done(((bf16[32,8,128,256]{3,2,1,0:T(8,128)(2,1)}), bf16[32,8,128,256]{3,2,1,0:T(8,128)(2,1)}, u32[]{:S(2)}, u32[]{:S(2)}) %all-to-all-start.1) | async-done | bytes 16777248 | tf_op jit(solution)/shard_map/all_to_all | solution.py:16
  808.3 12.3 %gather_fusion = bf16[128,128,256]{2,1,0:T(8,128)(2,1)} fusion(bf16[256,128,256]{2,1,0:T(8,128)(2,1)} %bitcast.4, s32[1024]{0:T(1024)S(1)} %pad_clamp_fusion), kind=kCustom, calls=%fused_computation | custom fusion | bytes 16777728 | tf_op jit(solution)/shard_map/gather | solution.py:66
  820.6 9.7 bitcast_reduce_fusion
  830.4 2.1 copy.46
  832.4 3.9 copy_add_fusion
  836.4 4.2 fusion
  840.6 136.5 %all-reduce.3.cloned.1.call-done = f32[256,256]{0,1:T(8,128)} async-done(((f32[256,256]{0,1:T(8,128)}), f32[256,256]{0,1:T(8,128)}) %all-reduce.3.cloned.1.call-update) | async-done | bytes 262160 | tf_op jit(solution)/shard_map/psum | solution.py:80
  979.2 11.7 %cholesky.50 = f32[128,128]{1,0:T(8,128)S(1)} custom-call(f32[128,128]{1,0:T(8,128)S(1)} %cholesky.118), custom_call_target="Cholesky" | custom-call | tf_op jit(solution)/shard_map/jit(cholesky)/cholesky | solution.py:81
  991.0 9.8 custom-call.14
  1001.3 12.0 %cholesky.105 = f32[128,128]{1,0:T(8,128)S(1)} custom-call(f32[128,128]{1,0:T(8,128)S(1)} %convolution_subtract_fusion.1), custom_call_target="Cholesky" | custom-call | tf_op jit(solution)/shard_map/jit(cholesky)/cholesky | solution.py:81
  1015.5 4.1 while.1
  1019.6 19.7 %custom-call.15 = f32[2,128,128]{1,2,0:T(8,128)S(1)} custom-call(f32[2,128,128]{2,1,0:T(8,128)S(1)} %get-tuple-element.9), custom_call_target="InvertDiagBlocksLowerTriangular" | custom-call | tf_op jit(solution)/shard_map/triangular_solve | solution.py:83
  (45 shorter events, 18.1 us)
Async XLA Ops:
  7.2 825.3 %copy-start = (bf16[16,128,128]{2,1,0:T(8,128)(2,1)S(1)}, bf16[16,128,128]{2,1,0:T(8,128)(2,1)}, u32[]{:S(2)}) copy-start(bf16[16,128,128]{2,1,0:T(8,128)(2,1)} %param.4) | copy-start | bytes 1572868
  10.1 44.7 %all-to-all-start = ((bf16[32,1,8]{2,1,0:T(2,128)(2,1)}), bf16[32,1,8]{2,1,0:T(2,128)(2,1)S(1)}, u32[]{:S(2)}, u32[]{:S(2)}) async-start(bf16[32,1,8]{2,1,0:T(2,128)(2,1)} %all_to_all.16), calls=%async_computation | async-start | bytes 32768 | tf_op jit(solution)/shard_map/all_to_all | solution.py:10
  54.8 6.0 copy-start.1
  54.8 371.7 %all-to-all-start.2 = ((bf16[32,8,128,256]{3,2,1,0:T(8,128)(2,1)}), bf16[32,8,128,256]{3,2,1,0:T(8,128)(2,1)}, u32[]{:S(2)}, u32[]{:S(2)}) async-start(bf16[32,8,128,256]{3,2,1,0:T(8,128)(2,1)} %bitcast.77), calls=%async_computation.2 | async-start | bytes 33554432 | tf_op jit(solution)/shard_map/all_to_all | solution.py:9
  426.5 381.8 %all-to-all-start.1 = ((bf16[32,8,128,256]{3,2,1,0:T(8,128)(2,1)}), bf16[32,8,128,256]{3,2,1,0:T(8,128)(2,1)}, u32[]{:S(2)}, u32[]{:S(2)}) async-start(bf16[32,8,128,256]{3,2,1,0:T(8,128)(2,1)} %copy.44), calls=%async_computation.1 | async-start | bytes 33554432 | tf_op jit(solution)/shard_map/all_to_all | solution.py:16
  442.6 534.5 %all-reduce.3.cloned.1.call-start = ((), (), s32[]{:S(2)}) async-start(), calls=%async_computation.3 | async-start | bytes 524288 | tf_op jit(solution)/shard_map/psum | solution.py:80
Sparse Core Ops, SparseCore 0:
  840.7 136.3 all-reduce.2
where the time goes:
time: 1060 us; the launch traced here: 1050 us
  waiting for transfers between devices  803 us (76%)
  local copies, waits for them, and re-layouts  103 us (10%)
  other arithmetic  55.4 us (5%)
  matrix products  46.7 us (4%)
  starting transfers between devices  29.6 us (3%)
  between operations  16.1 us (2%)
    all_to_all x1, waiting for transfers between devices, send_out(): lax.all_to_all(outgoing, ('rows', 'sub'), split_axis=0, concat_axis=0, ti...  352 us
    all_to_all x1, waiting for transfers between devices, send_back(): lax.all_to_all(reply, ('rows', 'sub'), split_axis=0, concat_axis=0, tiled...  314 us
    psum x1, waiting for transfers between devices, on_device(): gram = lax.psum(gram_local, ('rows', 'sub'))  137 us
    another operation x6, other arithmetic, on_device(): lower = jnp.linalg.cholesky(gram)  34.3 us
    scatter x1, local copies, waits for them, and re-layouts, on_device(): jnp.zeros((target_positions, edge, columns), jnp.bfloat16).at[where_to]  23.3 us
    dot_general x1, local copies, waits for them, and re-layouts, on_device(): jnp.dot(selector, received.reshape(target_positions, edge * columns), pre...  22.4 us
    unnamed x8, local copies, waits for them, and re-layouts  21.3 us
  transfers between devices with their start and end apart: 4, of which 3 were waited for; matrix products, arithmetic and copies ran while one was open for 10% of the time, Pallas kernels for 0%

commit v1 on v0

v1 whole, which is shorter than its diff:
```python
import functools
import math

import jax
import jax.numpy as jnp
from jax import lax
from jax.experimental import pallas as pl
from jax.experimental.pallas import tpu as pltpu
from jax.sharding import Mesh
from jax.sharding import PartitionSpec as P

LINE = "z"
PLANE = ("x", "y", "c")
ALL = (LINE,) + PLANE
VMEM_LIMIT = 48 * 1024 * 1024
TAIL = 16


def dot(a, b, contract=((1,), (0,)), precision=None):
    return lax.dot_general(
        a, b, (contract, ((), ())), precision=precision, preferred_element_type=jnp.float32
    )


def params():
    return pltpu.CompilerParams(vmem_limit_bytes=VMEM_LIMIT)


def pack_kernel(plane_ref, slot_ref, off_ref, label_ref, out_ref, sem, label_sem):
    count, edge, _ = off_ref.shape
    tail = label_ref.shape[1]
    last = out_ref.shape[1] - tail
    labels = pltpu.make_async_copy(label_ref, out_ref.at[:, pl.ds(last, tail), :], label_sem)
    labels.start()

    def send(entry, carry):
        row = pl.multiple_of(slot_ref[entry] * edge, edge)
        pltpu.make_async_copy(
            off_ref.at[entry], out_ref.at[plane_ref[entry], pl.ds(row, edge), :], sem
        ).start()
        return carry

    lax.fori_loop(0, count, send, 0)
    pltpu.make_async_copy(off_ref, off_ref, sem).wait()
    labels.wait()


def pack(off, to_plane, to_slot, labels, slots):
    count, edge, _ = off.shape
    planes, tail, _ = labels.shape
    return pl.pallas_call(
        pack_kernel,
        out_shape=jax.ShapeDtypeStruct((planes, slots * edge + tail, edge), off.dtype),
        grid_spec=pltpu.PrefetchScalarGridSpec(
            num_scalar_prefetch=2,
            grid=(),
            in_specs=[pl.BlockSpec(memory_space=pl.ANY), pl.BlockSpec(memory_space=pl.ANY)],
            out_specs=pl.BlockSpec(memory_space=pl.ANY),
            scratch_shapes=[pltpu.SemaphoreType.DMA, pltpu.SemaphoreType.DMA],
        ),
        compiler_params=params(),
        name="pack",
    )(to_plane, to_slot, off, labels)


def mirror_kernel(shift, most, row_ref, col_ref, block_ref, omega_ref, out_ref, total):
    source = pl.program_id(0)
    edge = block_ref.shape[2]

    @pl.when(source == 0)
    def _():
        total[...] = jnp.zeros_like(total)

    def one(m, carry):
        row = row_ref[source, shift * most + m]
        col = col_ref[source, shift * most + m]

        @pl.when(row >= 0)
        def _():
            block = block_ref[0, pl.ds(pl.multiple_of(m * edge, edge), edge), :]
            omega = omega_ref[0, pl.ds(pl.multiple_of(row * edge, edge), edge), :]
            total[col] += dot(block, omega, ((0,), (0,)))

        return carry

    lax.fori_loop(0, most, one, 0)

    @pl.when(source == pl.num_programs(0) - 1)
    def _():
        out_ref[...] = total[...].reshape(out_ref.shape).astype(out_ref.dtype)


def mirror_sum(blocks, omegas, rows, cols, shift, most, block_rows, dtype):
    planes, _, edge = blocks.shape
    _, height, columns = omegas.shape
    return pl.pallas_call(
        functools.partial(mirror_kernel, shift, most),
        out_shape=jax.ShapeDtypeStruct((height, columns), dtype),
        grid_spec=pltpu.PrefetchScalarGridSpec(
            num_scalar_prefetch=2,
            grid=(planes,),
            in_specs=[
                pl.BlockSpec((1, most * edge, edge), lambda p, *_: (p, shift, 0)),
                pl.BlockSpec((1, height, columns), lambda p, *_: (p, 0, 0)),
            ],
            out_specs=pl.BlockSpec((height, columns), lambda p, *_: (0, 0)),
            scratch_shapes=[pltpu.VMEM((block_rows, edge, columns), jnp.float32)],
        ),
        compiler_params=params(),
        cost_estimate=pl.CostEstimate(
            flops=2 * planes * most * edge * edge * columns,
            bytes_accessed=planes * (most * edge * edge + height * columns) * 2,
            transcendentals=0,
        ),
        name="mirror",
    )(rows, cols, blocks, omegas)


def far_kernel(most, row_ref, col_ref, block_ref, *rest):
    *omega_refs, out_ref, total = rest
    source = pl.program_id(0)
    edge = block_ref.shape[2]
    total[...] = jnp.zeros_like(total)
    for shift, omega_ref in enumerate(omega_refs):

        def one(m, carry, shift=shift, omega_ref=omega_ref):
            slot = shift * most + m
            row = row_ref[source, slot]
            col = col_ref[source, slot]

            @pl.when(row >= 0)
            def _():
                block = block_ref[0, pl.ds(pl.multiple_of(slot * edge, edge), edge), :]
                omega = omega_ref[pl.ds(pl.multiple_of(col * edge, edge), edge), :]
                total[row] += dot(block, omega)

            return carry

        lax.fori_loop(0, most, one, 0)
    out_ref[0] = total[...].reshape(out_ref.shape[1:]).astype(out_ref.dtype)


def far_sum(blocks, omegas, rows, cols, most, block_rows):
    planes, length, edge = blocks.shape
    height, columns = omegas[0].shape
    return pl.pallas_call(
        functools.partial(far_kernel, most),
        out_shape=jax.ShapeDtypeStruct((planes, height, columns), jnp.bfloat16),
        grid_spec=pltpu.PrefetchScalarGridSpec(
            num_scalar_prefetch=2,
            grid=(planes,),
            in_specs=[pl.BlockSpec((1, length, edge), lambda p, *_: (p, 0, 0))]
            + [pl.BlockSpec((height, columns), lambda p, *_: (0, 0))] * len(omegas),
            out_specs=pl.BlockSpec((1, height, columns), lambda p, *_: (p, 0, 0)),
            scratch_shapes=[pltpu.VMEM((block_rows, edge, columns), jnp.float32)],
        ),
        compiler_params=params(),
        cost_estimate=pl.CostEstimate(
            flops=2 * planes * length * edge * columns,
            bytes_accessed=planes * (length * edge + height * columns) * 2,
            transcendentals=0,
        ),
        name="far",
    )(rows, cols, blocks, *omegas)


def image_kernel(scale, diag_ref, omega_ref, far_ref, own_ref, *rest):
    *mirror_refs, image_ref, gram_ref = rest
    image = dot(diag_ref[0], omega_ref[...]) + own_ref[...]
    for source in range(far_ref.shape[0]):
        image += far_ref[source].astype(jnp.float32)
    for mirror_ref in mirror_refs:
        image += mirror_ref[...].astype(jnp.float32)
    image_ref[...] = image

    @pl.when(pl.program_id(0) == 0)
    def _():
        gram_ref[...] = jnp.zeros_like(gram_ref)

    gram_ref[...] += dot(image, image, ((0,), (0,)), lax.Precision.HIGHEST) * scale


def image_and_gram(diag, sketch, far, own, mirrors, total_rows):
    block_rows, edge, _ = diag.shape
    planes, height, columns = far.shape
    rows = pl.BlockSpec((edge, columns), lambda b: (b, 0))
    return pl.pallas_call(
        functools.partial(image_kernel, 1.0 / total_rows),
        out_shape=(
            jax.ShapeDtypeStruct((height, columns), jnp.float32),
            jax.ShapeDtypeStruct((columns, columns), jnp.float32),
        ),
        grid=(block_rows,),
        in_specs=[
            pl.BlockSpec((1, edge, edge), lambda b: (b, 0, 0)),
            rows,
            pl.BlockSpec((planes, edge, columns), lambda b: (0, b, 0)),
            rows,
        ]
        + [rows] * len(mirrors),
        out_specs=(rows, pl.BlockSpec((columns, columns), lambda b: (0, 0))),
        compiler_params=params(),
        name="image",
    )(diag, sketch, far, own, *mirrors)


def sum_over_devices(part, peers):
    rows, columns = part.shape
    pieces = lax.all_to_all(part.reshape(peers, rows // peers, columns), ALL, 0, 0, tiled=True)
    mine = jnp.broadcast_to(jnp.sum(pieces, axis=0), pieces.shape)
    return lax.all_to_all(mine, ALL, 0, 0, tiled=True).reshape(rows, columns)


def on_device(diag_blocks, off_blocks, col_blocks, sketch):
    block_rows, per_row = col_blocks.shape
    edge = diag_blocks.shape[1]
    layers = lax.axis_size(LINE)
    planes = lax.axis_size(PLANE)
    peers = layers * planes
    requests = block_rows * per_row
    most = max(2, (2 * requests + peers - 1) // peers)
    slots = layers * most
    layer = lax.axis_index(LINE)

    flat = col_blocks.reshape(requests)
    owners = flat // block_rows
    order = jnp.arange(requests)
    earlier = (owners[:, None] == owners[None, :]) & (order[None, :] < order[:, None])
    ranks = jnp.sum(earlier.astype(jnp.int32), axis=1)
    to_plane = owners % planes
    to_slot = lax.rem(owners // planes - layer + layers, layers) * most + ranks
    place = to_plane * slots + to_slot
    hit = place[:, None] == jnp.arange(planes * slots)[None, :]
    row_label = jnp.sum(jnp.where(hit, (order // per_row + 1)[:, None], 0), axis=0) - 1
    col_label = jnp.sum(jnp.where(hit, (flat % block_rows)[:, None], 0), axis=0)
    labels = jnp.stack([row_label.reshape(planes, slots), col_label.reshape(planes, slots)], axis=1)
    labels = jnp.pad(labels, ((0, 0), (0, TAIL - 2), (0, edge - slots))).astype(jnp.bfloat16)
    outgoing = pack(off_blocks.reshape(requests, edge, edge), to_plane, to_slot, labels, slots)

    blocks = lax.all_to_all(outgoing, PLANE, 0, 0, tiled=True)
    plane_omegas = lax.all_gather(sketch, PLANE)
    line_omegas = [sketch]
    for shift in range(1, layers):
        steps = [(z, (z - shift) % layers) for z in range(layers)]
        line_omegas.append(lax.ppermute(sketch, LINE, steps))
    rows = blocks[:, slots * edge, :slots].astype(jnp.int32)
    cols = blocks[:, slots * edge + 1, :slots].astype(jnp.int32)

    mirrors = []
    for shift in range(1, layers):
        part = mirror_sum(
            blocks, plane_omegas, rows, cols, shift, most, block_rows, jnp.bfloat16
        )
        steps = [(z, (z + shift) % layers) for z in range(layers)]
        mirrors.append(lax.ppermute(part, LINE, steps))
    far = far_sum(blocks, line_omegas, rows, cols, most, block_rows)
    far = lax.all_to_all(far, PLANE, 0, 0, tiled=True)
    own = mirror_sum(blocks, plane_omegas, rows, cols, 0, most, block_rows, jnp.float32)

    image, part = image_and_gram(
        diag_blocks, sketch, far, own, mirrors, block_rows * edge * peers
    )
    gram = sum_over_devices(part, peers)
    lower = jnp.linalg.cholesky(gram)
    basis = lax.linalg.triangular_solve(lower, image, left_side=False, lower=True, transpose_a=True)
    return basis, lower.T


def solution(mesh):
    rows, sub = mesh.devices.shape
    layers, cores = math.gcd(rows, 4), math.gcd(sub, 2)
    devices = mesh.devices.reshape(layers, rows // layers, sub // cores, cores)
    placed = (P(ALL, None, None), P(ALL, None, None, None), P(ALL, None), P(ALL, None))
    return jax.shard_map(
        on_device,
        mesh=Mesh(devices, ALL),
        in_specs=placed,
        out_specs=(P(ALL, None), P()),
        check_vma=False,
    )
```

time: 1060 us -> 424 us (0.40)
  waiting for transfers between devices: 803 us -> 186 us
  local copies, waits for them, and re-layouts: 103 us -> 13.2 us
  Pallas kernels: 0 us -> 86.2 us
  matrix products: 46.7 us -> 4.51 us
  blocking collectives: 0 us -> 13.5 us
  starting transfers between devices: 29.6 us -> 41.1 us
    all_to_all x3, waiting for transfers between devices: 666 us -> 170 us  [the longest x1 122 us: on_device(): blocks = lax.all_to_all(outgoing, PLANE, 0, 0, tiled=True)]
    psum x1 -> x0, waiting for transfers between devices: 137 us -> none  [on_device(): gram = lax.psum(gram_local, ('rows', 'sub'))]
    pallas_call x0 -> x7, Pallas kernels: none -> 86.2 us  [the longest x4 43.1 us: mirror_sum(): pl.pallas_call(functools.partial(mirror_kernel, shift, most), out_shape=j...]
    dot_general x6 -> x0, matrix products: 42.2 us -> none  [the longest x1 11.5 us: on_device(): jnp.dot(selector, received.reshape(target_positions, edge * columns), pre...]
    scatter x2 -> x0, local copies, waits for them, and re-layouts: 24.3 us -> none  [the longest x1 23.3 us: on_device(): jnp.zeros((target_positions, edge, columns), jnp.bfloat16).at[where_to]]
    dot_general x1 -> x0, local copies, waits for them, and re-layouts: 22.4 us -> none  [on_device(): jnp.dot(selector, received.reshape(target_positions, edge * columns), pre...]
    ppermute x0 -> x6, starting transfers between devices: none -> 16.6 us  [the longest x3 10.6 us: on_device(): mirrors.append(lax.ppermute(part, LINE, steps))]
    ppermute x0 -> x6, waiting for transfers between devices: none -> 14.9 us  [the longest x3 14.9 us: on_device(): mirrors.append(lax.ppermute(part, LINE, steps))]
  transfers between devices with their start and end apart: 4 -> 10, of which waited for: 3 -> 4; matrix products, arithmetic and copies ran while one was open for 10% -> 1% of each run, Pallas kernels for 0% -> 17%
where the time goes in v1:
time: 424 us; the launch traced here: 416 us
  waiting for transfers between devices  186 us (44%)
  Pallas kernels  86.2 us (20%)
  other arithmetic  56 us (13%)
  starting transfers between devices  41.1 us (10%)
  between operations  15.7 us (4%)
  blocking collectives  13.5 us (3%)
  local copies, waits for them, and re-layouts  13.2 us (3%)
  matrix products  4.51 us (1%)
    all_to_all x1, waiting for transfers between devices, on_device(): blocks = lax.all_to_all(outgoing, PLANE, 0, 0, tiled=True)  122 us
    pallas_call x4, Pallas kernels, mirror_sum(): pl.pallas_call(functools.partial(mirror_kernel, shift, most), out_shape=j...  43.1 us
    all_to_all x1, waiting for transfers between devices, on_device(): far = lax.all_to_all(far, PLANE, 0, 0, tiled=True)  38.2 us
    another operation x7, other arithmetic, on_device(): lower = jnp.linalg.cholesky(gram)  34.6 us
    pallas_call x1, Pallas kernels, far_sum(): pl.pallas_call(functools.partial(far_kernel, most), out_shape=jax.ShapeDt...  25.1 us
    another operation x3, other arithmetic, on_device(): lax.linalg.triangular_solve(lower, image, left_side=False, lower=True, tr...  20 us
    all_to_all x1, starting transfers between devices, on_device(): far = lax.all_to_all(far, PLANE, 0, 0, tiled=True)  16.3 us
    pallas_call x1, Pallas kernels, image_and_gram(): pl.pallas_call(functools.partial(image_kernel, 1.0 / total_rows), out_sha...  15.5 us
  transfers between devices with their start and end apart: 10, of which 4 were waited for; matrix products, arithmetic and copies ran while one was open for 1% of the time, Pallas kernels for 17%

profile of v1, /device:TPU:0, one launch (start us, length us, event | category | flops | bytes accessed | tf_op | source)
XLA Modules:
  0.0 415.9 jit_solution(15346741388506686612)
XLA Ops:
  9.3 2.2 copy-done.2
  11.5 2.5 pack.1
  14.1 5.4 %all-to-all-start = ((bf16[8,4112,128]{2,1,0:T(8,128)(2,1)}), bf16[8,4112,128]{2,1,0:T(8,128)(2,1)}, u32[]{:S(2)}, u32[]{:S(2)}) async-start(bf16[8,4112,128]{2,1,0:T(8,128)(2,1)} %pack.1), calls=%async_computation | async-start | bytes 16842752 | tf_op jit(solution)/shard_map/all_to_all | solution.py:240
  19.4 5.0 %collective-permute-start = (bf16[2048,256]{1,0:T(8,128)(2,1)S(1)}, bf16[2048,256]{1,0:T(8,128)(2,1)S(1)}, u32[]{:S(2)}, u32[]{:S(2)}) collective-permute-start(bf16[2048,256]{1,0:T(8,128)(2,1)S(1)} %copy-done), channel_id=1, source_target_pairs={{0,24},{8,0},{16,8},{24,16},{1,25},{9,1},{17,9},{25,17},{2,26},{10... | collective-permute-start | bytes 3145736 | tf_op jit(solution)/shard_map/ppermute | solution.py:245
  25.4 121.6 %all-to-all-done.block_ref = bf16[8,4112,128]{2,1,0:T(8,128)(2,1)} async-done(((bf16[8,4112,128]{2,1,0:T(8,128)(2,1)}), bf16[8,4112,128]{2,1,0:T(8,128)(2,1)}, u32[]{:S(2)}, u32[]{:S(2)}) %all-to-all-start) | async-done | bytes 8421408 | tf_op jit(solution)/shard_map/all_to_all | solution.py:240
  147.9 25.1 %far.1 = bf16[8,2048,256]{2,1,0:T(8,128)(2,1)} custom-call(s32[8,32]{1,0:T(8,128)S(1)} %bitcast.46, s32[8,32]{1,0:T(8,128)S(1)} %bitcast.41, bf16[8,4112,128]{2,1,0:T(8,128)(2,1)} %all-to-all-done.block_ref, bf16[2048,256]{1,0:T(8,128)(2,1)S(1)} %copy-done, bf16[2048,256]{1,0:T(8,128)(2,1)S(1)} %collective-permute-done.rest_1_, ...), custom_call_target="tpu_custom_call" | custom-call | flops 2155872256 | bytes 16809984 | tf_op jit(solution)/shard_map/far/pallas_call | solution.py:146
  172.9 16.3 %all-to-all-start.1 = ((bf16[8,2048,256]{2,1,0:T(8,128)(2,1)}), bf16[8,2048,256]{2,1,0:T(8,128)(2,1)}, u32[]{:S(2)}, u32[]{:S(2)}) async-start(bf16[8,2048,256]{2,1,0:T(8,128)(2,1)} %far.1), calls=%async_computation.1 | async-start | bytes 16777216 | tf_op jit(solution)/shard_map/all_to_all | solution.py:257
  189.3 15.3 %mirror.7 = bf16[2048,256]{1,0:T(8,128)(2,1)S(1)} custom-call(s32[8,32]{1,0:T(8,128)S(1)} %bitcast.47, s32[8,32]{1,0:T(8,128)S(1)} %bitcast.42, bf16[8,4112,128]{2,1,0:T(8,128)(2,1)} %all-to-all-done.block_ref, bf16[8,2048,256]{2,1,0:T(8,128)(2,1)} %bitcast.51), custom_call_target="tpu_custom_call" | custom-call | flops 536870912 | bytes 10485760 | tf_op jit(solution)/shard_map/mirror/pallas_call | solution.py:96
  204.7 6.9 %mirror.6 = bf16[2048,256]{1,0:T(8,128)(2,1)S(1)} custom-call(s32[8,32]{1,0:T(8,128)S(1)} %bitcast.48, s32[8,32]{1,0:T(8,128)S(1)} %bitcast.43, bf16[8,4112,128]{2,1,0:T(8,128)(2,1)} %all-to-all-done.block_ref, bf16[8,2048,256]{2,1,0:T(8,128)(2,1)} %bitcast.52), custom_call_target="tpu_custom_call" | custom-call | flops 536870912 | bytes 10485760 | tf_op jit(solution)/shard_map/mirror/pallas_call | solution.py:96
  211.6 8.6 %collective-permute-start.4 = (bf16[2048,256]{1,0:T(8,128)(2,1)S(1)}, bf16[2048,256]{1,0:T(8,128)(2,1)}, u32[]{:S(2)}, u32[]{:S(2)}) collective-permute-start(bf16[2048,256]{1,0:T(8,128)(2,1)S(1)} %mirror.6), channel_id=1, source_target_pairs={{0,16},{8,24},{16,0},{24,8},{1,17},{9,25},{17,1},{25,9},{2,18},{10... | collective-permute-start | bytes 3145736 | tf_op jit(solution)/shard_map/ppermute | solution.py:255
  220.2 7.9 %mirror.5 = bf16[2048,256]{1,0:T(8,128)(2,1)} custom-call(s32[8,32]{1,0:T(8,128)S(1)} %bitcast.49, s32[8,32]{1,0:T(8,128)S(1)} %bitcast.44, bf16[8,4112,128]{2,1,0:T(8,128)(2,1)} %all-to-all-done.block_ref, bf16[8,2048,256]{2,1,0:T(8,128)(2,1)} %bitcast.53), custom_call_target="tpu_custom_call" | custom-call | flops 536870912 | bytes 10485760 | tf_op jit(solution)/shard_map/mirror/pallas_call | solution.py:96
  228.1 1.9 collective-permute-start.3
  230.0 13.0 %mirror.4.own_ref = f32[2048,256]{1,0:T(8,128)S(1)} custom-call(s32[8,32]{1,0:T(8,128)S(1)} %bitcast.50, s32[8,32]{1,0:T(8,128)S(1)} %bitcast.45, bf16[8,4112,128]{2,1,0:T(8,128)(2,1)} %all-to-all-done.block_ref, bf16[8,2048,256]{2,1,0:T(8,128)(2,1)} %bitcast.54), custom_call_target="tpu_custom_call" | custom-call | flops 536870912 | bytes 10485760 | tf_op jit(solution)/shard_map/mirror/pallas_call | solution.py:96
  244.3 38.2 %all-to-all-done.1.far_ref = bf16[8,2048,256]{2,1,0:T(8,128)(2,1)} async-done(((bf16[8,2048,256]{2,1,0:T(8,128)(2,1)}), bf16[8,2048,256]{2,1,0:T(8,128)(2,1)}, u32[]{:S(2)}, u32[]{:S(2)}) %all-to-all-start.1) | async-done | bytes 8388640 | tf_op jit(solution)/shard_map/all_to_all | solution.py:257
  282.5 14.9 %collective-permute-done.4.rest_1_ = bf16[2048,256]{1,0:T(8,128)(2,1)} collective-permute-done((bf16[2048,256]{1,0:T(8,128)(2,1)S(1)}, bf16[2048,256]{1,0:T(8,128)(2,1)}, u32[]{:S(2)}, u32[]{:S(2)}) %collective-permute-start.4) | collective-permute-done | bytes 1048608 | tf_op jit(solution)/shard_map/ppermute | solution.py:255
  298.5 15.5 %image.1 = (f32[2048,256]{1,0:T(8,128)}, f32[256,256]{1,0:T(8,128)S(1)}) custom-call(bf16[16,128,128]{2,1,0:T(8,128)(2,1)S(1)} %copy-done.3, bf16[2048,256]{1,0:T(8,128)(2,1)S(1)} %copy-done, bf16[8,2048,256]{2,1,0:T(8,128)(2,1)} %all-to-all-done.1.far_ref, f32[2048,256]{1,0:T(8,128)} %copy-done.1, bf16[2048,256]{1,0:T(8,128)(2,1)} %collective-permute-done.3.rest_0_, ...), custom_call_target="tpu_custom_call" | custom-call | tf_op jit(solution)/shard_map/image/pallas_call | solution.py:187
  314.0 13.5 %all_to_all.20 = f32[32,8,256]{2,1,0:T(8,128)S(1)} all-to-all(f32[32,8,256]{2,1,0:T(8,128)S(1)} %bitcast.40), channel_id=1, replica_groups=mesh['z'=4,'x'=2,'y'=2,'c'=2] {'z','x','y','c'}, dimensions={0} | all-to-all | bytes 524288 | tf_op jit(solution)/shard_map/all_to_all | solution.py:209
  328.3 2.8 all-to-all-start.3
  331.1 10.4 %all-to-all-done.3 = f32[32,8,256]{2,1,0:T(8,128)S(1)} async-done(((f32[32,8,256]{2,1,0:T(8,128)}), f32[32,8,256]{2,1,0:T(8,128)S(1)}, u32[]{:S(2)}, u32[]{:S(2)}) %all-to-all-start.3) | async-done | bytes 262176 | tf_op jit(solution)/shard_map/all_to_all | solution.py:211
  341.6 11.7 %cholesky.50 = f32[128,128]{1,0:T(8,128)S(1)} custom-call(f32[128,128]{1,0:T(8,128)S(1)} %cholesky.118), custom_call_target="Cholesky" | custom-call | tf_op jit(solution)/shard_map/jit(cholesky)/cholesky | solution.py:264
  353.4 9.8 %custom-call.14 = f32[1,128,128]{1,2,0:T(8,128)S(1)} custom-call(f32[1,128,128]{2,1,0:T(8,128)S(1)} %get-tuple-element.42), custom_call_target="InvertDiagBlocksLowerTriangular" | custom-call | tf_op jit(solution)/shard_map/jit(cholesky)/cholesky | solution.py:264
  363.7 11.7 %cholesky.105 = f32[128,128]{1,0:T(8,128)S(1)} custom-call(f32[128,128]{1,0:T(8,128)S(1)} %convolution_subtract_fusion), custom_call_target="Cholesky" | custom-call | tf_op jit(solution)/shard_map/jit(cholesky)/cholesky | solution.py:264
  378.3 4.1 while.1
  382.3 19.9 %custom-call.15 = f32[2,128,128]{1,2,0:T(8,128)S(1)} custom-call(f32[2,128,128]{2,1,0:T(8,128)S(1)} %get-tuple-element.13), custom_call_target="InvertDiagBlocksLowerTriangular" | custom-call | tf_op jit(solution)/shard_map/triangular_solve | solution.py:265
  (60 shorter events, 20.2 us)
Async XLA Ops:
  7.2 182.1 %all-gather.3.cloned.1.call-start = ((), (), s32[]{:S(2)}) async-start(), calls=%async_computation.4 | async-start | bytes 9437184 | tf_op jit(solution)/shard_map/all_gather | solution.py:241
  9.3 2.2 copy-start.2
  14.1 5.4 %copy-start = (bf16[2048,256]{1,0:T(8,128)(2,1)S(1)}, bf16[2048,256]{1,0:T(8,128)(2,1)}, u32[]{:S(2)}) copy-start(bf16[2048,256]{1,0:T(8,128)(2,1)} %omega_ref.1) | copy-start | bytes 3145732
  14.1 133.0 %all-to-all-start = ((bf16[8,4112,128]{2,1,0:T(8,128)(2,1)}), bf16[8,4112,128]{2,1,0:T(8,128)(2,1)}, u32[]{:S(2)}, u32[]{:S(2)}) async-start(bf16[8,4112,128]{2,1,0:T(8,128)(2,1)} %pack.1), calls=%async_computation | async-start | bytes 16842752 | tf_op jit(solution)/shard_map/all_to_all | solution.py:240
  19.4 128.4 %collective-permute-start = (bf16[2048,256]{1,0:T(8,128)(2,1)S(1)}, bf16[2048,256]{1,0:T(8,128)(2,1)S(1)}, u32[]{:S(2)}, u32[]{:S(2)}) collective-permute-start(bf16[2048,256]{1,0:T(8,128)(2,1)S(1)} %copy-done), channel_id=1, source_target_pairs={{0,24},{8,0},{16,8},{24,16},{1,25},{9,1},{17,9},{25,17},{2,26},{10... | collective-permute-start | bytes 3145736 | tf_op jit(solution)/shard_map/ppermute | solution.py:245
  24.4 123.5 %collective-permute-start.1 = (bf16[2048,256]{1,0:T(8,128)(2,1)S(1)}, bf16[2048,256]{1,0:T(8,128)(2,1)S(1)}, u32[]{:S(2)}, u32[]{:S(2)}) collective-permute-start(bf16[2048,256]{1,0:T(8,128)(2,1)S(1)} %copy-done), channel_id=1, source_target_pairs={{0,16},{8,24},{16,0},{24,8},{1,17},{9,25},{17,1},{25,9},{2,18},{10... | collective-permute-start | bytes 3145736 | tf_op jit(solution)/shard_map/ppermute | solution.py:245
  24.4 123.5 %collective-permute-start.2 = (bf16[2048,256]{1,0:T(8,128)(2,1)S(1)}, bf16[2048,256]{1,0:T(8,128)(2,1)}, u32[]{:S(2)}, u32[]{:S(2)}) collective-permute-start(bf16[2048,256]{1,0:T(8,128)(2,1)S(1)} %copy-done), channel_id=1, source_target_pairs={{0,8},{8,16},{16,24},{24,0},{1,9},{9,17},{17,25},{25,1},{2,10},{10... | collective-permute-start | bytes 3145736 | tf_op jit(solution)/shard_map/ppermute | solution.py:245
  172.9 109.6 %all-to-all-start.1 = ((bf16[8,2048,256]{2,1,0:T(8,128)(2,1)}), bf16[8,2048,256]{2,1,0:T(8,128)(2,1)}, u32[]{:S(2)}, u32[]{:S(2)}) async-start(bf16[8,2048,256]{2,1,0:T(8,128)(2,1)} %far.1), calls=%async_computation.1 | async-start | bytes 16777216 | tf_op jit(solution)/shard_map/all_to_all | solution.py:257
  204.6 77.9 %collective-permute-start.5 = (bf16[2048,256]{1,0:T(8,128)(2,1)S(1)}, bf16[2048,256]{1,0:T(8,128)(2,1)}, u32[]{:S(2)}, u32[]{:S(2)}) collective-permute-start(bf16[2048,256]{1,0:T(8,128)(2,1)S(1)} %mirror.7), channel_id=1, source_target_pairs={{0,24},{8,0},{16,8},{24,16},{1,25},{9,1},{17,9},{25,17},{2,26},{10... | collective-permute-start | bytes 3145736 | tf_op jit(solution)/shard_map/ppermute | solution.py:255
  211.6 85.9 %collective-permute-start.4 = (bf16[2048,256]{1,0:T(8,128)(2,1)S(1)}, bf16[2048,256]{1,0:T(8,128)(2,1)}, u32[]{:S(2)}, u32[]{:S(2)}) collective-permute-start(bf16[2048,256]{1,0:T(8,128)(2,1)S(1)} %mirror.6), channel_id=1, source_target_pairs={{0,16},{8,24},{16,0},{24,8},{1,17},{9,25},{17,1},{25,9},{2,18},{10... | collective-permute-start | bytes 3145736 | tf_op jit(solution)/shard_map/ppermute | solution.py:255
  228.1 69.3 %collective-permute-start.3 = (bf16[2048,256]{1,0:T(8,128)(2,1)}, bf16[2048,256]{1,0:T(8,128)(2,1)}, u32[]{:S(2)}, u32[]{:S(2)}) collective-permute-start(bf16[2048,256]{1,0:T(8,128)(2,1)} %mirror.5), channel_id=1, source_target_pairs={{0,8},{8,16},{16,24},{24,0},{1,9},{9,17},{17,25},{25,1},{2,10},{10... | collective-permute-start | bytes 3145736 | tf_op jit(solution)/shard_map/ppermute | solution.py:255
  243.0 1.3 copy-start.1
  297.4 1.0 copy-start.3
  328.3 13.2 %all-to-all-start.3 = ((f32[32,8,256]{2,1,0:T(8,128)}), f32[32,8,256]{2,1,0:T(8,128)S(1)}, u32[]{:S(2)}, u32[]{:S(2)}) async-start(f32[32,8,256]{2,1,0:T(8,128)} %broadcast_in_dim.34), calls=%async_computation.3 | async-start | bytes 524288 | tf_op jit(solution)/shard_map/all_to_all | solution.py:211
  341.5 60.8 %copy-start.4 = (f32[2048,256]{1,0:T(8,128)S(1)}, f32[2048,256]{1,0:T(8,128)}, u32[]{:S(2)}) copy-start(f32[2048,256]{1,0:T(8,128)} %get-tuple-element.4) | copy-start | bytes 6291460
Sparse Core Ops, SparseCore 0:
  9.9 132.4 all-gather.2

commit v2 on v1

--- a/solution.py
+++ b/solution.py
@@ -22,9 +22,21 @@
     )
 
 
+NT = ((1,), (1,))
+TN = ((0,), (0,))
+
+
 def params():
     return pltpu.CompilerParams(vmem_limit_bytes=VMEM_LIMIT)
 
+
+def split(a):
+    high = a.astype(jnp.bfloat16)
+    return high, (a - high.astype(jnp.float32)).astype(jnp.bfloat16)
+
+def dot3(a, b, contract=((1,), (0,))):
+    (ah, al), (bh, bl) = a, b
+    return dot(ah, bh, contract) + (dot(ah, bl, contract) + dot(al, bh, contract))
 
 def pack_kernel(plane_ref, slot_ref, off_ref, label_ref, out_ref, sem, label_sem):
     count, edge, _ = off_ref.shape
@@ -66,28 +78,23 @@
 def mirror_kernel(shift, most, row_ref, col_ref, block_ref, omega_ref, out_ref, total):
     source = pl.program_id(0)
     edge = block_ref.shape[2]
+    spare = total.shape[0] - 1
 
     @pl.when(source == 0)
     def _():
         total[...] = jnp.zeros_like(total)
 
-    def one(m, carry):
-        row = row_ref[source, shift * most + m]
+    for m in range(most):
+        row = jnp.minimum(row_ref[source, shift * most + m], spare - 1)
         col = col_ref[source, shift * most + m]
-
-        @pl.when(row >= 0)
-        def _():
-            block = block_ref[0, pl.ds(pl.multiple_of(m * edge, edge), edge), :]
-            omega = omega_ref[0, pl.ds(pl.multiple_of(row * edge, edge), edge), :]
-            total[col] += dot(block, omega, ((0,), (0,)))
-
-        return carry
-
-    lax.fori_loop(0, most, one, 0)
+        block = block_ref[0, m * edge : (m + 1) * edge, :]
+        omega = omega_ref[0, pl.ds(pl.multiple_of(row * edge, edge), edge), :]
+        product = dot(block, omega, ((0,), (0,))).astype(jnp.bfloat16)
+        total[col] += product.astype(jnp.float32)
 
     @pl.when(source == pl.num_programs(0) - 1)
     def _():
-        out_ref[...] = total[...].reshape(out_ref.shape).astype(out_ref.dtype)
+        out_ref[...] = total[:spare].reshape(out_ref.shape).astype(out_ref.dtype)
 
 
 def mirror_sum(blocks, omegas, rows, cols, shift, most, block_rows, dtype):
@@ -104,7 +111,7 @@
                 pl.BlockSpec((1, height, columns), lambda p, *_: (p, 0, 0)),
             ],
             out_specs=pl.BlockSpec((height, columns), lambda p, *_: (0, 0)),
-            scratch_shapes=[pltpu.VMEM((block_rows, edge, columns), jnp.float32)],
+            scratch_shapes=[pltpu.VMEM((block_rows + 1, edge, columns), jnp.float32)],
         ),
         compiler_params=params(),
         cost_estimate=pl.CostEstimate(
@@ -120,24 +127,16 @@
     *omega_refs, out_ref, total = rest
     source = pl.program_id(0)
     edge = block_ref.shape[2]
+    spare = total.shape[0] - 1
     total[...] = jnp.zeros_like(total)
     for shift, omega_ref in enumerate(omega_refs):
-
-        def one(m, carry, shift=shift, omega_ref=omega_ref):
-            slot = shift * most + m
+        for slot in range(shift * most, (shift + 1) * most):
             row = row_ref[source, slot]
-            col = col_ref[source, slot]
-
-            @pl.when(row >= 0)
-            def _():
-                block = block_ref[0, pl.ds(pl.multiple_of(slot * edge, edge), edge), :]
-                omega = omega_ref[pl.ds(pl.multiple_of(col * edge, edge), edge), :]
-                total[row] += dot(block, omega)
-
-            return carry
-
-        lax.fori_loop(0, most, one, 0)
-    out_ref[0] = total[...].reshape(out_ref.shape[1:]).astype(out_ref.dtype)
+            col = jnp.minimum(col_ref[source, slot], spare - 1)
+            block = block_ref[0, slot * edge : (slot + 1) * edge, :]
+            omega = omega_ref[pl.ds(pl.multiple_of(col * edge, edge), edge), :]
+            total[row] += dot(block, omega)
+    out_ref[0] = total[:spare].reshape(out_ref.shape[1:]).astype(out_ref.dtype)
 
 
 def far_sum(blocks, omegas, rows, cols, most, block_rows):
@@ -152,7 +151,7 @@
             in_specs=[pl.BlockSpec((1, length, edge), lambda p, *_: (p, 0, 0))]
             + [pl.BlockSpec((height, columns), lambda p, *_: (0, 0))] * len(omegas),
             out_specs=pl.BlockSpec((1, height, columns), lambda p, *_: (p, 0, 0)),
-            scratch_shapes=[pltpu.VMEM((block_rows, edge, columns), jnp.float32)],
+            scratch_shapes=[pltpu.VMEM((block_rows + 1, edge, columns), jnp.float32)],
         ),
         compiler_params=params(),
         cost_estimate=pl.CostEstimate(
@@ -165,43 +164,127 @@
 
 
 def image_kernel(scale, diag_ref, omega_ref, far_ref, own_ref, *rest):
-    *mirror_refs, image_ref, gram_ref = rest
-    image = dot(diag_ref[0], omega_ref[...]) + own_ref[...]
+    *mirror_refs, image_ref, gram_ref, cross = rest
+    step = pl.program_id(0)
+    edge = diag_ref.shape[1]
+    near = [
+        dot(diag_ref[b], omega_ref[b * edge : (b + 1) * edge, :]) for b in range(diag_ref.shape[0])
+    ]
+    image = jnp.concatenate(near, axis=0) + own_ref[...]
     for source in range(far_ref.shape[0]):
         image += far_ref[source].astype(jnp.float32)
     for mirror_ref in mirror_refs:
         image += mirror_ref[...].astype(jnp.float32)
     image_ref[...] = image
 
-    @pl.when(pl.program_id(0) == 0)
+    @pl.when(step == 0)
     def _():
         gram_ref[...] = jnp.zeros_like(gram_ref)
-
-    gram_ref[...] += dot(image, image, ((0,), (0,)), lax.Precision.HIGHEST) * scale
+        cross[...] = jnp.zeros_like(cross)
+
+    high, low = split(image)
+    gram_ref[...] += dot(high, high, TN)
+    cross[...] += dot(high, low, TN)
+
+    @pl.when(step == pl.num_programs(0) - 1)
+    def _():
+        gram_ref[...] = (gram_ref[...] + (cross[...] + cross[...].T)) * scale
 
 
 def image_and_gram(diag, sketch, far, own, mirrors, total_rows):
     block_rows, edge, _ = diag.shape
     planes, height, columns = far.shape
-    rows = pl.BlockSpec((edge, columns), lambda b: (b, 0))
+    together = math.gcd(block_rows, 2)
+    rows = pl.BlockSpec((together * edge, columns), lambda b: (b, 0))
     return pl.pallas_call(
         functools.partial(image_kernel, 1.0 / total_rows),
         out_shape=(
             jax.ShapeDtypeStruct((height, columns), jnp.float32),
             jax.ShapeDtypeStruct((columns, columns), jnp.float32),
         ),
-        grid=(block_rows,),
+        grid=(block_rows // together,),
         in_specs=[
-            pl.BlockSpec((1, edge, edge), lambda b: (b, 0, 0)),
+            pl.BlockSpec((together, edge, edge), lambda b: (b, 0, 0)),
             rows,
-            pl.BlockSpec((planes, edge, columns), lambda b: (0, b, 0)),
+            pl.BlockSpec((planes, together * edge, columns), lambda b: (0, b, 0)),
             rows,
         ]
         + [rows] * len(mirrors),
         out_specs=(rows, pl.BlockSpec((columns, columns), lambda b: (0, 0))),
+        scratch_shapes=[pltpu.VMEM((columns, columns), jnp.float32)],
         compiler_params=params(),
         name="image",
     )(diag, sketch, far, own, *mirrors)
+
+
+def factor_kernel(rounds, gram_ref, image_ref, basis_ref, factor_ref, inverse, work):
+    n = gram_ref.shape[0]
+    exact = lax.Precision.HIGHEST
+
+    @pl.when(pl.program_id(0) == 0)
+    def _():
+        gram = gram_ref[...]
+        row = lax.broadcasted_iota(jnp.int32, (n, n), 0)
+        col = lax.broadcasted_iota(jnp.int32, (n, n), 1)
+        weight = jnp.where(row > col, 1.0, jnp.where(row == col, 0.5, 0.0))
+        one = jnp.where(row == col, 1.0, 0.0)
+        diagonal = jnp.where(row == col, gram, 0.0)
+        down = lax.rsqrt(jnp.sum(diagonal, axis=1, keepdims=True))
+        across = lax.rsqrt(jnp.sum(diagonal, axis=0, keepdims=True))
+        scaled = gram * down * across
+        step = one - weight * (scaled - one)
+        guess = step
+        for turn in range(rounds):
+            if turn == rounds - 1:
+                error = dot(dot(guess, scaled, precision=exact), guess, NT, precision=exact) - one
+                step = weight * error
+                guess = guess - dot(step, guess, precision=exact)
+            else:
+                g3 = split(guess)
+                error = dot3(split(dot3(g3, split(scaled))), g3, NT) - one
+                guess = guess - dot3(split(weight * error), g3)
+        guess = jnp.where(row >= col, guess, 0.0)
+        inverse[...] = guess * across
+        factor_ref[...] = jnp.where(row <= col, dot(inverse[...], gram, precision=exact), 0.0)
+        size = jnp.sum(error * error)
+
+        @pl.when(jnp.logical_not(size < 1e-6))
+        def _():
+            work[...] = gram
+            inverse[...] = one
+            lane = lax.broadcasted_iota(jnp.int32, (1, n), 1)
+
+            def eliminate(j, carry):
+                line = work[pl.ds(j, 1), :]
+                pivot = jnp.sum(jnp.where(lane == j, line, 0.0), axis=1, keepdims=True)
+                scale = lax.rsqrt(pivot)
+                line = jnp.where(lane >= j, line * scale, 0.0)
+                other = inverse[pl.ds(j, 1), :] * scale
+                below = jnp.where(lane > j, line, 0.0)
+                work[...] -= dot(below, line, TN, exact)
+                inverse[...] -= dot(below, other, TN, exact)
+                inverse[pl.ds(j, 1), :] = other
+                factor_ref[pl.ds(j, 1), :] = line
+                return carry
+
+            lax.fori_loop(0, n, eliminate, 0)
+
+    basis_ref[...] = dot3(split(image_ref[...]), split(inverse[...]), NT)
+
+def factor_and_basis(gram, image, tile=256, rounds=3):
+    height, n = image.shape
+    whole = pl.BlockSpec((n, n), lambda b: (0, 0))
+    tiles = pl.BlockSpec((tile, n), lambda b: (b, 0))
+    return pl.pallas_call(
+        functools.partial(factor_kernel, rounds),
+        out_shape=(jax.ShapeDtypeStruct((height, n), jnp.float32), jax.ShapeDtypeStruct((n, n), jnp.float32)),
+        grid=(height // tile,),
+        in_specs=[whole, tiles],
+        out_specs=(tiles, whole),
+        scratch_shapes=[pltpu.VMEM((n, n), jnp.float32)] * 2,
+        compiler_params=params(),
+        name="factor",
+    )(gram, image)
 
 
 def sum_over_devices(part, peers):
@@ -231,8 +314,12 @@
     to_slot = lax.rem(owners // planes - layer + layers, layers) * most + ranks
     place = to_plane * slots + to_slot
     hit = place[:, None] == jnp.arange(planes * slots)[None, :]
-    row_label = jnp.sum(jnp.where(hit, (order // per_row + 1)[:, None], 0), axis=0) - 1
-    col_label = jnp.sum(jnp.where(hit, (flat % block_rows)[:, None], 0), axis=0)
+    row_label = block_rows + jnp.sum(
+        jnp.where(hit, (order // per_row - block_rows)[:, None], 0), axis=0
+    )
+    col_label = block_rows + jnp.sum(
+        jnp.where(hit, (flat % block_rows - block_rows)[:, None], 0), axis=0
+    )
     labels = jnp.stack([row_label.reshape(planes, slots), col_label.reshape(planes, slots)], axis=1)
     labels = jnp.pad(labels, ((0, 0), (0, TAIL - 2), (0, edge - slots))).astype(jnp.bfloat16)
     outgoing = pack(off_blocks.reshape(requests, edge, edge), to_plane, to_slot, labels, slots)
@@ -261,9 +348,7 @@
         diag_blocks, sketch, far, own, mirrors, block_rows * edge * peers
     )
     gram = sum_over_devices(part, peers)
-    lower = jnp.linalg.cholesky(gram)
-    basis = lax.linalg.triangular_solve(lower, image, left_side=False, lower=True, transpose_a=True)
-    return basis, lower.T
+    return factor_and_basis(gram, image)
 
 
 def solution(mesh):

time: 424 us -> 508 us (1.20); the launches traced: 416 us -> 506 us
  Pallas kernels: 86.2 us -> 249 us
  other arithmetic: 56 us -> 1.22 us
  starting transfers between devices: 41.1 us -> 21.4 us
  blocking collectives: 13.5 us -> 29 us
  local copies, waits for them, and re-layouts: 13.2 us -> 7.17 us
    pallas_call x0 -> x1, Pallas kernels: none -> 189 us  [factor_and_basis(): pl.pallas_call(functools.partial(factor_kernel, rounds), out_shape=(jax.S...]
    another operation x12 -> x1, other arithmetic: 54.7 us -> 0.01 us  [the longest x7 34.6 us: on_device(): lower = jnp.linalg.cholesky(gram)]
    all_to_all x1, waiting for transfers between devices: 38.2 us -> 52.7 us  [on_device(): far = lax.all_to_all(far, PLANE, 0, 0, tiled=True)]
    all_to_all x0 -> x1, blocking collectives: none -> 12.8 us  [sum_over_devices(): return lax.all_to_all(mine, ALL, 0, 0, tiled=True).reshape(rows, columns)]
    pallas_call x1, Pallas kernels: 25.1 us -> 13 us  [far_sum(): pl.pallas_call(functools.partial(far_kernel, most), out_shape=jax.ShapeDt...]
    all_to_all x1, starting transfers between devices: 16.3 us -> 4.96 us  [on_device(): far = lax.all_to_all(far, PLANE, 0, 0, tiled=True)]
    all_to_all x1 -> x0, waiting for transfers between devices: 10.4 us -> none  [sum_over_devices(): return lax.all_to_all(mine, ALL, 0, 0, tiled=True).reshape(rows, columns)]
    pallas_call x4, Pallas kernels: 43.1 us -> 33.9 us  [mirror_sum(): pl.pallas_call(functools.partial(mirror_kernel, shift, most), out_shape=j...]
  transfers between devices with their start and end apart: 10 -> 9, of which waited for: 4 -> 3; matrix products, arithmetic and copies ran while one was open for 1% -> 0% of each run, Pallas kernels for 17% -> 10%
where the time goes in v2:
time: 508 us; the launch traced here: 506 us
  Pallas kernels  249 us (49%)
  waiting for transfers between devices  185 us (36%)
  blocking collectives  29 us (6%)
  starting transfers between devices  21.4 us (4%)
  between operations  14.2 us (3%)
  local copies, waits for them, and re-layouts  7.17 us (1%)
    pallas_call x1, Pallas kernels, factor_and_basis(): pl.pallas_call(functools.partial(factor_kernel, rounds), out_shape=(jax.S...  189 us
    all_to_all x1, waiting for transfers between devices, on_device(): blocks = lax.all_to_all(outgoing, PLANE, 0, 0, tiled=True)  122 us
    all_to_all x1, waiting for transfers between devices, on_device(): far = lax.all_to_all(far, PLANE, 0, 0, tiled=True)  52.7 us
    pallas_call x4, Pallas kernels, mirror_sum(): pl.pallas_call(functools.partial(mirror_kernel, shift, most), out_shape=j...  33.9 us
    all_to_all x1, blocking collectives, sum_over_devices(): lax.all_to_all(part.reshape(peers, rows // peers, columns), ALL, 0, 0, ti...  16.1 us
    pallas_call x1, Pallas kernels, far_sum(): pl.pallas_call(functools.partial(far_kernel, most), out_shape=jax.ShapeDt...  13 us
    all_to_all x1, blocking collectives, sum_over_devices(): return lax.all_to_all(mine, ALL, 0, 0, tiled=True).reshape(rows, columns)  12.8 us
  transfers between devices with their start and end apart: 9, of which 3 were waited for; matrix products, arithmetic and copies ran while one was open for 0% of the time, Pallas kernels for 10%

profile of v2, /device:TPU:0, one launch (start us, length us, event | category | flops | bytes accessed | tf_op | source)
XLA Modules:
  0.0 506.4 jit_solution(7880557900229216485)
XLA Ops:
  9.3 2.2 copy-done.2
  11.5 2.6 pack.1
  14.1 5.3 %all-to-all-start = ((bf16[8,4112,128]{2,1,0:T(8,128)(2,1)}), bf16[8,4112,128]{2,1,0:T(8,128)(2,1)}, u32[]{:S(2)}, u32[]{:S(2)}) async-start(bf16[8,4112,128]{2,1,0:T(8,128)(2,1)} %pack.1), calls=%async_computation | async-start | bytes 16842752 | tf_op jit(solution)/shard_map/all_to_all | solution.py:327
  19.4 5.0 collective-permute-start
  24.4 1.0 collective-permute-start.2
  25.4 121.7 %all-to-all-done.block_ref = bf16[8,4112,128]{2,1,0:T(8,128)(2,1)} async-done(((bf16[8,4112,128]{2,1,0:T(8,128)(2,1)}), bf16[8,4112,128]{2,1,0:T(8,128)(2,1)}, u32[]{:S(2)}, u32[]{:S(2)}) %all-to-all-start) | async-done | bytes 8421408 | tf_op jit(solution)/shard_map/all_to_all | solution.py:327
  147.1 0.8 slice_convert_fusion
  148.0 13.0 %far.1 = bf16[8,2048,256]{2,1,0:T(8,128)(2,1)} custom-call(s32[8,32]{1,0:T(8,128)S(1)} %bitcast.14, s32[8,32]{1,0:T(8,128)S(1)} %bitcast.9, bf16[8,4112,128]{2,1,0:T(8,128)(2,1)} %all-to-all-done.block_ref, bf16[2048,256]{1,0:T(8,128)(2,1)S(1)} %copy-done, bf16[2048,256]{1,0:T(8,128)(2,1)S(1)} %collective-permute-done.rest_1_, ...), custom_call_target="tpu_custom_call" | custom-call | flops 2155872256 | bytes 16809984 | tf_op jit(solution)/shard_map/far/pallas_call | solution.py:145
  161.0 5.0 all-to-all-start.1
  166.0 8.2 %mirror.7 = bf16[2048,256]{1,0:T(8,128)(2,1)S(1)} custom-call(s32[8,32]{1,0:T(8,128)S(1)} %bitcast.15, s32[8,32]{1,0:T(8,128)S(1)} %bitcast.10, bf16[8,4112,128]{2,1,0:T(8,128)(2,1)} %all-to-all-done.block_ref, bf16[8,2048,256]{2,1,0:T(8,128)(2,1)} %bitcast.19), custom_call_target="tpu_custom_call" | custom-call | flops 536870912 | bytes 10485760 | tf_op jit(solution)/shard_map/mirror/pallas_call | solution.py:103
  174.2 4.0 collective-permute-start.5
  178.2 8.2 %mirror.6 = bf16[2048,256]{1,0:T(8,128)(2,1)S(1)} custom-call(s32[8,32]{1,0:T(8,128)S(1)} %bitcast.16, s32[8,32]{1,0:T(8,128)S(1)} %bitcast.11, bf16[8,4112,128]{2,1,0:T(8,128)(2,1)} %all-to-all-done.block_ref, bf16[8,2048,256]{2,1,0:T(8,128)(2,1)} %bitcast.20), custom_call_target="tpu_custom_call" | custom-call | flops 536870912 | bytes 10485760 | tf_op jit(solution)/shard_map/mirror/pallas_call | solution.py:103
  186.5 9.2 %mirror.5 = bf16[2048,256]{1,0:T(8,128)(2,1)} custom-call(s32[8,32]{1,0:T(8,128)S(1)} %bitcast.17, s32[8,32]{1,0:T(8,128)S(1)} %bitcast.12, bf16[8,4112,128]{2,1,0:T(8,128)(2,1)} %all-to-all-done.block_ref, bf16[8,2048,256]{2,1,0:T(8,128)(2,1)} %bitcast.21), custom_call_target="tpu_custom_call" | custom-call | flops 536870912 | bytes 10485760 | tf_op jit(solution)/shard_map/mirror/pallas_call | solution.py:103
  195.7 1.1 collective-permute-start.3
  196.8 8.2 %mirror.4.own_ref = f32[2048,256]{1,0:T(8,128)S(1)} custom-call(s32[8,32]{1,0:T(8,128)S(1)} %bitcast.18, s32[8,32]{1,0:T(8,128)S(1)} %bitcast.13, bf16[8,4112,128]{2,1,0:T(8,128)(2,1)} %all-to-all-done.block_ref, bf16[8,2048,256]{2,1,0:T(8,128)(2,1)} %bitcast.22), custom_call_target="tpu_custom_call" | custom-call | flops 536870912 | bytes 10485760 | tf_op jit(solution)/shard_map/mirror/pallas_call | solution.py:103
  205.0 1.3 copy-done.1
  206.3 52.7 %all-to-all-done.1.far_ref = bf16[8,2048,256]{2,1,0:T(8,128)(2,1)} async-done(((bf16[8,2048,256]{2,1,0:T(8,128)(2,1)}), bf16[8,2048,256]{2,1,0:T(8,128)(2,1)}, u32[]{:S(2)}, u32[]{:S(2)}) %all-to-all-start.1) | async-done | bytes 8388640 | tf_op jit(solution)/shard_map/all_to_all | solution.py:344
  259.1 9.6 %collective-permute-done.4.rest_1_ = bf16[2048,256]{1,0:T(8,128)(2,1)} collective-permute-done((bf16[2048,256]{1,0:T(8,128)(2,1)S(1)}, bf16[2048,256]{1,0:T(8,128)(2,1)}, u32[]{:S(2)}, u32[]{:S(2)}) %collective-permute-start.4) | collective-permute-done | bytes 1048608 | tf_op jit(solution)/shard_map/ppermute | solution.py:342
  268.7 1.0 copy-done.4
  269.7 10.1 %image.1 = (f32[2048,256]{1,0:T(8,128)}, f32[256,256]{1,0:T(8,128)S(1)}) custom-call(bf16[16,128,128]{2,1,0:T(8,128)(2,1)S(1)} %copy-done.4, bf16[2048,256]{1,0:T(8,128)(2,1)S(1)} %copy-done, bf16[8,2048,256]{2,1,0:T(8,128)(2,1)} %all-to-all-done.1.far_ref, f32[2048,256]{1,0:T(8,128)} %copy-done.1, bf16[2048,256]{1,0:T(8,128)(2,1)} %collective-permute-done.3.rest_0_, ...), custom_call_target="tpu_custom_call" | custom-call | tf_op jit(solution)/shard_map/image/pallas_call | solution.py:199
  279.8 16.1 %all_to_all.20 = f32[32,8,256]{2,1,0:T(8,128)S(1)} all-to-all(f32[32,8,256]{2,1,0:T(8,128)S(1)} %bitcast.8), channel_id=1, replica_groups=mesh['z'=4,'x'=2,'y'=2,'c'=2] {'z','x','y','c'}, dimensions={0} | all-to-all | bytes 524288 | tf_op jit(solution)/shard_map/all_to_all | solution.py:292
  296.1 12.8 %all_to_all.21 = f32[32,8,256]{2,1,0:T(8,128)S(1)} all-to-all(f32[32,8,256]{2,1,0:T(8,128)S(1)} %broadcast_in_dim.32), channel_id=1, replica_groups=mesh['z'=4,'x'=2,'y'=2,'c'=2] {'z','x','y','c'}, dimensions={0} | all-to-all | bytes 524288 | tf_op jit(solution)/shard_map/all_to_all | solution.py:294
  308.9 1.6 copy-done.3
  310.5 189.1 %factor.1 = (f32[2048,256]{1,0:T(8,128)}, f32[256,256]{1,0:T(8,128)}) custom-call(f32[256,256]{1,0:T(8,128)S(1)} %bitcast.7, f32[2048,256]{1,0:T(8,128)S(1)} %copy-done.3), custom_call_target="tpu_custom_call" | custom-call | tf_op jit(solution)/shard_map/factor/pallas_call | solution.py:278
  (29 shorter events, 2.3 us)
Async XLA Ops:
  7.2 158.8 %all-gather.3.cloned.1.call-start = ((), (), s32[]{:S(2)}) async-start(), calls=%async_computation.4 | async-start | bytes 9437184 | tf_op jit(solution)/shard_map/all_gather | solution.py:328
  9.3 2.2 copy-start.2
  14.1 5.3 %copy-start = (bf16[2048,256]{1,0:T(8,128)(2,1)S(1)}, bf16[2048,256]{1,0:T(8,128)(2,1)}, u32[]{:S(2)}) copy-start(bf16[2048,256]{1,0:T(8,128)(2,1)} %omega_ref.1) | copy-start | bytes 3145732
  14.1 133.0 %all-to-all-start = ((bf16[8,4112,128]{2,1,0:T(8,128)(2,1)}), bf16[8,4112,128]{2,1,0:T(8,128)(2,1)}, u32[]{:S(2)}, u32[]{:S(2)}) async-start(bf16[8,4112,128]{2,1,0:T(8,128)(2,1)} %pack.1), calls=%async_computation | async-start | bytes 16842752 | tf_op jit(solution)/shard_map/all_to_all | solution.py:327
  19.4 128.5 %collective-permute-start = (bf16[2048,256]{1,0:T(8,128)(2,1)S(1)}, bf16[2048,256]{1,0:T(8,128)(2,1)S(1)}, u32[]{:S(2)}, u32[]{:S(2)}) collective-permute-start(bf16[2048,256]{1,0:T(8,128)(2,1)S(1)} %copy-done), channel_id=1, source_target_pairs={{0,24},{8,0},{16,8},{24,16},{1,25},{9,1},{17,9},{25,17},{2,26},{10... | collective-permute-start | bytes 3145736 | tf_op jit(solution)/shard_map/ppermute | solution.py:332
  24.4 123.5 %collective-permute-start.1 = (bf16[2048,256]{1,0:T(8,128)(2,1)S(1)}, bf16[2048,256]{1,0:T(8,128)(2,1)S(1)}, u32[]{:S(2)}, u32[]{:S(2)}) collective-permute-start(bf16[2048,256]{1,0:T(8,128)(2,1)S(1)} %copy-done), channel_id=1, source_target_pairs={{0,16},{8,24},{16,0},{24,8},{1,17},{9,25},{17,1},{25,9},{2,18},{10... | collective-permute-start | bytes 3145736 | tf_op jit(solution)/shard_map/ppermute | solution.py:332
  24.4 123.5 %collective-permute-start.2 = (bf16[2048,256]{1,0:T(8,128)(2,1)S(1)}, bf16[2048,256]{1,0:T(8,128)(2,1)}, u32[]{:S(2)}, u32[]{:S(2)}) collective-permute-start(bf16[2048,256]{1,0:T(8,128)(2,1)S(1)} %copy-done), channel_id=1, source_target_pairs={{0,8},{8,16},{16,24},{24,0},{1,9},{9,17},{17,25},{25,1},{2,10},{10... | collective-permute-start | bytes 3145736 | tf_op jit(solution)/shard_map/ppermute | solution.py:332
  161.0 98.1 %all-to-all-start.1 = ((bf16[8,2048,256]{2,1,0:T(8,128)(2,1)}), bf16[8,2048,256]{2,1,0:T(8,128)(2,1)}, u32[]{:S(2)}, u32[]{:S(2)}) async-start(bf16[8,2048,256]{2,1,0:T(8,128)(2,1)} %far.1), calls=%async_computation.1 | async-start | bytes 16777216 | tf_op jit(solution)/shard_map/all_to_all | solution.py:344
  174.2 84.9 %collective-permute-start.5 = (bf16[2048,256]{1,0:T(8,128)(2,1)S(1)}, bf16[2048,256]{1,0:T(8,128)(2,1)}, u32[]{:S(2)}, u32[]{:S(2)}) collective-permute-start(bf16[2048,256]{1,0:T(8,128)(2,1)S(1)} %mirror.7), channel_id=1, source_target_pairs={{0,24},{8,0},{16,8},{24,16},{1,25},{9,1},{17,9},{25,17},{2,26},{10... | collective-permute-start | bytes 3145736 | tf_op jit(solution)/shard_map/ppermute | solution.py:342
  186.4 82.3 %collective-permute-start.4 = (bf16[2048,256]{1,0:T(8,128)(2,1)S(1)}, bf16[2048,256]{1,0:T(8,128)(2,1)}, u32[]{:S(2)}, u32[]{:S(2)}) collective-permute-start(bf16[2048,256]{1,0:T(8,128)(2,1)S(1)} %mirror.6), channel_id=1, source_target_pairs={{0,16},{8,24},{16,0},{24,8},{1,17},{9,25},{17,1},{25,9},{2,18},{10... | collective-permute-start | bytes 3145736 | tf_op jit(solution)/shard_map/ppermute | solution.py:342
  195.7 73.0 %collective-permute-start.3 = (bf16[2048,256]{1,0:T(8,128)(2,1)}, bf16[2048,256]{1,0:T(8,128)(2,1)}, u32[]{:S(2)}, u32[]{:S(2)}) collective-permute-start(bf16[2048,256]{1,0:T(8,128)(2,1)} %mirror.5), channel_id=1, source_target_pairs={{0,8},{8,16},{16,24},{24,0},{1,9},{9,17},{17,25},{25,1},{2,10},{10... | collective-permute-start | bytes 3145736 | tf_op jit(solution)/shard_map/ppermute | solution.py:342
  205.0 1.3 copy-start.1
  268.7 1.0 copy-start.4
  308.9 1.6 copy-start.3
Sparse Core Ops, SparseCore 0:
  9.9 132.4 all-gather.2

commit v3 on v2

v3 whole, which is shorter than its diff:
```python
import functools
import math

import jax
import jax.numpy as jnp
from jax import lax
from jax.experimental import pallas as pl
from jax.experimental.pallas import tpu as pltpu
from jax.sharding import Mesh
from jax.sharding import PartitionSpec as P

LINE = "z"
PLANE = ("x", "y", "c")
ALL = (LINE,) + PLANE
CHIPS, CORE = PLANE[:2], PLANE[2]
VMEM_LIMIT = 48 * 1024 * 1024
COST = pl.CostEstimate(flops=10**12, bytes_accessed=10**11, transcendentals=0)
TAIL = 16


def dot(a, b, contract=((1,), (0,)), precision=None):
    return lax.dot_general(
        a, b, (contract, ((), ())), precision=precision, preferred_element_type=jnp.float32
    )


NT = ((1,), (1,))
TN = ((0,), (0,))


def params():
    return pltpu.CompilerParams(vmem_limit_bytes=VMEM_LIMIT)


def split(a):
    high = a.astype(jnp.bfloat16)
    return high, (a - high.astype(jnp.float32)).astype(jnp.bfloat16)

def dot3(a, b, contract=((1,), (0,))):
    (ah, al), (bh, bl) = a, b
    return dot(ah, bh, contract) + (dot(ah, bl, contract) + dot(al, bh, contract))

def pack_kernel(entry_ref, plane_ref, slot_ref, count_ref, off_ref, label_ref, *rest):
    *out_refs, sem, label_sem = rest
    _, edge, _ = off_ref.shape
    tail = label_ref.shape[1]
    first = out_refs[0]
    labels = pltpu.make_async_copy(
        label_ref, first.at[:, pl.ds(first.shape[1] - tail, tail), :], label_sem
    )
    labels.start()
    for part, out_ref in enumerate(out_refs):

        def send(place, carry, out_ref=out_ref):
            row = pl.multiple_of(slot_ref[place] * edge, edge)
            pltpu.make_async_copy(
                off_ref.at[entry_ref[place]], out_ref.at[plane_ref[place], pl.ds(row, edge), :], sem
            ).start()
            return carry

        lax.fori_loop(count_ref[part], count_ref[part + 1], send, 0)
    pltpu.make_async_copy(off_ref, off_ref, sem).wait()
    labels.wait()


def pack(off, route, labels, parts):
    count, edge, _ = off.shape
    planes, tail, _ = labels.shape
    lengths = [slots * edge + (tail if index == 0 else 0) for index, slots in enumerate(parts)]
    anywhere = pl.BlockSpec(memory_space=pl.ANY)
    return pl.pallas_call(
        pack_kernel,
        out_shape=[jax.ShapeDtypeStruct((planes, length, edge), off.dtype) for length in lengths],
        grid_spec=pltpu.PrefetchScalarGridSpec(
            num_scalar_prefetch=len(route),
            grid=(),
            in_specs=[pl.BlockSpec(memory_space=pltpu.VMEM), anywhere],
            out_specs=[anywhere] * len(parts),
            scratch_shapes=[pltpu.SemaphoreType.DMA, pltpu.SemaphoreType.DMA],
        ),
        compiler_params=params(),
        cost_estimate=COST,
        name="pack",
    )(*route, off, labels)


def hold_kernel(x_ref, *rest):
    del x_ref, rest


def hold(x, after):
    anywhere = pl.BlockSpec(memory_space=pl.ANY)
    return pl.pallas_call(
        hold_kernel,
        out_shape=jax.ShapeDtypeStruct(x.shape, x.dtype),
        in_specs=[anywhere] * (1 + len(after)),
        out_specs=anywhere,
        input_output_aliases={0: 0},
        cost_estimate=COST,
        name="hold",
    )(x, *after)


def mirror_kernel(begin, most, row_ref, col_ref, block_ref, omega_ref, *rest):
    out_ref, total = rest[-2:]
    source = pl.program_id(0)
    edge = block_ref.shape[2]
    spare = total.shape[0] - 1

    @pl.when(source == 0)
    def _():
        total[...] = jnp.zeros_like(total)

    for m in range(most):
        row = jnp.minimum(row_ref[source, begin + m], spare - 1)
        col = col_ref[source, begin + m]
        block = block_ref[0, m * edge : (m + 1) * edge, :]
        omega = omega_ref[0, pl.ds(pl.multiple_of(row * edge, edge), edge), :]
        product = dot(block, omega, ((0,), (0,))).astype(jnp.bfloat16)
        total[col] += product.astype(jnp.float32)

    @pl.when(source == pl.num_programs(0) - 1)
    def _():
        out_ref[...] = total[:spare].reshape(out_ref.shape).astype(out_ref.dtype)


def mirror_sum(blocks, omegas, rows, cols, inside, begin, most, block_rows, dtype, after=()):
    planes, _, edge = blocks.shape
    _, height, columns = omegas.shape
    return pl.pallas_call(
        functools.partial(mirror_kernel, begin, most),
        out_shape=jax.ShapeDtypeStruct((height, columns), dtype),
        grid_spec=pltpu.PrefetchScalarGridSpec(
            num_scalar_prefetch=2,
            grid=(planes,),
            in_specs=[
                pl.BlockSpec((1, most * edge, edge), lambda p, *_: (p, inside, 0)),
                pl.BlockSpec((1, height, columns), lambda p, *_: (p, 0, 0)),
            ]
            + [pl.BlockSpec(memory_space=pl.ANY)] * len(after),
            out_specs=pl.BlockSpec((height, columns), lambda p, *_: (0, 0)),
            scratch_shapes=[pltpu.VMEM((block_rows + 1, edge, columns), jnp.float32)],
        ),
        compiler_params=params(),
        cost_estimate=COST,
        name="mirror",
    )(rows, cols, blocks, omegas, *after)


def far_kernel(most, parts, lines, added, source_ref, place_ref, row_ref, col_ref, *rest):
    del place_ref
    part_refs, omega_refs = rest[:parts], rest[parts : parts + lines]
    out_ref, total = rest[-2:]
    source = source_ref[pl.program_id(0)]
    edge = part_refs[0].shape[2]
    spare = total.shape[0] - 1
    if added:
        total[:spare] = rest[parts + lines][0].reshape(spare, edge, -1)
    else:
        total[...] = jnp.zeros_like(total)
    each = len(omega_refs) // parts
    for index, omega_ref in enumerate(omega_refs):
        for m in range(most):
            row = row_ref[source, index * most + m]
            col = jnp.minimum(col_ref[source, index * most + m], spare - 1)
            slot = index % each * most + m
            block = part_refs[index // each][0, slot * edge : (slot + 1) * edge, :]
            omega = omega_ref[pl.ds(pl.multiple_of(col * edge, edge), edge), :]
            total[row] += dot(block, omega)
    out_ref[0] = total[:spare].reshape(out_ref.shape[1:]).astype(out_ref.dtype)


def far_sum(
    sources, places, slots, parts, omegas, rows, cols, most, block_rows, dtype, add=None, after=()
):
    edge = parts[0].shape[2]
    height, columns = omegas[0].shape
    more = [] if add is None else [add]
    return pl.pallas_call(
        functools.partial(far_kernel, most, len(parts), len(omegas), len(more)),
        out_shape=jax.ShapeDtypeStruct((slots, height, columns), dtype),
        grid_spec=pltpu.PrefetchScalarGridSpec(
            num_scalar_prefetch=4,
            grid=sources.shape,
            in_specs=[
                pl.BlockSpec((1, part.shape[1], edge), lambda k, source, *_: (source[k], 0, 0))
                for part in parts
            ]
            + [pl.BlockSpec((height, columns), lambda k, *_: (0, 0))] * len(omegas)
            + [pl.BlockSpec((1, height, columns), lambda k, *_: (k, 0, 0))] * len(more)
            + [pl.BlockSpec(memory_space=pl.ANY)] * len(after),
            out_specs=pl.BlockSpec(
                (1, height, columns), lambda k, source, place, *_: (place[k], 0, 0)
            ),
            scratch_shapes=[pltpu.VMEM((block_rows + 1, edge, columns), jnp.float32)],
        ),
        compiler_params=params(),
        cost_estimate=COST,
        name="far",
    )(sources, places, rows, cols, *parts, *omegas, *more, *after)


def image_kernel(scale, chip_ref, diag_ref, omega_ref, far_ref, *rest):
    *piece_refs, image_ref, gram_ref, cross = rest
    step = pl.program_id(0)
    edge = diag_ref.shape[1]
    near = [
        dot(diag_ref[b], omega_ref[b * edge : (b + 1) * edge, :]) for b in range(diag_ref.shape[0])
    ]
    image = jnp.concatenate(near, axis=0)
    for piece_ref in piece_refs:
        image += piece_ref[...].astype(jnp.float32)
    for chip in range(far_ref.shape[0]):
        piece = far_ref[chip].astype(jnp.float32)
        image += jnp.where(chip == chip_ref[0], 0.0, piece)
    image_ref[...] = image

    @pl.when(step == 0)
    def _():
        gram_ref[...] = jnp.zeros_like(gram_ref)
        cross[...] = jnp.zeros_like(cross)

    high, low = split(image)
    gram_ref[...] += dot(high, high, TN)
    cross[...] += dot(high, low, TN)

    @pl.when(step == pl.num_programs(0) - 1)
    def _():
        gram_ref[...] = (gram_ref[...] + (cross[...] + cross[...].T)) * scale


def image_and_gram(diag, sketch, chip, far, pieces, total_rows):
    block_rows, edge, _ = diag.shape
    height, columns = sketch.shape
    together = math.gcd(block_rows, 2)
    rows = pl.BlockSpec((together * edge, columns), lambda b, _: (b, 0))
    return pl.pallas_call(
        functools.partial(image_kernel, 1.0 / total_rows),
        out_shape=(
            jax.ShapeDtypeStruct((height, columns), jnp.float32),
            jax.ShapeDtypeStruct((columns, columns), jnp.float32),
        ),
        grid_spec=pltpu.PrefetchScalarGridSpec(
            num_scalar_prefetch=1,
            grid=(block_rows // together,),
            in_specs=[
                pl.BlockSpec((together, edge, edge), lambda b, _: (b, 0, 0)),
                rows,
                pl.BlockSpec((far.shape[0], together * edge, columns), lambda b, _: (0, b, 0)),
            ]
            + [rows] * len(pieces),
            out_specs=(rows, pl.BlockSpec((columns, columns), lambda b, _: (0, 0))),
            scratch_shapes=[pltpu.VMEM((columns, columns), jnp.float32)],
        ),
        compiler_params=params(),
        cost_estimate=COST,
        name="image",
    )(chip.reshape(1), diag, sketch, far, *pieces)


def factor_kernel(rounds, gram_ref, image_ref, basis_ref, factor_ref, inverse, work):
    n = gram_ref.shape[0]
    exact = lax.Precision.HIGHEST

    @pl.when(pl.program_id(0) == 0)
    def _():
        gram = gram_ref[...]
        row = lax.broadcasted_iota(jnp.int32, (n, n), 0)
        col = lax.broadcasted_iota(jnp.int32, (n, n), 1)
        weight = jnp.where(row > col, 1.0, jnp.where(row == col, 0.5, 0.0))
        one = jnp.where(row == col, 1.0, 0.0)
        diagonal = jnp.where(row == col, gram, 0.0)
        down = lax.rsqrt(jnp.sum(diagonal, axis=1, keepdims=True))
        across = lax.rsqrt(jnp.sum(diagonal, axis=0, keepdims=True))
        scaled = gram * down * across
        step = one - weight * (scaled - one)
        guess = step
        for turn in range(rounds):
            if turn == rounds - 1:
                error = dot(dot(guess, scaled, precision=exact), guess, NT, precision=exact) - one
                step = weight * error
                guess = guess - dot(step, guess, precision=exact)
            else:
                g3 = split(guess)
                error = dot3(split(dot3(g3, split(scaled))), g3, NT) - one
                guess = guess - dot3(split(weight * error), g3)
        guess = jnp.where(row >= col, guess, 0.0)
        inverse[...] = guess * across
        factor_ref[...] = jnp.where(row <= col, dot(inverse[...], gram, precision=exact), 0.0)
        size = jnp.sum(error * error)

        @pl.when(jnp.logical_not(size < 1e-6))
        def _():
            work[...] = gram
            inverse[...] = one
            lane = lax.broadcasted_iota(jnp.int32, (1, n), 1)

            def eliminate(j, carry):
                line = work[pl.ds(j, 1), :]
                pivot = jnp.sum(jnp.where(lane == j, line, 0.0), axis=1, keepdims=True)
                scale = lax.rsqrt(pivot)
                line = jnp.where(lane >= j, line * scale, 0.0)
                other = inverse[pl.ds(j, 1), :] * scale
                below = jnp.where(lane > j, line, 0.0)
                work[...] -= dot(below, line, TN, exact)
                inverse[...] -= dot(below, other, TN, exact)
                inverse[pl.ds(j, 1), :] = other
                factor_ref[pl.ds(j, 1), :] = line
                return carry

            lax.fori_loop(0, n, eliminate, 0)

    basis_ref[...] = dot3(split(image_ref[...]), split(inverse[...]), NT)

def factor_and_basis(gram, image, tile=256, rounds=3):
    height, n = image.shape
    whole = pl.BlockSpec((n, n), lambda b: (0, 0))
    tiles = pl.BlockSpec((tile, n), lambda b: (b, 0))
    return pl.pallas_call(
        functools.partial(factor_kernel, rounds),
        out_shape=(jax.ShapeDtypeStruct((height, n), jnp.float32), jax.ShapeDtypeStruct((n, n), jnp.float32)),
        grid=(height // tile,),
        in_specs=[whole, tiles],
        out_specs=(tiles, whole),
        scratch_shapes=[pltpu.VMEM((n, n), jnp.float32)] * 2,
        compiler_params=params(),
        name="factor",
    )(gram, image)


def sum_over_devices(part, peers):
    rows, columns = part.shape
    pieces = lax.all_to_all(part.reshape(peers, rows // peers, columns), ALL, 0, 0, tiled=True)
    mine = jnp.broadcast_to(jnp.sum(pieces, axis=0), pieces.shape)
    return lax.all_to_all(mine, ALL, 0, 0, tiled=True).reshape(rows, columns)


def on_device(diag_blocks, off_blocks, col_blocks, sketch):
    block_rows, per_row = col_blocks.shape
    edge = diag_blocks.shape[1]
    layers = lax.axis_size(LINE)
    planes = lax.axis_size(PLANE)
    peers = layers * planes
    requests = block_rows * per_row
    most = max(2, (2 * requests + peers - 1) // peers)
    slots = layers * most
    layer = lax.axis_index(LINE)
    shifts = sorted(range(layers), key=lambda shift: -min(shift, layers - shift))
    halves = math.gcd(layers, 2)

    flat = col_blocks.reshape(requests)
    owners = flat // block_rows
    order = jnp.arange(requests)
    earlier = (owners[:, None] == owners[None, :]) & (order[None, :] < order[:, None])
    ranks = jnp.sum(earlier.astype(jnp.int32), axis=1)
    to_plane = owners % planes
    away = lax.rem(owners // planes - layer + layers, layers)
    turn = sum(jnp.where(away == shift, index, 0) for index, shift in enumerate(shifts))
    to_slot = turn * most + ranks
    place = to_plane * slots + to_slot
    hit = place[:, None] == jnp.arange(planes * slots)[None, :]
    row_label = block_rows + jnp.sum(
        jnp.where(hit, (order // per_row - block_rows)[:, None], 0), axis=0
    )
    col_label = block_rows + jnp.sum(
        jnp.where(hit, (flat % block_rows - block_rows)[:, None], 0), axis=0
    )
    labels = jnp.stack([row_label.reshape(planes, slots), col_label.reshape(planes, slots)], axis=1)
    labels = jnp.pad(labels, ((0, 0), (0, TAIL - 2), (0, edge - slots))).astype(jnp.bfloat16)
    in_part = to_slot // (slots // halves)
    before = jnp.sum(
        (in_part[None, :] < in_part[:, None])
        | ((in_part[None, :] == in_part[:, None]) & (order[None, :] < order[:, None])),
        axis=1,
    )
    pick = before[None, :] == order[:, None]
    route = [
        jnp.sum(jnp.where(pick, values[None, :], 0), axis=1)
        for values in (order, to_plane, to_slot % (slots // halves))
    ]
    counts = jnp.sum(in_part[None, :] < jnp.arange(halves + 1)[:, None], axis=1)
    outgoing = pack(
        off_blocks.reshape(requests, edge, edge), route + [counts], labels, [slots // halves] * halves
    )

    plane_omegas = lax.all_gather(sketch, PLANE)
    line_omegas = []
    for shift in shifts:
        steps = [(z, (z - shift) % layers) for z in range(layers)]
        line_omegas.append(lax.ppermute(sketch, LINE, steps) if shift else sketch)
    parts = []
    for part in outgoing:
        part = hold(part, line_omegas) if parts else part
        parts.append(lax.all_to_all(part, PLANE, 0, 0, tiled=True))
    lines = slots // halves * edge
    rows = parts[0][:, lines, :slots].astype(jnp.int32)
    cols = parts[0][:, lines + 1, :slots].astype(jnp.int32)

    pieces = []
    latest = ()

    def send_mirror(index, after):
        part, inside = divmod(index, layers // halves)
        shift = shifts[index]
        kind = jnp.bfloat16 if shift else jnp.float32
        mirror = mirror_sum(
            parts[part], plane_omegas, rows, cols, inside, index * most, most, block_rows, kind, after
        )
        steps = [(z, (z + shift) % layers) for z in range(layers)]
        pieces.append(lax.ppermute(mirror, LINE, steps) if shift else mirror)
        return (mirror,)

    early = layers // halves
    for index in range(early):
        latest = send_mirror(index, latest)

    cores = lax.axis_size(CORE)
    chips = planes // cores
    chip, core = lax.axis_index(CHIPS), lax.axis_index(CORE)
    away = (chip + jnp.arange(1, chips)) % chips
    far = functools.partial(
        far_sum, parts=parts, omegas=line_omegas, rows=rows, cols=cols, most=most, block_rows=block_rows
    )

    def ask(chips_asked, after):
        if cores == 1:
            return None, after
        count = chips_asked.shape[0]
        other = far(
            chips_asked * cores + 1 - core, jnp.arange(count), count, dtype=jnp.float32, after=after
        )
        return lax.ppermute(other, CORE, [(0, 1), (1, 0)]), (other,)

    other, latest = ask(away, latest)
    for index in range(early, layers - 1):
        latest = send_mirror(index, latest)
    sent = far(away * cores + core, away, chips, dtype=jnp.bfloat16, add=other, after=latest)
    received = lax.all_to_all(sent, CHIPS, 0, 0, tiled=True)
    other, latest = ask(chip.reshape(1), (sent,))
    latest = send_mirror(layers - 1, latest)
    own = far(
        chip.reshape(1) * cores + core, jnp.arange(1), 1, dtype=jnp.float32, add=other, after=latest
    )
    pieces.append(own.reshape(sketch.shape))

    image, part = image_and_gram(
        diag_blocks, sketch, chip, received, pieces, block_rows * edge * peers
    )
    gram = sum_over_devices(part, peers)
    return factor_and_basis(gram, image)


def solution(mesh):
    rows, sub = mesh.devices.shape
    layers, cores = math.gcd(rows, 4), math.gcd(sub, 2)
    devices = mesh.devices.reshape(layers, rows // layers, sub // cores, cores)
    placed = (P(ALL, None, None), P(ALL, None, None, None), P(ALL, None), P(ALL, None))
    return jax.shard_map(
        on_device,
        mesh=Mesh(devices, ALL),
        in_specs=placed,
        out_specs=(P(ALL, None), P()),
        check_vma=False,
    )
```

time: 508 us -> 471 us (0.927)
  waiting for transfers between devices: 185 us -> 119 us
  Pallas kernels: 249 us -> 269 us
  starting transfers between devices: 21.4 us -> 27.7 us
    all_to_all x2 -> x3, waiting for transfers between devices: 174 us -> 48.6 us  [the longest x2 30 us: on_device(): parts.append(lax.all_to_all(part, PLANE, 0, 0, tiled=True))]
    ppermute x6 -> x8, waiting for transfers between devices: 9.62 us -> 59.7 us  [the longest x3 52.6 us: on_device(): line_omegas.append(lax.ppermute(sketch, LINE, steps) if shift else sketch)]
    pallas_call x6 -> x10, Pallas kernels: 49.5 us -> 70.6 us  [the longest x4 35.8 us: mirror_sum(): pl.pallas_call(functools.partial(mirror_kernel, begin, most), out_shape=j...]
    all_gather x1, waiting for transfers between devices: 0.02 us -> 10.8 us  [on_device(): plane_omegas = lax.all_gather(sketch, PLANE)]
    all_to_all x2 -> x3, starting transfers between devices: 10.3 us -> 14.1 us  [the longest x2 9.15 us: on_device(): parts.append(lax.all_to_all(part, PLANE, 0, 0, tiled=True))]
    ppermute x6 -> x8, starting transfers between devices: 11.1 us -> 13.6 us  [the longest x3 7.23 us: send_mirror(): pieces.append(lax.ppermute(mirror, LINE, steps) if shift else mirror)]
  transfers between devices with their start and end apart: 9 -> 12, of which waited for: 3 -> 7; matrix products, arithmetic and copies ran while one was open for 0% -> 1% of each run, Pallas kernels for 10% -> 15%
where the time goes in v3:
time: 471 us; the launch traced here: 470 us
  Pallas kernels  269 us (57%)
  waiting for transfers between devices  119 us (25%)
  blocking collectives  30.9 us (7%)
  starting transfers between devices  27.7 us (6%)
  between operations  14.2 us (3%)
  local copies, waits for them, and re-layouts  7.47 us (2%)
    pallas_call x1, Pallas kernels, factor_and_basis(): pl.pallas_call(functools.partial(factor_kernel, rounds), out_shape=(jax.S...  189 us
    ppermute x3, waiting for transfers between devices, on_device(): line_omegas.append(lax.ppermute(sketch, LINE, steps) if shift else sketch)  52.6 us
    pallas_call x4, Pallas kernels, mirror_sum(): pl.pallas_call(functools.partial(mirror_kernel, begin, most), out_shape=j...  35.8 us
    all_to_all x2, waiting for transfers between devices, on_device(): parts.append(lax.all_to_all(part, PLANE, 0, 0, tiled=True))  30 us
    pallas_call x4, Pallas kernels, far_sum(): pl.pallas_call(functools.partial(far_kernel, most, len(parts), len(omegas...  28.2 us
    all_to_all x1, waiting for transfers between devices, on_device(): received = lax.all_to_all(sent, CHIPS, 0, 0, tiled=True)  18.6 us
    all_to_all x1, blocking collectives, sum_over_devices(): lax.all_to_all(part.reshape(peers, rows // peers, columns), ALL, 0, 0, ti...  18.1 us
    all_to_all x1, blocking collectives, sum_over_devices(): return lax.all_to_all(mine, ALL, 0, 0, tiled=True).reshape(rows, columns)  12.8 us
  transfers between devices with their start and end apart: 12, of which 7 were waited for; matrix products, arithmetic and copies ran while one was open for 1% of the time, Pallas kernels for 15%

profile of v3, /device:TPU:0, one launch (start us, length us, event | category | flops | bytes accessed | tf_op | source)
XLA Modules:
  0.0 470.1 jit_solution(12580898915118757202)
XLA Ops:
  7.2 4.1 collective-permute-start
  15.3 6.5 %pack.1 = (bf16[8,2064,128]{2,1,0:T(8,128)(2,1)}, bf16[8,2048,128]{2,1,0:T(8,128)(2,1)S(1)}) custom-call(s32[128]{0:T(128)S(1)} %get-tuple-element.14.entry_ref, s32[128]{0:T(128)S(1)} %get-tuple-element.13.plane_ref, s32[128]{0:T(128)S(1)} %get-tuple-element.12.slot_ref, s32[3]{0:T(128)S(1)} %convert_reduce_fusion.2.count_ref, ...), custom_call_target="tpu_custom_call" | custom-call | flops 999999995904 | bytes 99999997952 | tf_op jit(solution)/shard_map/pack/pallas_call | solution.py:71
  23.8 4.6 all-to-all-start
  28.4 30.6 %collective-permute-done.rest_0_.rest_2_ = bf16[2048,256]{1,0:T(8,128)(2,1)} collective-permute-done((bf16[2048,256]{1,0:T(8,128)(2,1)}, bf16[2048,256]{1,0:T(8,128)(2,1)}, u32[]{:S(2)}, u32[]{:S(2)}) %collective-permute-start) | collective-permute-done | bytes 1048608 | tf_op jit(solution)/shard_map/ppermute | solution.py:390
  59.0 21.9 %collective-permute-done.2.rest_2_.rest_4_ = bf16[2048,256]{1,0:T(8,128)(2,1)} collective-permute-done((bf16[2048,256]{1,0:T(8,128)(2,1)}, bf16[2048,256]{1,0:T(8,128)(2,1)}, u32[]{:S(2)}, u32[]{:S(2)}) %collective-permute-start.2) | collective-permute-done | bytes 1048608 | tf_op jit(solution)/shard_map/ppermute | solution.py:390
  80.9 13.2 %all-to-all-done.block_ref.rest_0_ = bf16[8,2064,128]{2,1,0:T(8,128)(2,1)} async-done(((bf16[8,2064,128]{2,1,0:T(8,128)(2,1)}), bf16[8,2064,128]{2,1,0:T(8,128)(2,1)}, u32[]{:S(2)}, u32[]{:S(2)}) %all-to-all-start) | async-done | bytes 4227104 | tf_op jit(solution)/shard_map/all_to_all | solution.py:394
  94.2 4.6 all-to-all-start.1
  99.6 10.8 %all-gather.3.cloned.1.call-done = bf16[16384,256]{1,0:T(8,128)(2,1)} async-done(((bf16[2048,256]{1,0:T(8,128)(2,1)}), bf16[16384,256]{1,0:T(8,128)(2,1)}) %all-gather.3.cloned.1.call-update) | async-done | bytes 8388624 | tf_op jit(solution)/shard_map/all_gather | solution.py:386
  110.4 9.2 %mirror.4.rest_0_ = bf16[2048,256]{1,0:T(8,128)(2,1)} custom-call(s32[8,32]{1,0:T(8,128)S(1)} %bitcast.19, s32[8,32]{1,0:T(8,128)S(1)} %bitcast.11, bf16[8,2064,128]{2,1,0:T(8,128)(2,1)} %all-to-all-done.block_ref.rest_0_, bf16[8,2048,256]{2,1,0:T(8,128)(2,1)} %bitcast.27), custom_call_target="tpu_custom_call" | custom-call | flops 999999995904 | bytes 99999997952 | tf_op jit(solution)/shard_map/mirror/pallas_call | solution.py:130
  119.6 9.2 %mirror.5.rest_6_ = bf16[2048,256]{1,0:T(8,128)(2,1)} custom-call(s32[8,32]{1,0:T(8,128)S(1)} %bitcast.20, s32[8,32]{1,0:T(8,128)S(1)} %bitcast.12, bf16[8,2064,128]{2,1,0:T(8,128)(2,1)} %all-to-all-done.block_ref.rest_0_, bf16[8,2048,256]{2,1,0:T(8,128)(2,1)} %bitcast.28, bf16[2048,256]{1,0:T(8,128)(2,1)} %mirror.4.rest_0_), custom_call_target="tpu_custom_call" | custom-call | flops 999999995904 | bytes 99999997952 | tf_op jit(solution)/shard_map/mirror/pallas_call | solution.py:130
  132.7 16.7 %all-to-all-done.1.rest_1_.block_ref = bf16[8,2048,128]{2,1,0:T(8,128)(2,1)} async-done(((bf16[8,2048,128]{2,1,0:T(8,128)(2,1)}), bf16[8,2048,128]{2,1,0:T(8,128)(2,1)}, u32[]{:S(2)}, u32[]{:S(2)}) %all-to-all-start.1) | async-done | bytes 4194336 | tf_op jit(solution)/shard_map/all_to_all | solution.py:394
  149.4 8.1 %far.4.rest_0_ = f32[3,2048,256]{2,1,0:T(8,128)} custom-call(s32[3]{0:T(128)S(1)} %add_subtract_fusion.source_ref, s32[3]{0:T(128)S(1)} %iota.27.place_ref, s32[8,32]{1,0:T(8,128)S(1)} %bitcast.21, s32[8,32]{1,0:T(8,128)S(1)} %bitcast.13, bf16[8,2064,128]{2,1,0:T(8,128)(2,1)} %all-to-all-done.block_ref.rest_0_, ...), custom_call_target="tpu_custom_call" | custom-call | flops 999999995904 | bytes 99999997952 | tf_op jit(solution)/shard_map/far/pallas_call | solution.py:179
  157.5 9.2 %mirror.6.rest_7_ = bf16[2048,256]{1,0:T(8,128)(2,1)} custom-call(s32[8,32]{1,0:T(8,128)S(1)} %bitcast.22, s32[8,32]{1,0:T(8,128)S(1)} %bitcast.14, bf16[8,2048,128]{2,1,0:T(8,128)(2,1)} %all-to-all-done.1.rest_1_.block_ref, bf16[8,2048,256]{2,1,0:T(8,128)(2,1)} %bitcast.29, f32[3,2048,256]{2,1,0:T(8,128)} %far.4.rest_0_), custom_call_target="tpu_custom_call" | custom-call | flops 999999995904 | bytes 99999997952 | tf_op jit(solution)/shard_map/mirror/pallas_call | solution.py:130
  170.0 9.1 %far.5.rest_6_ = bf16[4,2048,256]{2,1,0:T(8,128)(2,1)} custom-call(s32[3]{0:T(128)S(1)} %get-tuple-element.25.source_ref, s32[3]{0:T(128)S(1)} %get-tuple-element.24.place_ref, s32[8,32]{1,0:T(8,128)S(1)} %bitcast.23, s32[8,32]{1,0:T(8,128)S(1)} %bitcast.15, bf16[8,2064,128]{2,1,0:T(8,128)(2,1)} %all-to-all-done.block_ref.rest_0_, ...), custom_call_target="tpu_custom_call" | custom-call | flops 999999995904 | bytes 99999997952 | tf_op jit(solution)/shard_map/far/pallas_call | solution.py:179
  179.2 4.9 %all-to-all-start.2 = ((bf16[4,2048,256]{2,1,0:T(8,128)(2,1)}), bf16[4,2048,256]{2,1,0:T(8,128)(2,1)}, u32[]{:S(2)}, u32[]{:S(2)}) async-start(bf16[4,2048,256]{2,1,0:T(8,128)(2,1)} %far.5.rest_6_), calls=%async_computation.2 | async-start | bytes 8388608 | tf_op jit(solution)/shard_map/all_to_all | solution.py:438
  184.1 5.1 %far.6.rest_0_ = f32[1,2048,256]{2,1,0:T(8,128)} custom-call(s32[1]{0:T(128)S(6)} %sub.64.source_ref, s32[1]{0:T(128)} %constant.127.clone.1.place_ref, s32[8,32]{1,0:T(8,128)S(1)} %bitcast.24, s32[8,32]{1,0:T(8,128)S(1)} %bitcast.16, bf16[8,2064,128]{2,1,0:T(8,128)(2,1)} %all-to-all-done.block_ref.rest_0_, ...), custom_call_target="tpu_custom_call" | custom-call | flops 999999995904 | bytes 99999997952 | tf_op jit(solution)/shard_map/far/pallas_call | solution.py:179
  191.0 8.2 %mirror.7.rest_7_.rest_3_ = f32[2048,256]{1,0:T(8,128)S(1)} custom-call(s32[8,32]{1,0:T(8,128)S(1)} %bitcast.25, s32[8,32]{1,0:T(8,128)S(1)} %bitcast.17, bf16[8,2048,128]{2,1,0:T(8,128)(2,1)} %all-to-all-done.1.rest_1_.block_ref, bf16[8,2048,256]{2,1,0:T(8,128)(2,1)} %bitcast.30, f32[1,2048,256]{2,1,0:T(8,128)S(1)} %copy-done.3), custom_call_target="tpu_custom_call" | custom-call | flops 999999995904 | bytes 99999997952 | tf_op jit(solution)/shard_map/mirror/pallas_call | solution.py:130
  200.6 5.8 %far.7 = f32[1,2048,256]{2,1,0:T(8,128)} custom-call(s32[1]{0:T(128)S(6)} %add.252.source_ref, s32[1]{0:T(128)} %constant.127.clone.1.place_ref, s32[8,32]{1,0:T(8,128)S(1)} %bitcast.26, s32[8,32]{1,0:T(8,128)S(1)} %bitcast.18, bf16[8,2064,128]{2,1,0:T(8,128)(2,1)} %all-to-all-done.block_ref.rest_0_, bf16[8,2048,128]{2,1,0:T(8,128)(2,1)} %all-to-all-done.1.rest_1_.block_ref, ...), custom_call_target="tpu_custom_call" | custom-call | flops 999999995904 | bytes 99999997952 | tf_op jit(solution)/shard_map/far/pallas_call | solution.py:179
  206.5 7.1 %collective-permute-done.6.rest_2_ = bf16[2048,256]{1,0:T(8,128)(2,1)} collective-permute-done((bf16[2048,256]{1,0:T(8,128)(2,1)}, bf16[2048,256]{1,0:T(8,128)(2,1)}, u32[]{:S(2)}, u32[]{:S(2)}) %collective-permute-start.6) | collective-permute-done | bytes 1048608 | tf_op jit(solution)/shard_map/ppermute | solution.py:410
  213.6 18.6 %all-to-all-done.2.far_ref = bf16[4,2048,256]{2,1,0:T(8,128)(2,1)} async-done(((bf16[4,2048,256]{2,1,0:T(8,128)(2,1)}), bf16[4,2048,256]{2,1,0:T(8,128)(2,1)}, u32[]{:S(2)}, u32[]{:S(2)}) %all-to-all-start.2) | async-done | bytes 4194336 | tf_op jit(solution)/shard_map/all_to_all | solution.py:438
  232.2 9.4 %image.1 = (f32[2048,256]{1,0:T(8,128)}, f32[256,256]{1,0:T(8,128)S(1)}) custom-call(s32[1]{0:T(128)} %bitcast.chip_ref, bf16[16,128,128]{2,1,0:T(8,128)(2,1)S(1)} %copy-done.4, bf16[2048,256]{1,0:T(8,128)(2,1)S(1)} %copy-done.2, bf16[4,2048,256]{2,1,0:T(8,128)(2,1)} %all-to-all-done.2.far_ref, bf16[2048,256]{1,0:T(8,128)(2,1)} %collective-permute-done.4.rest_0_, ...), custom_call_target="tpu_custom_call" | custom-call | flops 999999995904 | bytes 99999997952 | tf_op jit(solution)/shard_map/image/pallas_call | solution.py:237
  241.6 18.1 %all_to_all.25 = f32[32,8,256]{2,1,0:T(8,128)S(1)} all-to-all(f32[32,8,256]{2,1,0:T(8,128)S(1)} %bitcast.10), channel_id=1, replica_groups=mesh['z'=4,'x'=2,'y'=2,'c'=2] {'z','x','y','c'}, dimensions={0} | all-to-all | bytes 524288 | tf_op jit(solution)/shard_map/all_to_all | solution.py:333
  259.7 12.8 %all_to_all.26 = f32[32,8,256]{2,1,0:T(8,128)S(1)} all-to-all(f32[32,8,256]{2,1,0:T(8,128)S(1)} %broadcast_in_dim.80), channel_id=1, replica_groups=mesh['z'=4,'x'=2,'y'=2,'c'=2] {'z','x','y','c'}, dimensions={0} | all-to-all | bytes 524288 | tf_op jit(solution)/shard_map/all_to_all | solution.py:335
  274.1 189.1 %factor.1 = (f32[2048,256]{1,0:T(8,128)}, f32[256,256]{1,0:T(8,128)}) custom-call(f32[256,256]{1,0:T(8,128)S(1)} %bitcast.9, f32[2048,256]{1,0:T(8,128)S(1)} %copy-done.1), custom_call_target="tpu_custom_call" | custom-call | tf_op jit(solution)/shard_map/factor/pallas_call | solution.py:319
  (48 shorter events, 18.7 us)
Async XLA Ops:
  7.2 103.2 %all-gather.3.cloned.1.call-start = ((), (), s32[]{:S(2)}) async-start(), calls=%async_computation.5 | async-start | bytes 9437184 | tf_op jit(solution)/shard_map/all_gather | solution.py:386
  7.2 51.8 %collective-permute-start = (bf16[2048,256]{1,0:T(8,128)(2,1)}, bf16[2048,256]{1,0:T(8,128)(2,1)}, u32[]{:S(2)}, u32[]{:S(2)}) collective-permute-start(bf16[2048,256]{1,0:T(8,128)(2,1)} %omega_ref.1), channel_id=1, source_target_pairs={{0,16},{8,24},{16,0},{24,8},{1,17},{9,25},{17,1},{25,9},{2,18},{10... | collective-permute-start | bytes 3145736 | tf_op jit(solution)/shard_map/ppermute | solution.py:390
  11.3 47.7 %collective-permute-start.1 = (bf16[2048,256]{1,0:T(8,128)(2,1)}, bf16[2048,256]{1,0:T(8,128)(2,1)}, u32[]{:S(2)}, u32[]{:S(2)}) collective-permute-start(bf16[2048,256]{1,0:T(8,128)(2,1)} %omega_ref.1), channel_id=1, source_target_pairs={{0,24},{8,0},{16,8},{24,16},{1,25},{9,1},{17,9},{25,17},{2,26},{10... | collective-permute-start | bytes 3145736 | tf_op jit(solution)/shard_map/ppermute | solution.py:390
  12.7 68.3 %collective-permute-start.2 = (bf16[2048,256]{1,0:T(8,128)(2,1)}, bf16[2048,256]{1,0:T(8,128)(2,1)}, u32[]{:S(2)}, u32[]{:S(2)}) collective-permute-start(bf16[2048,256]{1,0:T(8,128)(2,1)} %omega_ref.1), channel_id=1, source_target_pairs={{0,8},{8,16},{16,24},{24,0},{1,9},{9,17},{17,25},{25,1},{2,10},{10... | collective-permute-start | bytes 3145736 | tf_op jit(solution)/shard_map/ppermute | solution.py:390
  21.8 1.9 copy-start
  23.8 70.4 %all-to-all-start = ((bf16[8,2064,128]{2,1,0:T(8,128)(2,1)}), bf16[8,2064,128]{2,1,0:T(8,128)(2,1)}, u32[]{:S(2)}, u32[]{:S(2)}) async-start(bf16[8,2064,128]{2,1,0:T(8,128)(2,1)} %get-tuple-element.6), calls=%async_computation | async-start | bytes 8454144 | tf_op jit(solution)/shard_map/all_to_all | solution.py:394
  94.2 55.2 %all-to-all-start.1 = ((bf16[8,2048,128]{2,1,0:T(8,128)(2,1)}), bf16[8,2048,128]{2,1,0:T(8,128)(2,1)}, u32[]{:S(2)}, u32[]{:S(2)}) async-start(bf16[8,2048,128]{2,1,0:T(8,128)(2,1)} %hold.1), calls=%async_computation.1 | async-start | bytes 8388608 | tf_op jit(solution)/shard_map/all_to_all | solution.py:394
  119.6 86.8 %collective-permute-start.4 = (bf16[2048,256]{1,0:T(8,128)(2,1)}, bf16[2048,256]{1,0:T(8,128)(2,1)}, u32[]{:S(2)}, u32[]{:S(2)}) collective-permute-start(bf16[2048,256]{1,0:T(8,128)(2,1)} %mirror.4.rest_0_), channel_id=1, source_target_pairs={{0,16},{8,24},{16,0},{24,8},{1,17},{9,25},{17,1},{25,9},{2,18},{10... | collective-permute-start | bytes 3145736 | tf_op jit(solution)/shard_map/ppermute | solution.py:410
  119.6 29.8 %copy-start.2 = (bf16[2048,256]{1,0:T(8,128)(2,1)S(1)}, bf16[2048,256]{1,0:T(8,128)(2,1)}, u32[]{:S(2)}) copy-start(bf16[2048,256]{1,0:T(8,128)(2,1)} %omega_ref.1) | copy-start | bytes 3145732
  128.8 77.7 %collective-permute-start.5 = (bf16[2048,256]{1,0:T(8,128)(2,1)}, bf16[2048,256]{1,0:T(8,128)(2,1)}, u32[]{:S(2)}, u32[]{:S(2)}) collective-permute-start(bf16[2048,256]{1,0:T(8,128)(2,1)} %mirror.5.rest_6_), channel_id=1, source_target_pairs={{0,8},{8,16},{16,24},{24,0},{1,9},{9,17},{17,25},{25,1},{2,10},{10... | collective-permute-start | bytes 3145736 | tf_op jit(solution)/shard_map/ppermute | solution.py:410
  157.5 12.5 %collective-permute-start.3 = (f32[3,2048,256]{2,1,0:T(8,128)}, f32[3,2048,256]{2,1,0:T(8,128)}, u32[]{:S(2)}, u32[]{:S(2)}) collective-permute-start(f32[3,2048,256]{2,1,0:T(8,128)} %far.4.rest_0_), channel_id=1, source_target_pairs={{0,1},{1,0},{2,3},{3,2},{4,5},{5,4},{6,7},{7,6},{8,9},{9,8},{10,11... | collective-permute-start | bytes 18874376 | tf_op jit(solution)/shard_map/ppermute | solution.py:432
  166.7 46.9 %collective-permute-start.6 = (bf16[2048,256]{1,0:T(8,128)(2,1)}, bf16[2048,256]{1,0:T(8,128)(2,1)}, u32[]{:S(2)}, u32[]{:S(2)}) collective-permute-start(bf16[2048,256]{1,0:T(8,128)(2,1)} %mirror.6.rest_7_), channel_id=1, source_target_pairs={{0,24},{8,0},{16,8},{24,16},{1,25},{9,1},{17,9},{25,17},{2,26},{10... | collective-permute-start | bytes 3145736 | tf_op jit(solution)/shard_map/ppermute | solution.py:410
  179.2 53.0 %all-to-all-start.2 = ((bf16[4,2048,256]{2,1,0:T(8,128)(2,1)}), bf16[4,2048,256]{2,1,0:T(8,128)(2,1)}, u32[]{:S(2)}, u32[]{:S(2)}) async-start(bf16[4,2048,256]{2,1,0:T(8,128)(2,1)} %far.5.rest_6_), calls=%async_computation.2 | async-start | bytes 8388608 | tf_op jit(solution)/shard_map/all_to_all | solution.py:438
  189.2 11.4 %collective-permute-start.7 = (f32[1,2048,256]{2,1,0:T(8,128)}, f32[1,2048,256]{2,1,0:T(8,128)}, u32[]{:S(2)}, u32[]{:S(2)}) collective-permute-start(f32[1,2048,256]{2,1,0:T(8,128)} %far.6.rest_0_), channel_id=1, source_target_pairs={{0,1},{1,0},{2,3},{3,2},{4,5},{5,4},{6,7},{7,6},{8,9},{9,8},{10,11... | collective-permute-start | bytes 6291464 | tf_op jit(solution)/shard_map/ppermute | solution.py:432
  189.4 1.6 copy-start.3
  199.3 1.3 copy-start.5
  200.6 31.6 %copy-start.4 = (bf16[16,128,128]{2,1,0:T(8,128)(2,1)S(1)}, bf16[16,128,128]{2,1,0:T(8,128)(2,1)}, u32[]{:S(2)}) copy-start(bf16[16,128,128]{2,1,0:T(8,128)(2,1)} %diag_ref.1) | copy-start | bytes 1572868
  272.5 1.6 copy-start.1
Sparse Core Ops, SparseCore 0:
  13.5 96.8 all-gather.2

commit v4 on v3

--- a/solution.py
+++ b/solution.py
@@ -101,50 +101,104 @@
     )(x, *after)
 
 
-def mirror_kernel(begin, most, row_ref, col_ref, block_ref, omega_ref, *rest):
-    out_ref, total = rest[-2:]
-    source = pl.program_id(0)
+def join_kernel(*refs):
+    count = (len(refs) - 2) // 2
+    in_refs, out_ref, held, sems = refs[:count], refs[count], refs[count + 1], refs[count + 2 :]
+    begin, moves = 0, []
+    for in_ref, sem in zip(in_refs, sems, strict=True):
+        rows = pl.ds(begin, in_ref.shape[0])
+        moves.append((rows, pltpu.make_async_copy(in_ref, held.at[rows, :], sem), sem))
+        moves[-1][1].start()
+        begin += in_ref.shape[0]
+    out = []
+    for rows, move, sem in moves:
+        move.wait()
+        out.append(pltpu.make_async_copy(held.at[rows, :], out_ref.at[rows, :], sem))
+        out[-1].start()
+    for move in out:
+        move.wait()
+
+
+def join(arrays):
+    shape = (sum(array.shape[0] for array in arrays), arrays[0].shape[1])
+    anywhere = pl.BlockSpec(memory_space=pl.ANY)
+    return pl.pallas_call(
+        join_kernel,
+        out_shape=jax.ShapeDtypeStruct(shape, arrays[0].dtype),
+        in_specs=[anywhere] * len(arrays),
+        out_specs=anywhere,
+        scratch_shapes=[pltpu.VMEM(shape, arrays[0].dtype)] + [pltpu.SemaphoreType.DMA] * len(arrays),
+        compiler_params=params(),
+        cost_estimate=COST,
+        name="join",
+    )(*arrays)
+
+
+def plane_kernel(begin, most, counts, mirrored, source_ref, row_ref, col_ref, block_ref, *rest):
+    omega_refs, (out_ref, total) = rest[: len(counts)], rest[-2:]
+    step = pl.program_id(0)
+    source = source_ref[step]
     edge = block_ref.shape[2]
     spare = total.shape[0] - 1
 
-    @pl.when(source == 0)
+    @pl.when(step == 0)
     def _():
         total[...] = jnp.zeros_like(total)
 
-    for m in range(most):
-        row = jnp.minimum(row_ref[source, begin + m], spare - 1)
-        col = col_ref[source, begin + m]
-        block = block_ref[0, m * edge : (m + 1) * edge, :]
-        omega = omega_ref[0, pl.ds(pl.multiple_of(row * edge, edge), edge), :]
-        product = dot(block, omega, ((0,), (0,))).astype(jnp.bfloat16)
-        total[col] += product.astype(jnp.float32)
-
-    @pl.when(source == pl.num_programs(0) - 1)
+    first = 0
+    for omega_ref, count in zip(omega_refs, counts, strict=True):
+
+        @pl.when((step >= first) & (step < first + count))
+        def _(omega_ref=omega_ref):
+            for m in range(most):
+                row = row_ref[source, begin + m]
+                col = col_ref[source, begin + m]
+                here, there = (row, col) if mirrored else (col, row)
+                here = pl.multiple_of(jnp.minimum(here, spare - 1) * edge, edge)
+                block = block_ref[0, m * edge : (m + 1) * edge, :]
+                omega = omega_ref[0, pl.ds(here, edge), :]
+                if mirrored:
+                    product = dot(block, omega, TN).astype(jnp.bfloat16).astype(jnp.float32)
+                else:
+                    product = dot(block, omega)
+                total[there] += product
+
+        first += count
+
+    @pl.when(step == pl.num_programs(0) - 1)
     def _():
         out_ref[...] = total[:spare].reshape(out_ref.shape).astype(out_ref.dtype)
 
 
-def mirror_sum(blocks, omegas, rows, cols, inside, begin, most, block_rows, dtype, after=()):
+def plane_sum(
+    blocks, omegas, sources, rows, cols, inside, begin, most, block_rows, dtype, mirrored, after=()
+):
     planes, _, edge = blocks.shape
-    _, height, columns = omegas.shape
-    return pl.pallas_call(
-        functools.partial(mirror_kernel, begin, most),
+    _, height, columns = omegas[0].shape
+    counts = [omega.shape[0] for omega in omegas]
+
+    def held(index):
+        first, last = sum(counts[:index]), counts[index] - 1
+        return lambda step, *_: (jnp.clip(step - first, 0, last), 0, 0)
+
+    return pl.pallas_call(
+        functools.partial(plane_kernel, begin, most, counts, mirrored),
         out_shape=jax.ShapeDtypeStruct((height, columns), dtype),
         grid_spec=pltpu.PrefetchScalarGridSpec(
-            num_scalar_prefetch=2,
+            num_scalar_prefetch=3,
             grid=(planes,),
             in_specs=[
-                pl.BlockSpec((1, most * edge, edge), lambda p, *_: (p, inside, 0)),
-                pl.BlockSpec((1, height, columns), lambda p, *_: (p, 0, 0)),
+                pl.BlockSpec((1, most * edge, edge), lambda p, source, *_: (source[p], inside, 0))
             ]
+            + [pl.BlockSpec((1, height, columns), held(index)) for index in range(len(counts))]
             + [pl.BlockSpec(memory_space=pl.ANY)] * len(after),
             out_specs=pl.BlockSpec((height, columns), lambda p, *_: (0, 0)),
             scratch_shapes=[pltpu.VMEM((block_rows + 1, edge, columns), jnp.float32)],
         ),
         compiler_params=params(),
         cost_estimate=COST,
-        name="mirror",
-    )(rows, cols, blocks, omegas, *after)
+        name="mirror" if mirrored else "home",
+    )(sources, rows, cols, blocks, *omegas, *after)
 
 
 def far_kernel(most, parts, lines, added, source_ref, place_ref, row_ref, col_ref, *rest):
@@ -158,13 +212,17 @@
         total[:spare] = rest[parts + lines][0].reshape(spare, edge, -1)
     else:
         total[...] = jnp.zeros_like(total)
-    each = len(omega_refs) // parts
-    for index, omega_ref in enumerate(omega_refs):
+    places = [
+        (part_ref, inside)
+        for part_ref in part_refs
+        for inside in range(part_ref.shape[1] // (most * edge))
+    ]
+    for index, (omega_ref, (part_ref, inside)) in enumerate(zip(omega_refs, places, strict=True)):
         for m in range(most):
             row = row_ref[source, index * most + m]
             col = jnp.minimum(col_ref[source, index * most + m], spare - 1)
-            slot = index % each * most + m
-            block = part_refs[index // each][0, slot * edge : (slot + 1) * edge, :]
+            slot = inside * most + m
+            block = part_ref[0, slot * edge : (slot + 1) * edge, :]
             omega = omega_ref[pl.ds(pl.multiple_of(col * edge, edge), edge), :]
             total[row] += dot(block, omega)
     out_ref[0] = total[:spare].reshape(out_ref.shape[1:]).astype(out_ref.dtype)
@@ -200,14 +258,40 @@
     )(sources, places, rows, cols, *parts, *omegas, *more, *after)
 
 
-def image_kernel(scale, chip_ref, diag_ref, omega_ref, far_ref, *rest):
-    *piece_refs, image_ref, gram_ref, cross = rest
-    step = pl.program_id(0)
+def base_kernel(diag_ref, omega_ref, *rest):
+    *piece_refs, out_ref = rest
     edge = diag_ref.shape[1]
     near = [
         dot(diag_ref[b], omega_ref[b * edge : (b + 1) * edge, :]) for b in range(diag_ref.shape[0])
     ]
-    image = jnp.concatenate(near, axis=0)
+    total = jnp.concatenate(near, axis=0)
+    for piece_ref in piece_refs:
+        total += piece_ref[...].astype(jnp.float32)
+    out_ref[...] = total
+
+
+def base_sum(diag, sketch, pieces):
+    block_rows, edge, _ = diag.shape
+    height, columns = sketch.shape
+    together = math.gcd(block_rows, 2)
+    rows = pl.BlockSpec((together * edge, columns), lambda b: (b, 0))
+    return pl.pallas_call(
+        base_kernel,
+        out_shape=jax.ShapeDtypeStruct((height, columns), jnp.float32),
+        grid=(block_rows // together,),
+        in_specs=[pl.BlockSpec((together, edge, edge), lambda b: (b, 0, 0)), rows]
+        + [rows] * len(pieces),
+        out_specs=rows,
+        compiler_params=params(),
+        cost_estimate=COST,
+        name="base",
+    )(diag, sketch, *pieces)
+
+
+def image_kernel(scale, chip_ref, base_ref, far_ref, *rest):
+    *piece_refs, image_ref, gram_ref, cross = rest
+    step = pl.program_id(0)
+    image = base_ref[...]
     for piece_ref in piece_refs:
         image += piece_ref[...].astype(jnp.float32)
     for chip in range(far_ref.shape[0]):
@@ -229,11 +313,10 @@
         gram_ref[...] = (gram_ref[...] + (cross[...] + cross[...].T)) * scale
 
 
-def image_and_gram(diag, sketch, chip, far, pieces, total_rows):
-    block_rows, edge, _ = diag.shape
-    height, columns = sketch.shape
-    together = math.gcd(block_rows, 2)
-    rows = pl.BlockSpec((together * edge, columns), lambda b, _: (b, 0))
+def image_and_gram(base, chip, far, pieces, total_rows):
+    height, columns = base.shape
+    tile = math.gcd(height, 256)
+    rows = pl.BlockSpec((tile, columns), lambda b, _: (b, 0))
     return pl.pallas_call(
         functools.partial(image_kernel, 1.0 / total_rows),
         out_shape=(
@@ -242,12 +325,8 @@
         ),
         grid_spec=pltpu.PrefetchScalarGridSpec(
             num_scalar_prefetch=1,
-            grid=(block_rows // together,),
-            in_specs=[
-                pl.BlockSpec((together, edge, edge), lambda b, _: (b, 0, 0)),
-                rows,
-                pl.BlockSpec((far.shape[0], together * edge, columns), lambda b, _: (0, b, 0)),
-            ]
+            grid=(height // tile,),
+            in_specs=[rows, pl.BlockSpec((far.shape[0], tile, columns), lambda b, _: (0, b, 0))]
             + [rows] * len(pieces),
             out_specs=(rows, pl.BlockSpec((columns, columns), lambda b, _: (0, 0))),
             scratch_shapes=[pltpu.VMEM((columns, columns), jnp.float32)],
@@ -255,7 +334,7 @@
         compiler_params=params(),
         cost_estimate=COST,
         name="image",
-    )(chip.reshape(1), diag, sketch, far, *pieces)
+    )(chip.reshape(1), base, far, *pieces)
 
 
 def factor_kernel(rounds, gram_ref, image_ref, basis_ref, factor_ref, inverse, work):
@@ -346,8 +425,8 @@
     slots = layers * most
     layer = lax.axis_index(LINE)
     shifts = sorted(range(layers), key=lambda shift: -min(shift, layers - shift))
-    halves = math.gcd(layers, 2)
-
+    cut = layers // 2
+    groups = [group for group in (shifts[:cut], shifts[cut:-1], shifts[-1:]) if group]
     flat = col_blocks.reshape(requests)
     owners = flat // block_rows
     order = jnp.arange(requests)
@@ -367,7 +446,10 @@
     )
     labels = jnp.stack([row_label.reshape(planes, slots), col_label.reshape(planes, slots)], axis=1)
     labels = jnp.pad(labels, ((0, 0), (0, TAIL - 2), (0, edge - slots))).astype(jnp.bfloat16)
-    in_part = to_slot // (slots // halves)
+    sizes = [len(group) * most for group in groups]
+    ends = [sum(sizes[: index + 1]) for index in range(len(sizes))]
+    in_part = sum((to_slot >= end).astype(jnp.int32) for end in ends)
+    begins = sum(jnp.where(in_part == index + 1, end, 0) for index, end in enumerate(ends))
     before = jnp.sum(
         (in_part[None, :] < in_part[:, None])
         | ((in_part[None, :] == in_part[:, None]) & (order[None, :] < order[:, None])),
@@ -376,50 +458,80 @@
     pick = before[None, :] == order[:, None]
     route = [
         jnp.sum(jnp.where(pick, values[None, :], 0), axis=1)
-        for values in (order, to_plane, to_slot % (slots // halves))
+        for values in (order, to_plane, to_slot - begins)
     ]
-    counts = jnp.sum(in_part[None, :] < jnp.arange(halves + 1)[:, None], axis=1)
-    outgoing = pack(
-        off_blocks.reshape(requests, edge, edge), route + [counts], labels, [slots // halves] * halves
-    )
-
-    plane_omegas = lax.all_gather(sketch, PLANE)
+    counts = jnp.sum(in_part[None, :] < jnp.arange(len(sizes) + 1)[:, None], axis=1)
+    outgoing = list(
+        pack(off_blocks.reshape(requests, edge, edge), route + [counts], labels, sizes)
+    )
+
     line_omegas = []
-    for shift in shifts:
+    for shift in shifts[:-1]:
         steps = [(z, (z - shift) % layers) for z in range(layers)]
-        line_omegas.append(lax.ppermute(sketch, LINE, steps) if shift else sketch)
-    parts = []
-    for part in outgoing:
-        part = hold(part, line_omegas) if parts else part
-        parts.append(lax.all_to_all(part, PLANE, 0, 0, tiled=True))
-    lines = slots // halves * edge
+        line_omegas.append(lax.ppermute(sketch, LINE, steps))
+    chip, core = lax.axis_index(CHIPS), lax.axis_index(CORE)
+    if [lax.axis_size(axis) for axis in PLANE] == [2, 2, 2]:
+        swap = [(0, 1), (1, 0)]
+        by_x, by_y = (lax.ppermute(sketch, axis, swap) for axis in CHIPS)
+        half = sketch.shape[0] // 2
+        across = [
+            lax.ppermute(by_y[:half], CHIPS[0], swap),
+            lax.ppermute(by_x[half:], CHIPS[1], swap),
+        ]
+        outgoing[0] = hold(outgoing[0], [by_x, by_y])
+        mine = join([sketch, by_y, by_x] + across)
+        plane_omegas = [
+            array.reshape((4,) + sketch.shape) for array in (mine, lax.ppermute(mine, CORE, swap))
+        ]
+        near_chips = (chip ^ jnp.arange(4)) * 2
+        sources = jnp.concatenate([near_chips + core, near_chips + 1 - core])
+    else:
+        plane_omegas = [lax.all_gather(sketch, PLANE)]
+        sources = jnp.arange(planes)
+    outgoing[1] = hold(outgoing[1], line_omegas)
+    parts = [lax.all_to_all(part, PLANE, 0, 0, tiled=True) for part in outgoing]
+    lines = sizes[0] * edge
     rows = parts[0][:, lines, :slots].astype(jnp.int32)
     cols = parts[0][:, lines + 1, :slots].astype(jnp.int32)
 
-    pieces = []
-    latest = ()
-
     def send_mirror(index, after):
-        part, inside = divmod(index, layers // halves)
+        part = sum(index * most >= end for end in ends)
+        inside = index - (ends[part] - sizes[part]) // most
         shift = shifts[index]
         kind = jnp.bfloat16 if shift else jnp.float32
-        mirror = mirror_sum(
-            parts[part], plane_omegas, rows, cols, inside, index * most, most, block_rows, kind, after
+        mirror = plane_sum(
+            parts[part],
+            plane_omegas,
+            sources,
+            rows,
+            cols,
+            inside,
+            index * most,
+            most,
+            block_rows,
+            kind,
+            True,
+            after,
         )
         steps = [(z, (z + shift) % layers) for z in range(layers)]
-        pieces.append(lax.ppermute(mirror, LINE, steps) if shift else mirror)
-        return (mirror,)
-
-    early = layers // halves
-    for index in range(early):
-        latest = send_mirror(index, latest)
+        return lax.ppermute(mirror, LINE, steps) if shift else mirror, (mirror,)
+
+    pieces, latest = [], ()
+    for index in range(cut):
+        piece, latest = send_mirror(index, latest)
+        pieces.append(piece)
 
     cores = lax.axis_size(CORE)
     chips = planes // cores
-    chip, core = lax.axis_index(CHIPS), lax.axis_index(CORE)
     away = (chip + jnp.arange(1, chips)) % chips
     far = functools.partial(
-        far_sum, parts=parts, omegas=line_omegas, rows=rows, cols=cols, most=most, block_rows=block_rows
+        far_sum,
+        parts=parts[:-1],
+        omegas=line_omegas,
+        rows=rows,
+        cols=cols,
+        most=most,
+        block_rows=block_rows,
     )
 
     def ask(chips_asked, after):
@@ -432,20 +544,33 @@
         return lax.ppermute(other, CORE, [(0, 1), (1, 0)]), (other,)
 
     other, latest = ask(away, latest)
-    for index in range(early, layers - 1):
-        latest = send_mirror(index, latest)
+    late = []
+    for index in range(cut, layers - 1):
+        piece, latest = send_mirror(index, latest)
+        late.append(piece)
     sent = far(away * cores + core, away, chips, dtype=jnp.bfloat16, add=other, after=latest)
-    received = lax.all_to_all(sent, CHIPS, 0, 0, tiled=True)
+    received = lax.all_to_all(hold(sent, parts[-1:]), CHIPS, 0, 0, tiled=True)
     other, latest = ask(chip.reshape(1), (sent,))
-    latest = send_mirror(layers - 1, latest)
+    mirror, latest = send_mirror(layers - 1, latest)
+    home = plane_sum(
+        outgoing[-1],
+        plane_omegas,
+        sources,
+        row_label.reshape(planes, slots),
+        col_label.reshape(planes, slots),
+        0,
+        slots - most,
+        most,
+        block_rows,
+        jnp.float32,
+        False,
+        latest,
+    )
     own = far(
-        chip.reshape(1) * cores + core, jnp.arange(1), 1, dtype=jnp.float32, add=other, after=latest
-    )
-    pieces.append(own.reshape(sketch.shape))
-
-    image, part = image_and_gram(
-        diag_blocks, sketch, chip, received, pieces, block_rows * edge * peers
-    )
+        chip.reshape(1) * cores + core, jnp.arange(1), 1, dtype=jnp.float32, add=other, after=(home,)
+    )
+    base = base_sum(diag_blocks, sketch, [home, mirror, own.reshape(sketch.shape)] + pieces)
+    image, part = image_and_gram(base, chip, received, late, block_rows * edge * peers)
     gram = sum_over_devices(part, peers)
     return factor_and_basis(gram, image)
 

time: 471 us -> 444 us (0.943)
  waiting for transfers between devices: 119 us -> 71.1 us
  starting transfers between devices: 27.7 us -> 45 us
  between operations: 14.2 us -> 0.92 us
  Pallas kernels: 269 us -> 281 us
  local copies, waits for them, and re-layouts: 7.47 us -> 15.4 us
    all_to_all x3 -> x4, waiting for transfers between devices: 48.6 us -> 24.3 us  [the longest x3 13.8 us: on_device(): parts = [lax.all_to_all(part, PLANE, 0, 0, tiled=True) for part in outgoing]]
    pallas_call x4 -> x7, Pallas kernels: 35.8 us -> 54.2 us  [the longest x5 44.6 us: plane_sum(): pl.pallas_call(functools.partial(plane_kernel, begin, most, counts, mirro...]
    ppermute x6 -> x11, starting transfers between devices: 13.4 us -> 26.3 us  [the longest x3 13.9 us: send_mirror(): return (lax.ppermute(mirror, LINE, steps) if shift else mirror, (mirror,))]
    ppermute x6 -> x11, waiting for transfers between devices: 59.7 us -> 46.8 us  [the longest x3 21.4 us: on_device(): line_omegas.append(lax.ppermute(sketch, LINE, steps))]
    all_gather x1 -> x0, waiting for transfers between devices: 10.8 us -> none  [on_device(): plane_omegas = lax.all_gather(sketch, PLANE)]
    all_to_all x3 -> x4, starting transfers between devices: 14.1 us -> 18.3 us  [the longest x3 13.4 us: on_device(): parts = [lax.all_to_all(part, PLANE, 0, 0, tiled=True) for part in outgoing]]
    unnamed x13 -> x25, local copies, waits for them, and re-layouts: 7.2 us -> 11.2 us
  transfers between devices with their start and end apart: 12 -> 17, of which waited for: 7 -> 7; matrix products, arithmetic and copies ran while one was open for 1% -> 2% of each run, Pallas kernels for 15% -> 19%
where the time goes in v4:
time: 444 us; the launch traced here: 443 us
  Pallas kernels  281 us (63%)
  waiting for transfers between devices  71.1 us (16%)
  starting transfers between devices  45 us (10%)
  blocking collectives  26.6 us (6%)
  local copies, waits for them, and re-layouts  15.4 us (3%)
    pallas_call x1, Pallas kernels, factor_and_basis(): pl.pallas_call(functools.partial(factor_kernel, rounds), out_shape=(jax.S...  189 us
    pallas_call x5, Pallas kernels, plane_sum(): pl.pallas_call(functools.partial(plane_kernel, begin, most, counts, mirro...  44.6 us
    pallas_call x4, Pallas kernels, far_sum(): pl.pallas_call(functools.partial(far_kernel, most, len(parts), len(omegas...  25.4 us
    ppermute x3, waiting for transfers between devices, on_device(): line_omegas.append(lax.ppermute(sketch, LINE, steps))  21.4 us
    ppermute x3, starting transfers between devices, send_mirror(): return (lax.ppermute(mirror, LINE, steps) if shift else mirror, (mirror,))  13.9 us
    all_to_all x3, waiting for transfers between devices, on_device(): parts = [lax.all_to_all(part, PLANE, 0, 0, tiled=True) for part in outgoing]  13.8 us
    all_to_all x1, blocking collectives, sum_over_devices(): lax.all_to_all(part.reshape(peers, rows // peers, columns), ALL, 0, 0, ti...  13.8 us
    all_to_all x3, starting transfers between devices, on_device(): parts = [lax.all_to_all(part, PLANE, 0, 0, tiled=True) for part in outgoing]  13.4 us
  transfers between devices with their start and end apart: 17, of which 7 were waited for; matrix products, arithmetic and copies ran while one was open for 2% of the time, Pallas kernels for 19%

profile of v4, /device:TPU:0, one launch (start us, length us, event | category | flops | bytes accessed | tf_op | source)
XLA Modules:
  0.0 442.7 jit_solution(4295865581549412382)
XLA Ops:
  12.3 6.1 %pack.1 = (bf16[8,2064,128]{2,1,0:T(8,128)(2,1)}, bf16[8,1024,128]{2,1,0:T(8,128)(2,1)S(1)}, bf16[8,1024,128]{2,1,0:T(8,128)(2,1)}) custom-call(s32[128]{0:T(128)S(1)} %get-tuple-element.14.entry_ref, s32[128]{0:T(128)S(1)} %get-tuple-element.13.plane_ref, s32[128]{0:T(128)S(1)} %get-tuple-element.12.slot_ref, s32[4]{0:T(128)S(1)} %convert_reduce_fusion.2.count_ref, ...), custom_call_target="tpu_custom_call" | custom-call | flops 999999995904 | bytes 99999997952 | tf_op jit(solution)/shard_map/pack/pallas_call | solution.py:71
  20.0 7.2 %collective-permute-done.refs_1_.rest_1_ = bf16[2048,256]{1,0:T(8,128)(2,1)} collective-permute-done((bf16[2048,256]{1,0:T(8,128)(2,1)}, bf16[2048,256]{1,0:T(8,128)(2,1)}, u32[]{:S(2)}, u32[]{:S(2)}) %collective-permute-start) | collective-permute-done | bytes 1048608 | tf_op jit(solution)/shard_map/ppermute | solution.py:475
  34.1 4.7 %all-to-all-start = ((bf16[8,2064,128]{2,1,0:T(8,128)(2,1)}), bf16[8,2064,128]{2,1,0:T(8,128)(2,1)}, u32[]{:S(2)}, u32[]{:S(2)}) async-start(bf16[8,2064,128]{2,1,0:T(8,128)(2,1)} %hold.3), calls=%async_computation | async-start | bytes 8454144 | tf_op jit(solution)/shard_map/all_to_all | solution.py:492
  42.7 9.3 %collective-permute-done.3.refs_4_ = bf16[1024,256]{1,0:T(8,128)(2,1)} collective-permute-done((bf16[1024,256]{1,0:T(8,128)(2,1)}, bf16[1024,256]{1,0:T(8,128)(2,1)}, u32[]{:S(2)}, u32[]{:S(2)}) %collective-permute-start.3) | collective-permute-done | bytes 524320 | tf_op jit(solution)/shard_map/ppermute | solution.py:479
  55.5 21.4 %collective-permute-done.5.rest_0_.rest_2_ = bf16[2048,256]{1,0:T(8,128)(2,1)} collective-permute-done((bf16[2048,256]{1,0:T(8,128)(2,1)}, bf16[2048,256]{1,0:T(8,128)(2,1)}, u32[]{:S(2)}, u32[]{:S(2)}) %collective-permute-start.5) | collective-permute-done | bytes 1048608 | tf_op jit(solution)/shard_map/ppermute | solution.py:471
  76.9 13.8 %all-to-all-done.block_ref.rest_0_ = bf16[8,2064,128]{2,1,0:T(8,128)(2,1)} async-done(((bf16[8,2064,128]{2,1,0:T(8,128)(2,1)}), bf16[8,2064,128]{2,1,0:T(8,128)(2,1)}, u32[]{:S(2)}, u32[]{:S(2)}) %all-to-all-start) | async-done | bytes 4227104 | tf_op jit(solution)/shard_map/all_to_all | solution.py:492
  98.1 8.7 %mirror.4.rest_2_ = bf16[2048,256]{1,0:T(8,128)(2,1)} custom-call(s32[8]{0:T(128)S(1)} %pad_add_fusion.source_ref, s32[8,32]{1,0:T(8,128)S(1)} %bitcast.20, s32[8,32]{1,0:T(8,128)S(1)} %bitcast.12, bf16[8,2064,128]{2,1,0:T(8,128)(2,1)} %all-to-all-done.block_ref.rest_0_, bf16[4,2048,256]{2,1,0:T(8,128)(2,1)S(1)} %bitcast.32, ...), custom_call_target="tpu_custom_call" | custom-call | flops 999999995904 | bytes 99999997952 | tf_op jit(solution)/shard_map/mirror/pallas_call | solution.py:184
  106.8 10.0 %collective-permute-start.10 = (bf16[2048,256]{1,0:T(8,128)(2,1)}, bf16[2048,256]{1,0:T(8,128)(2,1)}, u32[]{:S(2)}, u32[]{:S(2)}) collective-permute-start(bf16[2048,256]{1,0:T(8,128)(2,1)} %mirror.4.rest_2_), channel_id=1, source_target_pairs={{0,16},{8,24},{16,0},{24,8},{1,17},{9,25},{17,1},{25,9},{2,18},{10... | collective-permute-start | bytes 3145736 | tf_op jit(solution)/shard_map/ppermute | solution.py:517
  116.9 9.5 %mirror.5.rest_5_ = bf16[2048,256]{1,0:T(8,128)(2,1)} custom-call(s32[8]{0:T(128)S(1)} %pad_add_fusion.source_ref, s32[8,32]{1,0:T(8,128)S(1)} %bitcast.21, s32[8,32]{1,0:T(8,128)S(1)} %bitcast.13, bf16[8,2064,128]{2,1,0:T(8,128)(2,1)} %all-to-all-done.block_ref.rest_0_, bf16[4,2048,256]{2,1,0:T(8,128)(2,1)} %bitcast.28, ...), custom_call_target="tpu_custom_call" | custom-call | flops 999999995904 | bytes 99999997952 | tf_op jit(solution)/shard_map/mirror/pallas_call | solution.py:184
  126.4 4.4 all-to-all-start.1
  130.7 7.5 %far.4.rest_2_ = f32[3,2048,256]{2,1,0:T(8,128)} custom-call(s32[3]{0:T(128)S(1)} %add_subtract_fusion.source_ref, s32[3]{0:T(128)S(1)} %iota.31.place_ref, s32[8,32]{1,0:T(8,128)S(1)} %bitcast.22, s32[8,32]{1,0:T(8,128)S(1)} %bitcast.14, bf16[8,2064,128]{2,1,0:T(8,128)(2,1)} %all-to-all-done.block_ref.rest_0_, ...), custom_call_target="tpu_custom_call" | custom-call | flops 999999995904 | bytes 99999997952 | tf_op jit(solution)/shard_map/far/pallas_call | solution.py:237
  138.6 9.5 %mirror.6.rest_6_ = bf16[2048,256]{1,0:T(8,128)(2,1)} custom-call(s32[8]{0:T(128)S(1)} %pad_add_fusion.source_ref, s32[8,32]{1,0:T(8,128)S(1)} %bitcast.23, s32[8,32]{1,0:T(8,128)S(1)} %bitcast.15, bf16[8,1024,128]{2,1,0:T(8,128)(2,1)} %all-to-all-done.2.rest_1_.block_ref, bf16[4,2048,256]{2,1,0:T(8,128)(2,1)} %bitcast.29, ...), custom_call_target="tpu_custom_call" | custom-call | flops 999999995904 | bytes 99999997952 | tf_op jit(solution)/shard_map/mirror/pallas_call | solution.py:184
  151.9 8.7 %far.5.rest_5_.x_ref = bf16[4,2048,256]{2,1,0:T(8,128)(2,1)} custom-call(s32[3]{0:T(128)S(1)} %get-tuple-element.31.source_ref, s32[3]{0:T(128)S(1)} %get-tuple-element.30.place_ref, s32[8,32]{1,0:T(8,128)S(1)} %bitcast.24, s32[8,32]{1,0:T(8,128)S(1)} %bitcast.16, bf16[8,2064,128]{2,1,0:T(8,128)(2,1)} %all-to-all-done.block_ref.rest_0_, ...), custom_call_target="tpu_custom_call" | custom-call | flops 999999995904 | bytes 99999997952 | tf_op jit(solution)/shard_map/far/pallas_call | solution.py:237
  160.6 4.9 %far.6.rest_2_ = f32[1,2048,256]{2,1,0:T(8,128)} custom-call(s32[1]{0:T(128)S(6)} %sub.71.source_ref, s32[1]{0:T(128)} %constant.121.clone.1.place_ref, s32[8,32]{1,0:T(8,128)S(1)} %bitcast.25, s32[8,32]{1,0:T(8,128)S(1)} %bitcast.17, bf16[8,2064,128]{2,1,0:T(8,128)(2,1)} %all-to-all-done.block_ref.rest_0_, ...), custom_call_target="tpu_custom_call" | custom-call | flops 999999995904 | bytes 99999997952 | tf_op jit(solution)/shard_map/far/pallas_call | solution.py:237
  165.5 4.9 %all-to-all-start.3 = ((bf16[4,2048,256]{2,1,0:T(8,128)(2,1)}), bf16[4,2048,256]{2,1,0:T(8,128)(2,1)}, u32[]{:S(2)}, u32[]{:S(2)}) async-start(bf16[4,2048,256]{2,1,0:T(8,128)(2,1)} %hold.5), calls=%async_computation.3 | async-start | bytes 8388608 | tf_op jit(solution)/shard_map/all_to_all | solution.py:552
  170.4 8.6 %mirror.7.rest_2_.rest_1_ = f32[2048,256]{1,0:T(8,128)S(1)} custom-call(s32[8]{0:T(128)S(1)} %pad_add_fusion.source_ref, s32[8,32]{1,0:T(8,128)S(1)} %bitcast.26, s32[8,32]{1,0:T(8,128)S(1)} %bitcast.18, bf16[8,1024,128]{2,1,0:T(8,128)(2,1)} %all-to-all-done.1.block_ref.rest_0_, bf16[4,2048,256]{2,1,0:T(8,128)(2,1)} %bitcast.30, ...), custom_call_target="tpu_custom_call" | custom-call | flops 999999995904 | bytes 99999997952 | tf_op jit(solution)/shard_map/mirror/pallas_call | solution.py:184
  180.3 8.4 %home.1.rest_6_.rest_0_ = f32[2048,256]{1,0:T(8,128)S(1)} custom-call(s32[8]{0:T(128)S(1)} %pad_add_fusion.source_ref, s32[8,32]{1,0:T(8,128)S(1)} %add.284.row_ref, s32[8,32]{1,0:T(8,128)S(1)} %add.287.col_ref, bf16[8,1024,128]{2,1,0:T(8,128)(2,1)} %get-tuple-element.7.block_ref, bf16[4,2048,256]{2,1,0:T(8,128)(2,1)} %bitcast.31, ...), custom_call_target="tpu_custom_call" | custom-call | flops 999999995904 | bytes 99999997952 | tf_op jit(solution)/shard_map/home/pallas_call | solution.py:184
  195.7 6.2 %base.1.base_ref = f32[2048,256]{1,0:T(8,128)S(1)} custom-call(bf16[16,128,128]{2,1,0:T(8,128)(2,1)S(1)} %copy-done.4, bf16[2048,256]{1,0:T(8,128)(2,1)S(1)} %copy-done.3, f32[2048,256]{1,0:T(8,128)} %copy-done.6, f32[2048,256]{1,0:T(8,128)} %copy-done.7, f32[2048,256]{1,0:T(8,128)} %bitcast.33, bf16[2048,256]{1,0:T(8,128)(2,1)} %collective-permute-done.10.rest_3_, ...), custom_call_target="tpu_custom_call" | custom-call | flops 999999995904 | bytes 99999997952 | tf_op jit(solution)/shard_map/base/pallas_call | solution.py:278
  203.2 5.1 %collective-permute-done.12.rest_0_ = bf16[2048,256]{1,0:T(8,128)(2,1)} collective-permute-done((bf16[2048,256]{1,0:T(8,128)(2,1)}, bf16[2048,256]{1,0:T(8,128)(2,1)}, u32[]{:S(2)}, u32[]{:S(2)}) %collective-permute-start.12) | collective-permute-done | bytes 1048608 | tf_op jit(solution)/shard_map/ppermute | solution.py:517
  208.3 10.5 %all-to-all-done.3.far_ref = bf16[4,2048,256]{2,1,0:T(8,128)(2,1)} async-done(((bf16[4,2048,256]{2,1,0:T(8,128)(2,1)}), bf16[4,2048,256]{2,1,0:T(8,128)(2,1)}, u32[]{:S(2)}, u32[]{:S(2)}) %all-to-all-start.3) | async-done | bytes 4194336 | tf_op jit(solution)/shard_map/all_to_all | solution.py:552
  220.3 6.5 %image.1 = (f32[2048,256]{1,0:T(8,128)S(1)}, f32[256,256]{1,0:T(8,128)S(1)}) custom-call(s32[1]{0:T(128)} %bitcast.chip_ref, f32[2048,256]{1,0:T(8,128)S(1)} %copy-done.9, bf16[4,2048,256]{2,1,0:T(8,128)(2,1)} %all-to-all-done.3.far_ref, bf16[2048,256]{1,0:T(8,128)(2,1)} %collective-permute-done.12.rest_0_), custom_call_target="tpu_custom_call" | custom-call | flops 999999995904 | bytes 99999997952 | tf_op jit(solution)/shard_map/image/pallas_call | solution.py:320
  226.8 13.8 %all_to_all.30 = f32[32,8,256]{2,1,0:T(8,128)S(1)} all-to-all(f32[32,8,256]{2,1,0:T(8,128)S(1)} %bitcast.11), channel_id=1, replica_groups=mesh['z'=4,'x'=2,'y'=2,'c'=2] {'z','x','y','c'}, dimensions={0} | all-to-all | bytes 524288 | tf_op jit(solution)/shard_map/all_to_all | solution.py:412
  240.7 12.8 %all_to_all.31 = f32[32,8,256]{2,1,0:T(8,128)S(1)} all-to-all(f32[32,8,256]{2,1,0:T(8,128)S(1)} %broadcast_in_dim.86), channel_id=1, replica_groups=mesh['z'=4,'x'=2,'y'=2,'c'=2] {'z','x','y','c'}, dimensions={0} | all-to-all | bytes 524288 | tf_op jit(solution)/shard_map/all_to_all | solution.py:414
  253.5 189.1 %factor.1 = (f32[2048,256]{1,0:T(8,128)}, f32[256,256]{1,0:T(8,128)}) custom-call(f32[256,256]{1,0:T(8,128)S(1)} %bitcast.10, f32[2048,256]{1,0:T(8,128)S(1)} %get-tuple-element.11.image_ref), custom_call_target="tpu_custom_call" | custom-call | tf_op jit(solution)/shard_map/factor/pallas_call | solution.py:398
  (80 shorter events, 50.3 us)
Async XLA Ops:
  0.6 26.5 %collective-permute-start = (bf16[2048,256]{1,0:T(8,128)(2,1)}, bf16[2048,256]{1,0:T(8,128)(2,1)}, u32[]{:S(2)}, u32[]{:S(2)}) collective-permute-start(bf16[2048,256]{1,0:T(8,128)(2,1)} %omega_ref.1), channel_id=1, source_target_pairs={{0,2},{2,0},{1,3},{3,1},{4,6},{6,4},{5,7},{7,5},{8,10},{10,8},{9,1... | collective-permute-start | bytes 3145736 | tf_op jit(solution)/shard_map/ppermute | solution.py:475
  3.7 27.1 %collective-permute-start.1 = (bf16[2048,256]{1,0:T(8,128)(2,1)}, bf16[2048,256]{1,0:T(8,128)(2,1)}, u32[]{:S(2)}, u32[]{:S(2)}) collective-permute-start(bf16[2048,256]{1,0:T(8,128)(2,1)} %omega_ref.1), channel_id=1, source_target_pairs={{0,4},{4,0},{1,5},{5,1},{2,6},{6,2},{3,7},{7,3},{8,12},{12,8},{9,1... | collective-permute-start | bytes 3145736 | tf_op jit(solution)/shard_map/ppermute | solution.py:475
  5.2 71.7 %collective-permute-start.5 = (bf16[2048,256]{1,0:T(8,128)(2,1)}, bf16[2048,256]{1,0:T(8,128)(2,1)}, u32[]{:S(2)}, u32[]{:S(2)}) collective-permute-start(bf16[2048,256]{1,0:T(8,128)(2,1)} %omega_ref.1), channel_id=1, source_target_pairs={{0,16},{8,24},{16,0},{24,8},{1,17},{9,25},{17,1},{25,9},{2,18},{10... | collective-permute-start | bytes 3145736 | tf_op jit(solution)/shard_map/ppermute | solution.py:471
  7.7 69.1 %collective-permute-start.6 = (bf16[2048,256]{1,0:T(8,128)(2,1)}, bf16[2048,256]{1,0:T(8,128)(2,1)}, u32[]{:S(2)}, u32[]{:S(2)}) collective-permute-start(bf16[2048,256]{1,0:T(8,128)(2,1)} %omega_ref.1), channel_id=1, source_target_pairs={{0,24},{8,0},{16,8},{24,16},{1,25},{9,1},{17,9},{25,17},{2,26},{10... | collective-permute-start | bytes 3145736 | tf_op jit(solution)/shard_map/ppermute | solution.py:471
  9.1 67.8 %collective-permute-start.7 = (bf16[2048,256]{1,0:T(8,128)(2,1)}, bf16[2048,256]{1,0:T(8,128)(2,1)}, u32[]{:S(2)}, u32[]{:S(2)}) collective-permute-start(bf16[2048,256]{1,0:T(8,128)(2,1)} %omega_ref.1), channel_id=1, source_target_pairs={{0,8},{8,16},{16,24},{24,0},{1,9},{9,17},{17,25},{25,1},{2,10},{10... | collective-permute-start | bytes 3145736 | tf_op jit(solution)/shard_map/ppermute | solution.py:471
  12.2 7.5 %copy-start.11 = (s32[256]{0:T(256)S(1)}, s32[256]{0:T(256)}, u32[]{:S(2)}) copy-start(s32[256]{0:T(256)} %get-tuple-element.24) | copy-start | bytes 3076
  12.2 7.5 %copy-start.10 = (s32[256]{0:T(256)S(1)}, s32[256]{0:T(256)}, u32[]{:S(2)}) copy-start(s32[256]{0:T(256)} %get-tuple-element.34) | copy-start | bytes 3076
  29.0 13.7 %collective-permute-start.2 = (bf16[1024,256]{1,0:T(8,128)(2,1)}, bf16[1024,256]{1,0:T(8,128)(2,1)}, u32[]{:S(2)}, u32[]{:S(2)}) collective-permute-start(bf16[1024,256]{1,0:T(8,128)(2,1)} %slice.16), channel_id=1, source_target_pairs={{0,4},{4,0},{1,5},{5,1},{2,6},{6,2},{3,7},{7,3},{8,12},{12,8},{9,1... | collective-permute-start | bytes 1572872 | tf_op jit(solution)/shard_map/ppermute | solution.py:478
  32.6 19.4 %collective-permute-start.3 = (bf16[1024,256]{1,0:T(8,128)(2,1)}, bf16[1024,256]{1,0:T(8,128)(2,1)}, u32[]{:S(2)}, u32[]{:S(2)}) collective-permute-start(bf16[1024,256]{1,0:T(8,128)(2,1)} %slice.17), channel_id=1, source_target_pairs={{0,2},{2,0},{1,3},{3,1},{4,6},{6,4},{5,7},{7,5},{8,10},{10,8},{9,1... | collective-permute-start | bytes 1572872 | tf_op jit(solution)/shard_map/ppermute | solution.py:479
  34.1 17.9 %copy-start.2 = (bf16[2048,256]{1,0:T(8,128)(2,1)S(1)}, bf16[2048,256]{1,0:T(8,128)(2,1)}, u32[]{:S(2)}) copy-start(bf16[2048,256]{1,0:T(8,128)(2,1)} %omega_ref.1) | copy-start | bytes 3145732
  34.1 56.6 %all-to-all-start = ((bf16[8,2064,128]{2,1,0:T(8,128)(2,1)}), bf16[8,2064,128]{2,1,0:T(8,128)(2,1)}, u32[]{:S(2)}, u32[]{:S(2)}) async-start(bf16[8,2064,128]{2,1,0:T(8,128)(2,1)} %hold.3), calls=%async_computation | async-start | bytes 8454144 | tf_op jit(solution)/shard_map/all_to_all | solution.py:492
  55.4 40.5 %collective-permute-start.4 = (bf16[8192,256]{1,0:T(8,128)(2,1)}, bf16[8192,256]{1,0:T(8,128)(2,1)}, u32[]{:S(2)}, u32[]{:S(2)}) collective-permute-start(bf16[8192,256]{1,0:T(8,128)(2,1)} %join.1), channel_id=1, source_target_pairs={{0,1},{1,0},{2,3},{3,2},{4,5},{5,4},{6,7},{7,6},{8,9},{9,8},{10,11... | collective-permute-start | bytes 12582920 | tf_op jit(solution)/shard_map/ppermute | solution.py:484
  90.7 35.6 %all-to-all-start.2 = ((bf16[8,1024,128]{2,1,0:T(8,128)(2,1)}), bf16[8,1024,128]{2,1,0:T(8,128)(2,1)}, u32[]{:S(2)}, u32[]{:S(2)}) async-start(bf16[8,1024,128]{2,1,0:T(8,128)(2,1)} %hold.4), calls=%async_computation.2 | async-start | bytes 4194304 | tf_op jit(solution)/shard_map/all_to_all | solution.py:492
  95.9 2.2 copy-start.1
  106.8 88.9 %collective-permute-start.10 = (bf16[2048,256]{1,0:T(8,128)(2,1)}, bf16[2048,256]{1,0:T(8,128)(2,1)}, u32[]{:S(2)}, u32[]{:S(2)}) collective-permute-start(bf16[2048,256]{1,0:T(8,128)(2,1)} %mirror.4.rest_2_), channel_id=1, source_target_pairs={{0,16},{8,24},{16,0},{24,8},{1,17},{9,25},{17,1},{25,9},{2,18},{10... | collective-permute-start | bytes 3145736 | tf_op jit(solution)/shard_map/ppermute | solution.py:517
  126.4 69.3 %collective-permute-start.11 = (bf16[2048,256]{1,0:T(8,128)(2,1)}, bf16[2048,256]{1,0:T(8,128)(2,1)}, u32[]{:S(2)}, u32[]{:S(2)}) collective-permute-start(bf16[2048,256]{1,0:T(8,128)(2,1)} %mirror.5.rest_5_), channel_id=1, source_target_pairs={{0,8},{8,16},{16,24},{24,0},{1,9},{9,17},{17,25},{25,1},{2,10},{10... | collective-permute-start | bytes 3145736 | tf_op jit(solution)/shard_map/ppermute | solution.py:517
  126.4 39.1 %all-to-all-start.1 = ((bf16[8,1024,128]{2,1,0:T(8,128)(2,1)}), bf16[8,1024,128]{2,1,0:T(8,128)(2,1)}, u32[]{:S(2)}, u32[]{:S(2)}) async-start(bf16[8,1024,128]{2,1,0:T(8,128)(2,1)} %get-tuple-element.7.block_ref), calls=%async_computation.1 | async-start | bytes 4194304 | tf_op jit(solution)/shard_map/all_to_all | solution.py:492
  138.3 13.6 %collective-permute-start.8 = (f32[3,2048,256]{2,1,0:T(8,128)}, f32[3,2048,256]{2,1,0:T(8,128)}, u32[]{:S(2)}, u32[]{:S(2)}) collective-permute-start(f32[3,2048,256]{2,1,0:T(8,128)} %far.4.rest_2_), channel_id=1, source_target_pairs={{0,1},{1,0},{2,3},{3,2},{4,5},{5,4},{6,7},{7,6},{8,9},{9,8},{10,11... | collective-permute-start | bytes 18874376 | tf_op jit(solution)/shard_map/ppermute | solution.py:544
  148.1 60.2 %collective-permute-start.12 = (bf16[2048,256]{1,0:T(8,128)(2,1)}, bf16[2048,256]{1,0:T(8,128)(2,1)}, u32[]{:S(2)}, u32[]{:S(2)}) collective-permute-start(bf16[2048,256]{1,0:T(8,128)(2,1)} %mirror.6.rest_6_), channel_id=1, source_target_pairs={{0,24},{8,0},{16,8},{24,16},{1,25},{9,1},{17,9},{25,17},{2,26},{10... | collective-permute-start | bytes 3145736 | tf_op jit(solution)/shard_map/ppermute | solution.py:517
  165.5 24.5 %collective-permute-start.9 = (f32[1,2048,256]{2,1,0:T(8,128)}, f32[1,2048,256]{2,1,0:T(8,128)}, u32[]{:S(2)}, u32[]{:S(2)}) collective-permute-start(f32[1,2048,256]{2,1,0:T(8,128)} %far.6.rest_2_), channel_id=1, source_target_pairs={{0,1},{1,0},{2,3},{3,2},{4,5},{5,4},{6,7},{7,6},{8,9},{9,8},{10,11... | collective-permute-start | bytes 6291464 | tf_op jit(solution)/shard_map/ppermute | solution.py:544
  165.5 53.2 %all-to-all-start.3 = ((bf16[4,2048,256]{2,1,0:T(8,128)(2,1)}), bf16[4,2048,256]{2,1,0:T(8,128)(2,1)}, u32[]{:S(2)}, u32[]{:S(2)}) async-start(bf16[4,2048,256]{2,1,0:T(8,128)(2,1)} %hold.5), calls=%async_computation.3 | async-start | bytes 8388608 | tf_op jit(solution)/shard_map/all_to_all | solution.py:552
  190.0 5.7 %copy-start.3 = (bf16[2048,256]{1,0:T(8,128)(2,1)S(1)}, bf16[2048,256]{1,0:T(8,128)(2,1)}, u32[]{:S(2)}) copy-start(bf16[2048,256]{1,0:T(8,128)(2,1)} %omega_ref.1) | copy-start | bytes 3145732
  190.0 5.7 %copy-start.4 = (bf16[16,128,128]{2,1,0:T(8,128)(2,1)S(1)}, bf16[16,128,128]{2,1,0:T(8,128)(2,1)}, u32[]{:S(2)}) copy-start(bf16[16,128,128]{2,1,0:T(8,128)(2,1)} %diag_ref.1) | copy-start | bytes 1572868
  218.7 1.6 copy-start.9
  (5 other events, 6.7 us)

commit v5 on v4

--- a/solution.py
+++ b/solution.py
@@ -14,6 +14,7 @@
 ALL = (LINE,) + PLANE
 CHIPS, CORE = PLANE[:2], PLANE[2]
 VMEM_LIMIT = 48 * 1024 * 1024
+VMEM_ALL = 60 * 1024 * 1024
 COST = pl.CostEstimate(flops=10**12, bytes_accessed=10**11, transcendentals=0)
 TAIL = 16
 
@@ -28,8 +29,8 @@
 TN = ((0,), (0,))
 
 
-def params():
-    return pltpu.CompilerParams(vmem_limit_bytes=VMEM_LIMIT)
+def params(limit=VMEM_LIMIT):
+    return pltpu.CompilerParams(vmem_limit_bytes=limit)
 
 
 def split(a):
@@ -134,40 +135,43 @@
     )(*arrays)
 
 
-def plane_kernel(begin, most, counts, mirrored, source_ref, row_ref, col_ref, block_ref, *rest):
-    omega_refs, (out_ref, total) = rest[: len(counts)], rest[-2:]
-    step = pl.program_id(0)
-    source = source_ref[step]
-    edge = block_ref.shape[2]
+def plane_kernel(inside, begin, most, counts, mirrored, source_ref, row_ref, col_ref, *rest):
+    block_ref, *omega_refs = rest[: 1 + len(counts)]
+    out_ref, total, blocks, omegas, block_sem, omega_sem = rest[-6:]
+    edge = blocks.shape[2]
     spare = total.shape[0] - 1
-
-    @pl.when(step == 0)
-    def _():
-        total[...] = jnp.zeros_like(total)
-
-    first = 0
-    for omega_ref, count in zip(omega_refs, counts, strict=True):
-
-        @pl.when((step >= first) & (step < first + count))
-        def _(omega_ref=omega_ref):
-            for m in range(most):
-                row = row_ref[source, begin + m]
-                col = col_ref[source, begin + m]
-                here, there = (row, col) if mirrored else (col, row)
-                here = pl.multiple_of(jnp.minimum(here, spare - 1) * edge, edge)
-                block = block_ref[0, m * edge : (m + 1) * edge, :]
-                omega = omega_ref[0, pl.ds(here, edge), :]
-                if mirrored:
-                    product = dot(block, omega, TN).astype(jnp.bfloat16).astype(jnp.float32)
-                else:
-                    product = dot(block, omega)
-                total[there] += product
-
-        first += count
-
-    @pl.when(step == pl.num_programs(0) - 1)
-    def _():
-        out_ref[...] = total[:spare].reshape(out_ref.shape).astype(out_ref.dtype)
+    places = [(omega_ref, k) for omega_ref, count in zip(omega_refs, counts) for k in range(count)]
+    moves = []
+    for step, (omega_ref, k) in enumerate(places):
+        rows = pl.ds(inside * most * edge, most * edge)
+        moves.append(
+            (
+                pltpu.make_async_copy(
+                    block_ref.at[source_ref[step], rows, :], blocks.at[step], block_sem.at[step]
+                ),
+                pltpu.make_async_copy(omega_ref.at[k], omegas.at[step], omega_sem.at[step]),
+            )
+        )
+        for move in moves[-1]:
+            move.start()
+    total[...] = jnp.zeros_like(total)
+    for step in range(len(places)):
+        source = source_ref[step]
+        for move in moves[step]:
+            move.wait()
+        for m in range(most):
+            row = row_ref[source, begin + m]
+            col = col_ref[source, begin + m]
+            here, there = (row, col) if mirrored else (col, row)
+            here = pl.multiple_of(jnp.minimum(here, spare - 1) * edge, edge)
+            block = blocks[step, m * edge : (m + 1) * edge, :]
+            omega = omegas[step, pl.ds(here, edge), :]
+            if mirrored:
+                product = dot(block, omega, TN).astype(jnp.bfloat16).astype(jnp.float32)
+            else:
+                product = dot(block, omega)
+            total[there] += product
+    out_ref[...] = total[:spare].reshape(out_ref.shape).astype(out_ref.dtype)
 
 
 def plane_sum(
@@ -176,56 +180,95 @@
     planes, _, edge = blocks.shape
     _, height, columns = omegas[0].shape
     counts = [omega.shape[0] for omega in omegas]
-
-    def held(index):
-        first, last = sum(counts[:index]), counts[index] - 1
-        return lambda step, *_: (jnp.clip(step - first, 0, last), 0, 0)
-
-    return pl.pallas_call(
-        functools.partial(plane_kernel, begin, most, counts, mirrored),
+    anywhere = pl.BlockSpec(memory_space=pl.ANY)
+    return pl.pallas_call(
+        functools.partial(plane_kernel, inside, begin, most, counts, mirrored),
         out_shape=jax.ShapeDtypeStruct((height, columns), dtype),
         grid_spec=pltpu.PrefetchScalarGridSpec(
             num_scalar_prefetch=3,
-            grid=(planes,),
-            in_specs=[
-                pl.BlockSpec((1, most * edge, edge), lambda p, source, *_: (source[p], inside, 0))
-            ]
-            + [pl.BlockSpec((1, height, columns), held(index)) for index in range(len(counts))]
-            + [pl.BlockSpec(memory_space=pl.ANY)] * len(after),
-            out_specs=pl.BlockSpec((height, columns), lambda p, *_: (0, 0)),
-            scratch_shapes=[pltpu.VMEM((block_rows + 1, edge, columns), jnp.float32)],
+            grid=(),
+            in_specs=[anywhere] * (1 + len(omegas) + len(after)),
+            out_specs=pl.BlockSpec(memory_space=pltpu.VMEM),
+            scratch_shapes=[
+                pltpu.VMEM((block_rows + 1, edge, columns), jnp.float32),
+                pltpu.VMEM((planes, most * edge, edge), blocks.dtype),
+                pltpu.VMEM((planes, height, columns), omegas[0].dtype),
+                pltpu.SemaphoreType.DMA((planes,)),
+                pltpu.SemaphoreType.DMA((planes,)),
+            ],
         ),
-        compiler_params=params(),
+        compiler_params=params(VMEM_ALL),
         cost_estimate=COST,
         name="mirror" if mirrored else "home",
     )(sources, rows, cols, blocks, *omegas, *after)
 
 
-def far_kernel(most, parts, lines, added, source_ref, place_ref, row_ref, col_ref, *rest):
-    del place_ref
+def far_kernel(most, sizes, lines, added, source_ref, place_ref, row_ref, col_ref, *rest):
+    parts = len(sizes)
     part_refs, omega_refs = rest[:parts], rest[parts : parts + lines]
-    out_ref, total = rest[-2:]
-    source = source_ref[pl.program_id(0)]
-    edge = part_refs[0].shape[2]
+    out_ref, total, omegas, omega_sem, adds, add_sem, outs, out_sem, part_sem, *blocks = rest[-9 - parts :]
+    edge = total.shape[1]
     spare = total.shape[0] - 1
-    if added:
-        total[:spare] = rest[parts + lines][0].reshape(spare, edge, -1)
-    else:
-        total[...] = jnp.zeros_like(total)
-    places = [
-        (part_ref, inside)
-        for part_ref in part_refs
-        for inside in range(part_ref.shape[1] // (most * edge))
+    count, depth = source_ref.shape[0], outs.shape[0]
+
+    def arrive(k):
+        slot, source = k % depth, source_ref[k]
+        moves = [
+            pltpu.make_async_copy(
+                part_refs[p].at[source, pl.ds(0, sizes[p] * edge), :],
+                blocks[p].at[slot],
+                part_sem.at[p, slot],
+            )
+            for p in range(parts)
+        ]
+        if added:
+            moves.append(
+                pltpu.make_async_copy(rest[parts + lines].at[k], adds.at[slot], add_sem.at[slot])
+            )
+        return moves
+
+    def leave(k):
+        slot = k % depth
+        return pltpu.make_async_copy(outs.at[slot], out_ref.at[place_ref[k]], out_sem.at[slot])
+
+    lead = [
+        pltpu.make_async_copy(omega_refs[index], omegas.at[index], omega_sem.at[index])
+        for index in range(lines)
     ]
-    for index, (omega_ref, (part_ref, inside)) in enumerate(zip(omega_refs, places, strict=True)):
-        for m in range(most):
-            row = row_ref[source, index * most + m]
-            col = jnp.minimum(col_ref[source, index * most + m], spare - 1)
-            slot = inside * most + m
-            block = part_ref[0, slot * edge : (slot + 1) * edge, :]
-            omega = omega_ref[pl.ds(pl.multiple_of(col * edge, edge), edge), :]
-            total[row] += dot(block, omega)
-    out_ref[0] = total[:spare].reshape(out_ref.shape[1:]).astype(out_ref.dtype)
+    for k in range(min(depth, count)):
+        for move in arrive(k):
+            move.start()
+        if k == 0:
+            for move in lead:
+                move.start()
+    for k in range(count):
+        slot, source = k % depth, source_ref[k]
+        for move in arrive(k):
+            move.wait()
+        if added:
+            total[:spare] = adds[slot].reshape(spare, edge, -1)
+        else:
+            total[...] = jnp.zeros_like(total)
+        index = 0
+        for p in range(parts):
+            for place in range(sizes[p]):
+                line = index // most
+                if k == 0 and index % most == 0:
+                    lead[line].wait()
+                row = row_ref[source, index]
+                col = pl.multiple_of(jnp.minimum(col_ref[source, index], spare - 1) * edge, edge)
+                block = blocks[p][slot, place * edge : (place + 1) * edge, :]
+                total[row] += dot(block, omegas[line, pl.ds(col, edge), :])
+                index += 1
+        if k >= depth:
+            leave(k - depth).wait()
+        outs[slot] = total[:spare].reshape(outs.shape[1:]).astype(outs.dtype)
+        leave(k).start()
+        if k + depth < count:
+            for move in arrive(k + depth):
+                move.start()
+    for k in range(max(0, count - depth), count):
+        leave(k).wait()
 
 
 def far_sum(
@@ -234,25 +277,31 @@
     edge = parts[0].shape[2]
     height, columns = omegas[0].shape
     more = [] if add is None else [add]
-    return pl.pallas_call(
-        functools.partial(far_kernel, most, len(parts), len(omegas), len(more)),
+    lines = len(omegas)
+    sizes = [part.shape[1] // (most * edge) * most for part in parts]
+    depth = min(3, sources.shape[0])
+    anywhere = pl.BlockSpec(memory_space=pl.ANY)
+    return pl.pallas_call(
+        functools.partial(far_kernel, most, sizes, lines, len(more)),
         out_shape=jax.ShapeDtypeStruct((slots, height, columns), dtype),
         grid_spec=pltpu.PrefetchScalarGridSpec(
             num_scalar_prefetch=4,
-            grid=sources.shape,
-            in_specs=[
-                pl.BlockSpec((1, part.shape[1], edge), lambda k, source, *_: (source[k], 0, 0))
-                for part in parts
+            grid=(),
+            in_specs=[anywhere] * (len(parts) + lines + len(more) + len(after)),
+            out_specs=anywhere,
+            scratch_shapes=[
+                pltpu.VMEM((block_rows + 1, edge, columns), jnp.float32),
+                pltpu.VMEM((lines, height, columns), omegas[0].dtype),
+                pltpu.SemaphoreType.DMA((lines,)),
+                pltpu.VMEM((depth if more else 1, height, columns), jnp.float32),
+                pltpu.SemaphoreType.DMA((depth,)),
+                pltpu.VMEM((depth, height, columns), dtype),
+                pltpu.SemaphoreType.DMA((depth,)),
+                pltpu.SemaphoreType.DMA((len(parts), depth)),
             ]
-            + [pl.BlockSpec((height, columns), lambda k, *_: (0, 0))] * len(omegas)
-            + [pl.BlockSpec((1, height, columns), lambda k, *_: (k, 0, 0))] * len(more)
-            + [pl.BlockSpec(memory_space=pl.ANY)] * len(after),
-            out_specs=pl.BlockSpec(
-                (1, height, columns), lambda k, source, place, *_: (place[k], 0, 0)
-            ),
-            scratch_shapes=[pltpu.VMEM((block_rows + 1, edge, columns), jnp.float32)],
+            + [pltpu.VMEM((depth, size * edge, edge), parts[0].dtype) for size in sizes],
         ),
-        compiler_params=params(),
+        compiler_params=params(VMEM_ALL),
         cost_estimate=COST,
         name="far",
     )(sources, places, rows, cols, *parts, *omegas, *more, *after)
@@ -488,7 +537,7 @@
     else:
         plane_omegas = [lax.all_gather(sketch, PLANE)]
         sources = jnp.arange(planes)
-    outgoing[1] = hold(outgoing[1], line_omegas)
+    outgoing[1] = hold(outgoing[1], line_omegas[1:])
     parts = [lax.all_to_all(part, PLANE, 0, 0, tiled=True) for part in outgoing]
     lines = sizes[0] * edge
     rows = parts[0][:, lines, :slots].astype(jnp.int32)
@@ -548,10 +597,11 @@
     for index in range(cut, layers - 1):
         piece, latest = send_mirror(index, latest)
         late.append(piece)
+    own_other, latest = ask(chip.reshape(1), latest)
     sent = far(away * cores + core, away, chips, dtype=jnp.bfloat16, add=other, after=latest)
-    received = lax.all_to_all(hold(sent, parts[-1:]), CHIPS, 0, 0, tiled=True)
-    other, latest = ask(chip.reshape(1), (sent,))
-    mirror, latest = send_mirror(layers - 1, latest)
+    sent = hold(sent, parts[-1:])
+    received = lax.all_to_all(sent, CHIPS, 0, 0, tiled=True)
+    mirror, latest = send_mirror(layers - 1, (sent,))
     home = plane_sum(
         outgoing[-1],
         plane_omegas,
@@ -567,7 +617,7 @@
         latest,
     )
     own = far(
-        chip.reshape(1) * cores + core, jnp.arange(1), 1, dtype=jnp.float32, add=other, after=(home,)
+        chip.reshape(1) * cores + core, jnp.arange(1), 1, dtype=jnp.float32, add=own_other, after=(home,)
     )
     base = base_sum(diag_blocks, sketch, [home, mirror, own.reshape(sketch.shape)] + pieces)
     image, part = image_and_gram(base, chip, received, late, block_rows * edge * peers)

time: 444 us -> 433 us (0.975)
  Pallas kernels: 281 us -> 268 us
  waiting for transfers between devices: 71.1 us -> 81.8 us
  starting transfers between devices: 45 us -> 39.4 us
  local copies, waits for them, and re-layouts: 15.4 us -> 10.9 us
    all_to_all x3, waiting for transfers between devices: 13.8 us -> 41.8 us  [on_device(): parts = [lax.all_to_all(part, PLANE, 0, 0, tiled=True) for part in outgoing]]
    ppermute x3, waiting for transfers between devices: 21.4 us -> 0.72 us  [on_device(): line_omegas.append(lax.ppermute(sketch, LINE, steps))]
    pallas_call x9, Pallas kernels: 70 us -> 57.5 us  [the longest x5 32.4 us: plane_sum(): pl.pallas_call(functools.partial(plane_kernel, inside, begin, most, count...]
    unnamed x25 -> x15, local copies, waits for them, and re-layouts: 11.2 us -> 5.01 us
    ppermute x3, starting transfers between devices: 13.9 us -> 7.95 us  [send_mirror(): return (lax.ppermute(mirror, LINE, steps) if shift else mirror, (mirror,))]
    ppermute x3, waiting for transfers between devices: 5.06 us -> 9.58 us  [send_mirror(): return (lax.ppermute(mirror, LINE, steps) if shift else mirror, (mirror,))]
  transfers between devices with their start and end apart: 17 -> 17, of which waited for: 7 -> 8; matrix products, arithmetic and copies ran while one was open for 2% -> 3% of each run, Pallas kernels for 19% -> 17%
where the time goes in v5:
time: 433 us; the launch traced here: 431 us
  Pallas kernels  268 us (62%)
  waiting for transfers between devices  81.8 us (19%)
  starting transfers between devices  39.4 us (9%)
  blocking collectives  25.1 us (6%)
  local copies, waits for them, and re-layouts  10.9 us (3%)
  other arithmetic  4.62 us (1%)
    pallas_call x1, Pallas kernels, factor_and_basis(): pl.pallas_call(functools.partial(factor_kernel, rounds), out_shape=(jax.S...  189 us
    all_to_all x3, waiting for transfers between devices, on_device(): parts = [lax.all_to_all(part, PLANE, 0, 0, tiled=True) for part in outgoing]  41.8 us
    pallas_call x5, Pallas kernels, plane_sum(): pl.pallas_call(functools.partial(plane_kernel, inside, begin, most, count...  32.4 us
    pallas_call x4, Pallas kernels, far_sum(): pl.pallas_call(functools.partial(far_kernel, most, sizes, lines, len(more...  25.1 us
    all_to_all x3, starting transfers between devices, on_device(): parts = [lax.all_to_all(part, PLANE, 0, 0, tiled=True) for part in outgoing]  13.6 us
    all_to_all x1, blocking collectives, sum_over_devices(): return lax.all_to_all(mine, ALL, 0, 0, tiled=True).reshape(rows, columns)  12.8 us
    all_to_all x1, blocking collectives, sum_over_devices(): lax.all_to_all(part.reshape(peers, rows // peers, columns), ALL, 0, 0, ti...  12.3 us
    all_to_all x1, waiting for transfers between devices, on_device(): received = lax.all_to_all(sent, CHIPS, 0, 0, tiled=True)  11.9 us
  transfers between devices with their start and end apart: 17, of which 8 were waited for; matrix products, arithmetic and copies ran while one was open for 3% of the time, Pallas kernels for 17%

profile of v5, /device:TPU:0, one launch (start us, length us, event | category | flops | bytes accessed | tf_op | source)
XLA Modules:
  0.0 431.3 jit_solution(17268413986739367930)
XLA Ops:
  12.3 5.7 %pack.1 = (bf16[8,2064,128]{2,1,0:T(8,128)(2,1)}, bf16[8,1024,128]{2,1,0:T(8,128)(2,1)S(1)}, bf16[8,1024,128]{2,1,0:T(8,128)(2,1)}) custom-call(s32[128]{0:T(128)S(1)} %get-tuple-element.14.entry_ref, s32[128]{0:T(128)S(1)} %get-tuple-element.13.plane_ref, s32[128]{0:T(128)S(1)} %get-tuple-element.12.slot_ref, s32[4]{0:T(128)S(1)} %convert_reduce_fusion.2.count_ref, ...), custom_call_target="tpu_custom_call" | custom-call | flops 999999995904 | bytes 99999997952 | tf_op jit(solution)/shard_map/pack/pallas_call | solution.py:72
  22.4 4.7 %collective-permute-done.refs_1_.rest_1_ = bf16[2048,256]{1,0:T(8,128)(2,1)} collective-permute-done((bf16[2048,256]{1,0:T(8,128)(2,1)}, bf16[2048,256]{1,0:T(8,128)(2,1)}, u32[]{:S(2)}, u32[]{:S(2)}) %collective-permute-start) | collective-permute-done | bytes 1048608 | tf_op jit(solution)/shard_map/ppermute | solution.py:524
  34.1 4.7 %all-to-all-start = ((bf16[8,2064,128]{2,1,0:T(8,128)(2,1)}), bf16[8,2064,128]{2,1,0:T(8,128)(2,1)}, u32[]{:S(2)}, u32[]{:S(2)}) async-start(bf16[8,2064,128]{2,1,0:T(8,128)(2,1)} %hold.3), calls=%async_computation | async-start | bytes 8454144 | tf_op jit(solution)/shard_map/all_to_all | solution.py:541
  42.7 9.3 %collective-permute-done.3.refs_4_ = bf16[1024,256]{1,0:T(8,128)(2,1)} collective-permute-done((bf16[1024,256]{1,0:T(8,128)(2,1)}, bf16[1024,256]{1,0:T(8,128)(2,1)}, u32[]{:S(2)}, u32[]{:S(2)}) %collective-permute-start.3) | collective-permute-done | bytes 524320 | tf_op jit(solution)/shard_map/ppermute | solution.py:528
  56.2 34.6 %all-to-all-done.rest_0_ = bf16[8,2064,128]{2,1,0:T(8,128)(2,1)} async-done(((bf16[8,2064,128]{2,1,0:T(8,128)(2,1)}), bf16[8,2064,128]{2,1,0:T(8,128)(2,1)}, u32[]{:S(2)}, u32[]{:S(2)}) %all-to-all-start) | async-done | bytes 4227104 | tf_op jit(solution)/shard_map/all_to_all | solution.py:541
  96.5 6.4 %mirror.4.rest_3_ = bf16[2048,256]{1,0:T(8,128)(2,1)} custom-call(s32[8]{0:T(128)} %pad_add_fusion.source_ref, s32[8,32]{1,0:T(8,128)} %bitcast.20, s32[8,32]{1,0:T(8,128)} %bitcast.12, bf16[8,2064,128]{2,1,0:T(8,128)(2,1)} %all-to-all-done.rest_0_, bf16[4,2048,256]{2,1,0:T(8,128)(2,1)} %bitcast.29, bf16[4,2048,256]{2,1,0:T(8,128)(2,1)} %bitcast.3.rest_2_), custom_call_target="tpu_custom_call" | custom-call | flops 999999995904 | bytes 99999997952 | tf_op jit(solution)/shard_map/mirror/pallas_call | solution.py:184
  105.5 6.4 %mirror.5.rest_5_ = bf16[2048,256]{1,0:T(8,128)(2,1)} custom-call(s32[8]{0:T(128)} %pad_add_fusion.source_ref, s32[8,32]{1,0:T(8,128)} %bitcast.21, s32[8,32]{1,0:T(8,128)} %bitcast.13, bf16[8,2064,128]{2,1,0:T(8,128)(2,1)} %all-to-all-done.rest_0_, bf16[4,2048,256]{2,1,0:T(8,128)(2,1)} %bitcast.30, bf16[4,2048,256]{2,1,0:T(8,128)(2,1)} %bitcast.3.rest_2_, ...), custom_call_target="tpu_custom_call" | custom-call | flops 999999995904 | bytes 99999997952 | tf_op jit(solution)/shard_map/mirror/pallas_call | solution.py:184
  113.6 7.2 %all-to-all-done.2.rest_1_.rest_0_ = bf16[8,1024,128]{2,1,0:T(8,128)(2,1)} async-done(((bf16[8,1024,128]{2,1,0:T(8,128)(2,1)}), bf16[8,1024,128]{2,1,0:T(8,128)(2,1)}, u32[]{:S(2)}, u32[]{:S(2)}) %all-to-all-start.2) | async-done | bytes 2097184 | tf_op jit(solution)/shard_map/all_to_all | solution.py:541
  120.8 4.5 %all-to-all-start.1 = ((bf16[8,1024,128]{2,1,0:T(8,128)(2,1)}), bf16[8,1024,128]{2,1,0:T(8,128)(2,1)}, u32[]{:S(2)}, u32[]{:S(2)}) async-start(bf16[8,1024,128]{2,1,0:T(8,128)(2,1)} %get-tuple-element.7.rest_0_), calls=%async_computation.1 | async-start | bytes 4194304 | tf_op jit(solution)/shard_map/all_to_all | solution.py:541
  125.9 6.7 %far.4.rest_3_ = f32[3,2048,256]{2,1,0:T(8,128)} custom-call(s32[3]{0:T(128)} %add_subtract_fusion.source_ref, s32[3]{0:T(128)} %iota.31.place_ref, s32[8,32]{1,0:T(8,128)} %bitcast.22, s32[8,32]{1,0:T(8,128)} %bitcast.14, bf16[8,2064,128]{2,1,0:T(8,128)(2,1)} %all-to-all-done.rest_0_, bf16[8,1024,128]{2,1,0:T(8,128)(2,1)} %all-to-all-done.2.rest_1_.rest_0_, ...), custom_call_target="tpu_custom_call" | custom-call | flops 999999995904 | bytes 99999997952 | tf_op jit(solution)/shard_map/far/pallas_call | solution.py:284
  132.9 6.3 %mirror.6.rest_5_ = bf16[2048,256]{1,0:T(8,128)(2,1)} custom-call(s32[8]{0:T(128)} %pad_add_fusion.source_ref, s32[8,32]{1,0:T(8,128)} %bitcast.23, s32[8,32]{1,0:T(8,128)} %bitcast.15, bf16[8,1024,128]{2,1,0:T(8,128)(2,1)} %all-to-all-done.2.rest_1_.rest_0_, bf16[4,2048,256]{2,1,0:T(8,128)(2,1)} %bitcast.31, bf16[4,2048,256]{2,1,0:T(8,128)(2,1)} %bitcast.3.rest_2_, ...), custom_call_target="tpu_custom_call" | custom-call | flops 999999995904 | bytes 99999997952 | tf_op jit(solution)/shard_map/mirror/pallas_call | solution.py:184
  142.9 5.1 %far.5.rest_6_ = f32[1,2048,256]{2,1,0:T(8,128)} custom-call(s32[1]{0:T(128)S(6)} %sub.72.source_ref, s32[1]{0:T(128)} %constant.121.clone.1.place_ref, s32[8,32]{1,0:T(8,128)} %bitcast.24, s32[8,32]{1,0:T(8,128)} %bitcast.16, bf16[8,2064,128]{2,1,0:T(8,128)(2,1)} %all-to-all-done.rest_0_, bf16[8,1024,128]{2,1,0:T(8,128)(2,1)} %all-to-all-done.2.rest_1_.rest_0_, ...), custom_call_target="tpu_custom_call" | custom-call | flops 999999995904 | bytes 99999997952 | tf_op jit(solution)/shard_map/far/pallas_call | solution.py:284
  148.1 7.4 %far.6.x_ref = bf16[4,2048,256]{2,1,0:T(8,128)(2,1)} custom-call(s32[3]{0:T(128)} %get-tuple-element.31.source_ref, s32[3]{0:T(128)} %get-tuple-element.30.place_ref, s32[8,32]{1,0:T(8,128)} %bitcast.25, s32[8,32]{1,0:T(8,128)} %bitcast.17, bf16[8,2064,128]{2,1,0:T(8,128)(2,1)} %all-to-all-done.rest_0_, ...), custom_call_target="tpu_custom_call" | custom-call | flops 999999995904 | bytes 99999997952 | tf_op jit(solution)/shard_map/far/pallas_call | solution.py:284
  155.5 5.1 %all-to-all-start.3 = ((bf16[4,2048,256]{2,1,0:T(8,128)(2,1)}), bf16[4,2048,256]{2,1,0:T(8,128)(2,1)}, u32[]{:S(2)}, u32[]{:S(2)}) async-start(bf16[4,2048,256]{2,1,0:T(8,128)(2,1)} %hold.5.rest_3_), calls=%async_computation.3 | async-start | bytes 8388608 | tf_op jit(solution)/shard_map/all_to_all | solution.py:603
  160.6 6.7 %mirror.7.rest_3_.rest_1_ = f32[2048,256]{1,0:T(8,128)} custom-call(s32[8]{0:T(128)} %pad_add_fusion.source_ref, s32[8,32]{1,0:T(8,128)} %bitcast.26, s32[8,32]{1,0:T(8,128)} %bitcast.18, bf16[8,1024,128]{2,1,0:T(8,128)(2,1)} %all-to-all-done.1.rest_0_, bf16[4,2048,256]{2,1,0:T(8,128)(2,1)} %bitcast.32, bf16[4,2048,256]{2,1,0:T(8,128)(2,1)} %bitcast.3.rest_2_, ...), custom_call_target="tpu_custom_call" | custom-call | flops 999999995904 | bytes 99999997952 | tf_op jit(solution)/shard_map/mirror/pallas_call | solution.py:184
  167.3 6.6 %home.1.rest_6_.rest_0_ = f32[2048,256]{1,0:T(8,128)} custom-call(s32[8]{0:T(128)} %pad_add_fusion.source_ref, s32[8,32]{1,0:T(8,128)} %add.284.row_ref, s32[8,32]{1,0:T(8,128)} %add.287.col_ref, bf16[8,1024,128]{2,1,0:T(8,128)(2,1)} %get-tuple-element.7.rest_0_, bf16[4,2048,256]{2,1,0:T(8,128)(2,1)} %bitcast.33, bf16[4,2048,256]{2,1,0:T(8,128)(2,1)} %bitcast.3.rest_2_, ...), custom_call_target="tpu_custom_call" | custom-call | flops 999999995904 | bytes 99999997952 | tf_op jit(solution)/shard_map/home/pallas_call | solution.py:184
  173.9 5.9 %far.7 = f32[1,2048,256]{2,1,0:T(8,128)} custom-call(s32[1]{0:T(128)S(6)} %add.302.source_ref, s32[1]{0:T(128)} %constant.121.clone.1.place_ref, s32[8,32]{1,0:T(8,128)} %bitcast.27, s32[8,32]{1,0:T(8,128)} %bitcast.19, bf16[8,2064,128]{2,1,0:T(8,128)(2,1)} %all-to-all-done.rest_0_, bf16[8,1024,128]{2,1,0:T(8,128)(2,1)} %all-to-all-done.2.rest_1_.rest_0_, ...), custom_call_target="tpu_custom_call" | custom-call | flops 999999995904 | bytes 99999997952 | tf_op jit(solution)/shard_map/far/pallas_call | solution.py:284
  179.9 6.2 %base.1.base_ref = f32[2048,256]{1,0:T(8,128)S(1)} custom-call(bf16[16,128,128]{2,1,0:T(8,128)(2,1)S(1)} %copy-done.2, bf16[2048,256]{1,0:T(8,128)(2,1)S(1)} %copy-done.1, f32[2048,256]{1,0:T(8,128)} %home.1.rest_6_.rest_0_, f32[2048,256]{1,0:T(8,128)} %mirror.7.rest_3_.rest_1_, f32[2048,256]{1,0:T(8,128)} %bitcast.34, ...), custom_call_target="tpu_custom_call" | custom-call | flops 999999995904 | bytes 99999997952 | tf_op jit(solution)/shard_map/base/pallas_call | solution.py:327
  187.4 9.6 %collective-permute-done.12.rest_0_ = bf16[2048,256]{1,0:T(8,128)(2,1)} collective-permute-done((bf16[2048,256]{1,0:T(8,128)(2,1)}, bf16[2048,256]{1,0:T(8,128)(2,1)}, u32[]{:S(2)}, u32[]{:S(2)}) %collective-permute-start.12) | collective-permute-done | bytes 1048608 | tf_op jit(solution)/shard_map/ppermute | solution.py:566
  197.0 11.9 %all-to-all-done.3.far_ref = bf16[4,2048,256]{2,1,0:T(8,128)(2,1)} async-done(((bf16[4,2048,256]{2,1,0:T(8,128)(2,1)}), bf16[4,2048,256]{2,1,0:T(8,128)(2,1)}, u32[]{:S(2)}, u32[]{:S(2)}) %all-to-all-start.3) | async-done | bytes 4194336 | tf_op jit(solution)/shard_map/all_to_all | solution.py:603
  210.5 6.5 %image.1 = (f32[2048,256]{1,0:T(8,128)S(1)}, f32[256,256]{1,0:T(8,128)S(1)}) custom-call(s32[1]{0:T(128)} %bitcast.chip_ref, f32[2048,256]{1,0:T(8,128)S(1)} %copy-done.4, bf16[4,2048,256]{2,1,0:T(8,128)(2,1)} %all-to-all-done.3.far_ref, bf16[2048,256]{1,0:T(8,128)(2,1)} %collective-permute-done.12.rest_0_), custom_call_target="tpu_custom_call" | custom-call | flops 999999995904 | bytes 99999997952 | tf_op jit(solution)/shard_map/image/pallas_call | solution.py:369
  217.0 12.3 %all_to_all.30 = f32[32,8,256]{2,1,0:T(8,128)S(1)} all-to-all(f32[32,8,256]{2,1,0:T(8,128)S(1)} %bitcast.11), channel_id=1, replica_groups=mesh['z'=4,'x'=2,'y'=2,'c'=2] {'z','x','y','c'}, dimensions={0} | all-to-all | bytes 524288 | tf_op jit(solution)/shard_map/all_to_all | solution.py:461
  229.4 12.8 %all_to_all.31 = f32[32,8,256]{2,1,0:T(8,128)S(1)} all-to-all(f32[32,8,256]{2,1,0:T(8,128)S(1)} %broadcast_in_dim.86), channel_id=1, replica_groups=mesh['z'=4,'x'=2,'y'=2,'c'=2] {'z','x','y','c'}, dimensions={0} | all-to-all | bytes 524288 | tf_op jit(solution)/shard_map/all_to_all | solution.py:463
  242.2 189.1 %factor.1 = (f32[2048,256]{1,0:T(8,128)}, f32[256,256]{1,0:T(8,128)}) custom-call(f32[256,256]{1,0:T(8,128)S(1)} %bitcast.10, f32[2048,256]{1,0:T(8,128)S(1)} %get-tuple-element.11.image_ref), custom_call_target="tpu_custom_call" | custom-call | tf_op jit(solution)/shard_map/factor/pallas_call | solution.py:447
  (70 shorter events, 48.7 us)
Async XLA Ops:
  0.6 26.5 %collective-permute-start = (bf16[2048,256]{1,0:T(8,128)(2,1)}, bf16[2048,256]{1,0:T(8,128)(2,1)}, u32[]{:S(2)}, u32[]{:S(2)}) collective-permute-start(bf16[2048,256]{1,0:T(8,128)(2,1)} %omega_ref.1), channel_id=1, source_target_pairs={{0,2},{2,0},{1,3},{3,1},{4,6},{6,4},{5,7},{7,5},{8,10},{10,8},{9,1... | collective-permute-start | bytes 3145736 | tf_op jit(solution)/shard_map/ppermute | solution.py:524
  3.7 27.1 %collective-permute-start.1 = (bf16[2048,256]{1,0:T(8,128)(2,1)}, bf16[2048,256]{1,0:T(8,128)(2,1)}, u32[]{:S(2)}, u32[]{:S(2)}) collective-permute-start(bf16[2048,256]{1,0:T(8,128)(2,1)} %omega_ref.1), channel_id=1, source_target_pairs={{0,4},{4,0},{1,5},{5,1},{2,6},{6,2},{3,7},{7,3},{8,12},{12,8},{9,1... | collective-permute-start | bytes 3145736 | tf_op jit(solution)/shard_map/ppermute | solution.py:524
  5.2 50.3 %collective-permute-start.5 = (bf16[2048,256]{1,0:T(8,128)(2,1)}, bf16[2048,256]{1,0:T(8,128)(2,1)}, u32[]{:S(2)}, u32[]{:S(2)}) collective-permute-start(bf16[2048,256]{1,0:T(8,128)(2,1)} %omega_ref.1), channel_id=1, source_target_pairs={{0,24},{8,0},{16,8},{24,16},{1,25},{9,1},{17,9},{25,17},{2,26},{10... | collective-permute-start | bytes 3145736 | tf_op jit(solution)/shard_map/ppermute | solution.py:520
  8.8 47.4 %collective-permute-start.6 = (bf16[2048,256]{1,0:T(8,128)(2,1)}, bf16[2048,256]{1,0:T(8,128)(2,1)}, u32[]{:S(2)}, u32[]{:S(2)}) collective-permute-start(bf16[2048,256]{1,0:T(8,128)(2,1)} %omega_ref.1), channel_id=1, source_target_pairs={{0,8},{8,16},{16,24},{24,0},{1,9},{9,17},{17,25},{25,1},{2,10},{10... | collective-permute-start | bytes 3145736 | tf_op jit(solution)/shard_map/ppermute | solution.py:520
  8.8 116.6 %collective-permute-start.7 = (bf16[2048,256]{1,0:T(8,128)(2,1)}, bf16[2048,256]{1,0:T(8,128)(2,1)}, u32[]{:S(2)}, u32[]{:S(2)}) collective-permute-start(bf16[2048,256]{1,0:T(8,128)(2,1)} %omega_ref.1), channel_id=1, source_target_pairs={{0,16},{8,24},{16,0},{24,8},{1,17},{9,25},{17,1},{25,9},{2,18},{10... | collective-permute-start | bytes 3145736 | tf_op jit(solution)/shard_map/ppermute | solution.py:520
  12.2 7.1 %copy-start.6 = (s32[256]{0:T(256)S(1)}, s32[256]{0:T(256)}, u32[]{:S(2)}) copy-start(s32[256]{0:T(256)} %get-tuple-element.24) | copy-start | bytes 3076
  12.2 7.7 %copy-start.5 = (s32[256]{0:T(256)S(1)}, s32[256]{0:T(256)}, u32[]{:S(2)}) copy-start(s32[256]{0:T(256)} %get-tuple-element.34) | copy-start | bytes 3076
  18.0 1.3 copy-start
  29.0 13.7 %collective-permute-start.2 = (bf16[1024,256]{1,0:T(8,128)(2,1)}, bf16[1024,256]{1,0:T(8,128)(2,1)}, u32[]{:S(2)}, u32[]{:S(2)}) collective-permute-start(bf16[1024,256]{1,0:T(8,128)(2,1)} %slice.16), channel_id=1, source_target_pairs={{0,4},{4,0},{1,5},{5,1},{2,6},{6,2},{3,7},{7,3},{8,12},{12,8},{9,1... | collective-permute-start | bytes 1572872 | tf_op jit(solution)/shard_map/ppermute | solution.py:527
  32.6 19.4 %collective-permute-start.3 = (bf16[1024,256]{1,0:T(8,128)(2,1)}, bf16[1024,256]{1,0:T(8,128)(2,1)}, u32[]{:S(2)}, u32[]{:S(2)}) collective-permute-start(bf16[1024,256]{1,0:T(8,128)(2,1)} %slice.17), channel_id=1, source_target_pairs={{0,2},{2,0},{1,3},{3,1},{4,6},{6,4},{5,7},{7,5},{8,10},{10,8},{9,1... | collective-permute-start | bytes 1572872 | tf_op jit(solution)/shard_map/ppermute | solution.py:528
  34.1 17.9 %copy-start.1 = (bf16[2048,256]{1,0:T(8,128)(2,1)S(1)}, bf16[2048,256]{1,0:T(8,128)(2,1)}, u32[]{:S(2)}) copy-start(bf16[2048,256]{1,0:T(8,128)(2,1)} %omega_ref.1) | copy-start | bytes 3145732
  34.1 56.6 %all-to-all-start = ((bf16[8,2064,128]{2,1,0:T(8,128)(2,1)}), bf16[8,2064,128]{2,1,0:T(8,128)(2,1)}, u32[]{:S(2)}, u32[]{:S(2)}) async-start(bf16[8,2064,128]{2,1,0:T(8,128)(2,1)} %hold.3), calls=%async_computation | async-start | bytes 8454144 | tf_op jit(solution)/shard_map/all_to_all | solution.py:541
  55.4 41.1 %collective-permute-start.4 = (bf16[8192,256]{1,0:T(8,128)(2,1)}, bf16[8192,256]{1,0:T(8,128)(2,1)}, u32[]{:S(2)}, u32[]{:S(2)}) collective-permute-start(bf16[8192,256]{1,0:T(8,128)(2,1)} %join.1), channel_id=1, source_target_pairs={{0,1},{1,0},{2,3},{3,2},{4,5},{5,4},{6,7},{7,6},{8,9},{9,8},{10,11... | collective-permute-start | bytes 12582920 | tf_op jit(solution)/shard_map/ppermute | solution.py:533
  90.7 30.1 %all-to-all-start.2 = ((bf16[8,1024,128]{2,1,0:T(8,128)(2,1)}), bf16[8,1024,128]{2,1,0:T(8,128)(2,1)}, u32[]{:S(2)}, u32[]{:S(2)}) async-start(bf16[8,1024,128]{2,1,0:T(8,128)(2,1)} %hold.4), calls=%async_computation.2 | async-start | bytes 4194304 | tf_op jit(solution)/shard_map/all_to_all | solution.py:541
  102.9 77.0 %collective-permute-start.10 = (bf16[2048,256]{1,0:T(8,128)(2,1)}, bf16[2048,256]{1,0:T(8,128)(2,1)}, u32[]{:S(2)}, u32[]{:S(2)}) collective-permute-start(bf16[2048,256]{1,0:T(8,128)(2,1)} %mirror.4.rest_3_), channel_id=1, source_target_pairs={{0,16},{8,24},{16,0},{24,8},{1,17},{9,25},{17,1},{25,9},{2,18},{10... | collective-permute-start | bytes 3145736 | tf_op jit(solution)/shard_map/ppermute | solution.py:566
  111.9 68.0 %collective-permute-start.11 = (bf16[2048,256]{1,0:T(8,128)(2,1)}, bf16[2048,256]{1,0:T(8,128)(2,1)}, u32[]{:S(2)}, u32[]{:S(2)}) collective-permute-start(bf16[2048,256]{1,0:T(8,128)(2,1)} %mirror.5.rest_5_), channel_id=1, source_target_pairs={{0,8},{8,16},{16,24},{24,0},{1,9},{9,17},{17,25},{25,1},{2,10},{10... | collective-permute-start | bytes 3145736 | tf_op jit(solution)/shard_map/ppermute | solution.py:566
  120.8 34.7 %all-to-all-start.1 = ((bf16[8,1024,128]{2,1,0:T(8,128)(2,1)}), bf16[8,1024,128]{2,1,0:T(8,128)(2,1)}, u32[]{:S(2)}, u32[]{:S(2)}) async-start(bf16[8,1024,128]{2,1,0:T(8,128)(2,1)} %get-tuple-element.7.rest_0_), calls=%async_computation.1 | async-start | bytes 4194304 | tf_op jit(solution)/shard_map/all_to_all | solution.py:541
  132.6 15.4 %collective-permute-start.8 = (f32[3,2048,256]{2,1,0:T(8,128)}, f32[3,2048,256]{2,1,0:T(8,128)}, u32[]{:S(2)}, u32[]{:S(2)}) collective-permute-start(f32[3,2048,256]{2,1,0:T(8,128)} %far.4.rest_3_), channel_id=1, source_target_pairs={{0,1},{1,0},{2,3},{3,2},{4,5},{5,4},{6,7},{7,6},{8,9},{9,8},{10,11... | collective-permute-start | bytes 18874376 | tf_op jit(solution)/shard_map/ppermute | solution.py:593
  139.2 57.8 %collective-permute-start.12 = (bf16[2048,256]{1,0:T(8,128)(2,1)}, bf16[2048,256]{1,0:T(8,128)(2,1)}, u32[]{:S(2)}, u32[]{:S(2)}) collective-permute-start(bf16[2048,256]{1,0:T(8,128)(2,1)} %mirror.6.rest_5_), channel_id=1, source_target_pairs={{0,24},{8,0},{16,8},{24,16},{1,25},{9,1},{17,9},{25,17},{2,26},{10... | collective-permute-start | bytes 3145736 | tf_op jit(solution)/shard_map/ppermute | solution.py:566
  147.9 26.0 %collective-permute-start.9 = (f32[1,2048,256]{2,1,0:T(8,128)}, f32[1,2048,256]{2,1,0:T(8,128)}, u32[]{:S(2)}, u32[]{:S(2)}) collective-permute-start(f32[1,2048,256]{2,1,0:T(8,128)} %far.5.rest_6_), channel_id=1, source_target_pairs={{0,1},{1,0},{2,3},{3,2},{4,5},{5,4},{6,7},{7,6},{8,9},{9,8},{10,11... | collective-permute-start | bytes 6291464 | tf_op jit(solution)/shard_map/ppermute | solution.py:593
  155.5 53.4 %all-to-all-start.3 = ((bf16[4,2048,256]{2,1,0:T(8,128)(2,1)}), bf16[4,2048,256]{2,1,0:T(8,128)(2,1)}, u32[]{:S(2)}, u32[]{:S(2)}) async-start(bf16[4,2048,256]{2,1,0:T(8,128)(2,1)} %hold.5.rest_3_), calls=%async_computation.3 | async-start | bytes 8388608 | tf_op jit(solution)/shard_map/all_to_all | solution.py:603
  173.9 6.0 %copy-start.2 = (bf16[16,128,128]{2,1,0:T(8,128)(2,1)S(1)}, bf16[16,128,128]{2,1,0:T(8,128)(2,1)}, u32[]{:S(2)}) copy-start(bf16[16,128,128]{2,1,0:T(8,128)(2,1)} %diag_ref.1) | copy-start | bytes 1572868
  186.1 1.3 copy-start.3
  208.9 1.6 copy-start.4

commit v6 on v5

--- a/solution.py
+++ b/solution.py
@@ -203,66 +203,83 @@
     )(sources, rows, cols, blocks, *omegas, *after)
 
 
-def far_kernel(most, sizes, lines, added, source_ref, place_ref, row_ref, col_ref, *rest):
-    parts = len(sizes)
-    part_refs, omega_refs = rest[:parts], rest[parts : parts + lines]
-    out_ref, total, omegas, omega_sem, adds, add_sem, outs, out_sem, part_sem, *blocks = rest[-9 - parts :]
+def far_kernel(most, begin, sizes, lines, added, at_home, *refs):
+    source_ref, place_ref, above_ref, row_ref, col_ref, home_row_ref, home_col_ref, *refs = refs
+    part_refs, refs = refs[: len(sizes)], refs[len(sizes) :]
+    omega_refs, refs = refs[: 2 * lines], refs[2 * lines :]
+    home_refs, refs = refs[: 2 * at_home], refs[2 * at_home :]
+    add_refs = refs[:added]
+    scratch = refs[len(refs) - 7 - len(sizes) - added - 2 * at_home :]
+    out_ref, total, omegas, omega_sem, outs, out_sem, sems, *held = scratch
+    blocks, adds, homes = held[: len(sizes)], held[len(sizes) : len(sizes) + added], held[len(sizes) + added :]
     edge = total.shape[1]
     spare = total.shape[0] - 1
     count, depth = source_ref.shape[0], outs.shape[0]
 
     def arrive(k):
         slot, source = k % depth, source_ref[k]
-        moves = [
-            pltpu.make_async_copy(
-                part_refs[p].at[source, pl.ds(0, sizes[p] * edge), :],
-                blocks[p].at[slot],
-                part_sem.at[p, slot],
-            )
-            for p in range(parts)
+        pairs = [
+            (part_ref.at[source, pl.ds(0, size * edge), :], block.at[slot])
+            for part_ref, size, block in zip(part_refs, sizes, blocks)
         ]
-        if added:
-            moves.append(
-                pltpu.make_async_copy(rest[parts + lines].at[k], adds.at[slot], add_sem.at[slot])
-            )
-        return moves
+        if at_home:
+            pairs.append((home_refs[0].at[source], homes[0].at[slot]))
+        pairs += [(add_ref.at[k], add.at[slot]) for add_ref, add in zip(add_refs, adds)]
+        return [pltpu.make_async_copy(a, b, sems.at[slot, i]) for i, (a, b) in enumerate(pairs)]
 
     def leave(k):
         slot = k % depth
         return pltpu.make_async_copy(outs.at[slot], out_ref.at[place_ref[k]], out_sem.at[slot])
 
     lead = [
-        pltpu.make_async_copy(omega_refs[index], omegas.at[index], omega_sem.at[index])
+        [
+            pltpu.make_async_copy(omega_ref, omegas.at[index], omega_sem.at[index])
+            for omega_ref in omega_refs[2 * index : 2 * index + 2]
+        ]
         for index in range(lines)
     ]
+    if at_home:
+        own = pltpu.make_async_copy(home_refs[1], homes[1], omega_sem.at[lines])
     for k in range(min(depth, count)):
         for move in arrive(k):
             move.start()
         if k == 0:
-            for move in lead:
-                move.start()
+            if at_home:
+                own.start()
+            for index, (above, below) in enumerate(lead):
+                pl.when(above_ref[index] == 1)(above.start)
+                pl.when(above_ref[index] == 0)(below.start)
     for k in range(count):
         slot, source = k % depth, source_ref[k]
         for move in arrive(k):
             move.wait()
-        if added:
-            total[:spare] = adds[slot].reshape(spare, edge, -1)
-        else:
-            total[...] = jnp.zeros_like(total)
+        total[...] = jnp.zeros_like(total)
+        if at_home:
+            if k == 0:
+                own.wait()
+            for place in range(most):
+                row = jnp.minimum(home_row_ref[source, place], spare - 1)
+                row = pl.multiple_of(row * edge, edge)
+                block = homes[0][slot, place * edge : (place + 1) * edge, :]
+                product = dot(block, homes[1][pl.ds(row, edge), :], TN).astype(jnp.bfloat16)
+                total[home_col_ref[source, place]] += product.astype(jnp.float32)
         index = 0
-        for p in range(parts):
-            for place in range(sizes[p]):
+        for block_ref, size in zip(blocks, sizes):
+            for place in range(size):
                 line = index // most
                 if k == 0 and index % most == 0:
-                    lead[line].wait()
-                row = row_ref[source, index]
-                col = pl.multiple_of(jnp.minimum(col_ref[source, index], spare - 1) * edge, edge)
-                block = blocks[p][slot, place * edge : (place + 1) * edge, :]
-                total[row] += dot(block, omegas[line, pl.ds(col, edge), :])
+                    lead[line][0].wait()
+                row = row_ref[source, begin + index]
+                col = jnp.minimum(col_ref[source, begin + index], spare - 1)
+                block = block_ref[slot, place * edge : (place + 1) * edge, :]
+                total[row] += dot(block, omegas[line, pl.ds(pl.multiple_of(col * edge, edge), edge), :])
                 index += 1
         if k >= depth:
             leave(k - depth).wait()
-        outs[slot] = total[:spare].reshape(outs.shape[1:]).astype(outs.dtype)
+        result = total[:spare].reshape(outs.shape[1:])
+        for add in adds:
+            result += add[slot].astype(jnp.float32)
+        outs[slot] = result.astype(outs.dtype)
         leave(k).start()
         if k + depth < count:
             for move in arrive(k + depth):
@@ -272,39 +289,45 @@
 
 
 def far_sum(
-    sources, places, slots, parts, omegas, rows, cols, most, block_rows, dtype, add=None, after=()
+    sources, places, slots, begin, parts, omegas, rows, cols, home, most, block_rows, dtype, adds=(), after=()
 ):
     edge = parts[0].shape[2]
-    height, columns = omegas[0].shape
-    more = [] if add is None else [add]
+    height, columns = omegas[0][0].shape
     lines = len(omegas)
+    above = jnp.stack([choice for _, _, choice in omegas])
+    pairs = [omega for pair in omegas for omega in pair[:2]]
     sizes = [part.shape[1] // (most * edge) * most for part in parts]
     depth = min(3, sources.shape[0])
+    home_rows, home_cols, *at_home = home if home else (rows[:, :most], cols[:, :most])
+    arrays = [*parts, *pairs, *at_home, *adds, *after]
     anywhere = pl.BlockSpec(memory_space=pl.ANY)
     return pl.pallas_call(
-        functools.partial(far_kernel, most, sizes, lines, len(more)),
+        functools.partial(far_kernel, most, begin, sizes, lines, len(adds), 1 if home else 0),
         out_shape=jax.ShapeDtypeStruct((slots, height, columns), dtype),
         grid_spec=pltpu.PrefetchScalarGridSpec(
-            num_scalar_prefetch=4,
+            num_scalar_prefetch=7,
             grid=(),
-            in_specs=[anywhere] * (len(parts) + lines + len(more) + len(after)),
+            in_specs=[anywhere] * len(arrays),
             out_specs=anywhere,
             scratch_shapes=[
                 pltpu.VMEM((block_rows + 1, edge, columns), jnp.float32),
-                pltpu.VMEM((lines, height, columns), omegas[0].dtype),
-                pltpu.SemaphoreType.DMA((lines,)),
-                pltpu.VMEM((depth if more else 1, height, columns), jnp.float32),
-                pltpu.SemaphoreType.DMA((depth,)),
+                pltpu.VMEM((lines, height, columns), pairs[0].dtype),
+                pltpu.SemaphoreType.DMA((lines + 1,)),
                 pltpu.VMEM((depth, height, columns), dtype),
                 pltpu.SemaphoreType.DMA((depth,)),
-                pltpu.SemaphoreType.DMA((len(parts), depth)),
+                pltpu.SemaphoreType.DMA((depth, len(parts) + 1 + len(adds))),
             ]
-            + [pltpu.VMEM((depth, size * edge, edge), parts[0].dtype) for size in sizes],
+            + [pltpu.VMEM((depth, size * edge, edge), parts[0].dtype) for size in sizes]
+            + [pltpu.VMEM((depth, height, columns), add.dtype) for add in adds]
+            + [
+                pltpu.VMEM(shape, parts[0].dtype)
+                for shape in ([(depth, most * edge, edge), (height, columns)] if home else [])
+            ],
         ),
         compiler_params=params(VMEM_ALL),
         cost_estimate=COST,
         name="far",
-    )(sources, places, rows, cols, *parts, *omegas, *more, *after)
+    )(sources, places, above, rows, cols, home_rows, home_cols, *arrays)
 
 
 def base_kernel(diag_ref, omega_ref, *rest):
@@ -338,34 +361,49 @@
 
 
 def image_kernel(scale, chip_ref, base_ref, far_ref, *rest):
-    *piece_refs, image_ref, gram_ref, cross = rest
-    step = pl.program_id(0)
-    image = base_ref[...]
-    for piece_ref in piece_refs:
-        image += piece_ref[...].astype(jnp.float32)
-    for chip in range(far_ref.shape[0]):
-        piece = far_ref[chip].astype(jnp.float32)
-        image += jnp.where(chip == chip_ref[0], 0.0, piece)
-    image_ref[...] = image
-
-    @pl.when(step == 0)
-    def _():
-        gram_ref[...] = jnp.zeros_like(gram_ref)
-        cross[...] = jnp.zeros_like(cross)
-
-    high, low = split(image)
-    gram_ref[...] += dot(high, high, TN)
-    cross[...] += dot(high, low, TN)
-
-    @pl.when(step == pl.num_programs(0) - 1)
-    def _():
-        gram_ref[...] = (gram_ref[...] + (cross[...] + cross[...].T)) * scale
+    *piece_refs, image_ref, gram_ref, cross, bases, fars, pieces, images, sems, out_sem = rest
+    chips, (tiles, tile, _) = far_ref.shape[0], bases.shape
+    from_chips = [lax.rem(chip_ref[0] + step, chips) for step in range(1, chips)]
+    waits = []
+    for t in range(tiles):
+        rows = pl.ds(t * tile, tile)
+        pairs = [(base_ref.at[rows, :], bases.at[t])]
+        pairs += [(far_ref.at[chip, rows, :], fars.at[t, i]) for i, chip in enumerate(from_chips)]
+        pairs += [(ref.at[rows, :], pieces.at[t, i]) for i, ref in enumerate(piece_refs)]
+        waits.append([pltpu.make_async_copy(a, b, sems.at[t, i]) for i, (a, b) in enumerate(pairs)])
+        for move in waits[-1]:
+            move.start()
+    gram_ref[...] = jnp.zeros_like(gram_ref)
+    cross[...] = jnp.zeros_like(cross)
+    leave = []
+    for t in range(tiles):
+        for move in waits[t]:
+            move.wait()
+        image = bases[t]
+        for i in range(len(piece_refs)):
+            image += pieces[t, i].astype(jnp.float32)
+        for i in range(chips - 1):
+            image += fars[t, i].astype(jnp.float32)
+        images[t] = image
+        leave.append(
+            pltpu.make_async_copy(
+                images.at[t], image_ref.at[pl.ds(t * tile, tile), :], out_sem.at[t]
+            )
+        )
+        leave[-1].start()
+        high, low = split(image)
+        gram_ref[...] += dot(high, high, TN)
+        cross[...] += dot(high, low, TN)
+    gram_ref[...] = (gram_ref[...] + (cross[...] + cross[...].T)) * scale
+    for move in leave:
+        move.wait()
 
 
 def image_and_gram(base, chip, far, pieces, total_rows):
     height, columns = base.shape
     tile = math.gcd(height, 256)
-    rows = pl.BlockSpec((tile, columns), lambda b, _: (b, 0))
+    tiles, chips = height // tile, far.shape[0]
+    anywhere = pl.BlockSpec(memory_space=pl.ANY)
     return pl.pallas_call(
         functools.partial(image_kernel, 1.0 / total_rows),
         out_shape=(
@@ -374,84 +412,108 @@
         ),
         grid_spec=pltpu.PrefetchScalarGridSpec(
             num_scalar_prefetch=1,
-            grid=(height // tile,),
-            in_specs=[rows, pl.BlockSpec((far.shape[0], tile, columns), lambda b, _: (0, b, 0))]
-            + [rows] * len(pieces),
-            out_specs=(rows, pl.BlockSpec((columns, columns), lambda b, _: (0, 0))),
-            scratch_shapes=[pltpu.VMEM((columns, columns), jnp.float32)],
+            grid=(),
+            in_specs=[anywhere] * (2 + len(pieces)),
+            out_specs=(anywhere, pl.BlockSpec(memory_space=pltpu.VMEM)),
+            scratch_shapes=[
+                pltpu.VMEM((columns, columns), jnp.float32),
+                pltpu.VMEM((tiles, tile, columns), jnp.float32),
+                pltpu.VMEM((tiles, max(1, chips - 1), tile, columns), far.dtype),
+                pltpu.VMEM((tiles, len(pieces), tile, columns), pieces[0].dtype),
+                pltpu.VMEM((tiles, tile, columns), jnp.float32),
+                pltpu.SemaphoreType.DMA((tiles, chips + len(pieces))),
+                pltpu.SemaphoreType.DMA((tiles,)),
+            ],
         ),
-        compiler_params=params(),
+        compiler_params=params(VMEM_ALL),
         cost_estimate=COST,
         name="image",
     )(chip.reshape(1), base, far, *pieces)
 
 
-def factor_kernel(rounds, gram_ref, image_ref, basis_ref, factor_ref, inverse, work):
+def factor_kernel(rounds, gram_ref, image_ref, basis_ref, factor_ref, inverse, work, images, tile_sem, bases, out_sem):
     n = gram_ref.shape[0]
-    exact = lax.Precision.HIGHEST
-
-    @pl.when(pl.program_id(0) == 0)
+    tiles, tile, _ = images.shape
+    arrive = [
+        pltpu.make_async_copy(image_ref.at[pl.ds(t * tile, tile), :], images.at[t], tile_sem.at[t])
+        for t in range(tiles)
+    ]
+    for move in arrive:
+        move.start()
+
+    gram = gram_ref[...]
+    row = lax.broadcasted_iota(jnp.int32, (n, n), 0)
+    col = lax.broadcasted_iota(jnp.int32, (n, n), 1)
+    weight = jnp.where(row > col, 1.0, jnp.where(row == col, 0.5, 0.0))
+    one = jnp.where(row == col, 1.0, 0.0)
+    diagonal = jnp.where(row == col, gram, 0.0)
+    down = lax.rsqrt(jnp.sum(diagonal, axis=1, keepdims=True))
+    across = lax.rsqrt(jnp.sum(diagonal, axis=0, keepdims=True))
+    scaled = gram * down * across
+    scaled3 = split(scaled)
+    guess = one - weight * (scaled - one)
+    for _ in range(rounds):
+        guess3 = split(guess)
+        error = dot3(split(dot3(guess3, scaled3)), guess3, NT) - one
+        guess = guess - dot3(split(weight * error), guess3)
+    guess = jnp.where(row >= col, guess, 0.0) * across
+    inverse[...] = guess
+    factor_ref[...] = jnp.where(row <= col, dot3(split(guess), split(gram)), 0.0)
+    size = jnp.sum(error * error)
+
+    @pl.when(jnp.logical_not(size < 1e-6))
     def _():
-        gram = gram_ref[...]
-        row = lax.broadcasted_iota(jnp.int32, (n, n), 0)
-        col = lax.broadcasted_iota(jnp.int32, (n, n), 1)
-        weight = jnp.where(row > col, 1.0, jnp.where(row == col, 0.5, 0.0))
-        one = jnp.where(row == col, 1.0, 0.0)
-        diagonal = jnp.where(row == col, gram, 0.0)
-        down = lax.rsqrt(jnp.sum(diagonal, axis=1, keepdims=True))
-        across = lax.rsqrt(jnp.sum(diagonal, axis=0, keepdims=True))
-        scaled = gram * down * across
-        step = one - weight * (scaled - one)
-        guess = step
-        for turn in range(rounds):
-            if turn == rounds - 1:
-                error = dot(dot(guess, scaled, precision=exact), guess, NT, precision=exact) - one
-                step = weight * error
-                guess = guess - dot(step, guess, precision=exact)
-            else:
-                g3 = split(guess)
-                error = dot3(split(dot3(g3, split(scaled))), g3, NT) - one
-                guess = guess - dot3(split(weight * error), g3)
-        guess = jnp.where(row >= col, guess, 0.0)
-        inverse[...] = guess * across
-        factor_ref[...] = jnp.where(row <= col, dot(inverse[...], gram, precision=exact), 0.0)
-        size = jnp.sum(error * error)
-
-        @pl.when(jnp.logical_not(size < 1e-6))
-        def _():
-            work[...] = gram
-            inverse[...] = one
-            lane = lax.broadcasted_iota(jnp.int32, (1, n), 1)
-
-            def eliminate(j, carry):
-                line = work[pl.ds(j, 1), :]
-                pivot = jnp.sum(jnp.where(lane == j, line, 0.0), axis=1, keepdims=True)
-                scale = lax.rsqrt(pivot)
-                line = jnp.where(lane >= j, line * scale, 0.0)
-                other = inverse[pl.ds(j, 1), :] * scale
-                below = jnp.where(lane > j, line, 0.0)
-                work[...] -= dot(below, line, TN, exact)
-                inverse[...] -= dot(below, other, TN, exact)
-                inverse[pl.ds(j, 1), :] = other
-                factor_ref[pl.ds(j, 1), :] = line
-                return carry
-
-            lax.fori_loop(0, n, eliminate, 0)
-
-    basis_ref[...] = dot3(split(image_ref[...]), split(inverse[...]), NT)
-
-def factor_and_basis(gram, image, tile=256, rounds=3):
+        exact = lax.Precision.HIGHEST
+        work[...] = gram
+        inverse[...] = one
+        lane = lax.broadcasted_iota(jnp.int32, (1, n), 1)
+
+        def eliminate(j, carry):
+            line = work[pl.ds(j, 1), :]
+            pivot = jnp.sum(jnp.where(lane == j, line, 0.0), axis=1, keepdims=True)
+            scale = lax.rsqrt(pivot)
+            line = jnp.where(lane >= j, line * scale, 0.0)
+            other = inverse[pl.ds(j, 1), :] * scale
+            below = jnp.where(lane > j, line, 0.0)
+            work[...] -= dot(below, line, TN, exact)
+            inverse[...] -= dot(below, other, TN, exact)
+            inverse[pl.ds(j, 1), :] = other
+            factor_ref[pl.ds(j, 1), :] = line
+            return carry
+
+        lax.fori_loop(0, n, eliminate, 0)
+
+    inverse3 = split(inverse[...])
+    leave = []
+    for t in range(tiles):
+        arrive[t].wait()
+        bases[t] = dot3(split(images[t]), inverse3, NT)
+        leave.append(
+            pltpu.make_async_copy(bases.at[t], basis_ref.at[pl.ds(t * tile, tile), :], out_sem.at[t])
+        )
+        leave[-1].start()
+    for move in leave:
+        move.wait()
+
+
+def factor_and_basis(gram, image, rounds=3):
     height, n = image.shape
-    whole = pl.BlockSpec((n, n), lambda b: (0, 0))
-    tiles = pl.BlockSpec((tile, n), lambda b: (b, 0))
+    tile = math.gcd(height, 256)
+    tiles = height // tile
+    square, anywhere = pl.BlockSpec(memory_space=pltpu.VMEM), pl.BlockSpec(memory_space=pl.ANY)
+    held = pltpu.VMEM((tiles, tile, n), jnp.float32)
     return pl.pallas_call(
         functools.partial(factor_kernel, rounds),
-        out_shape=(jax.ShapeDtypeStruct((height, n), jnp.float32), jax.ShapeDtypeStruct((n, n), jnp.float32)),
-        grid=(height // tile,),
-        in_specs=[whole, tiles],
-        out_specs=(tiles, whole),
-        scratch_shapes=[pltpu.VMEM((n, n), jnp.float32)] * 2,
-        compiler_params=params(),
+        out_shape=(
+            jax.ShapeDtypeStruct((height, n), jnp.float32),
+            jax.ShapeDtypeStruct((n, n), jnp.float32),
+        ),
+        in_specs=[square, anywhere],
+        out_specs=(anywhere, square),
+        scratch_shapes=[pltpu.VMEM((n, n), jnp.float32)] * 2
+        + [held, pltpu.SemaphoreType.DMA((tiles,))] * 2,
+        compiler_params=params(VMEM_ALL),
+        cost_estimate=COST,
         name="factor",
     )(gram, image)
 
@@ -474,7 +536,7 @@
     slots = layers * most
     layer = lax.axis_index(LINE)
     shifts = sorted(range(layers), key=lambda shift: -min(shift, layers - shift))
-    cut = layers // 2
+    cut = 1
     groups = [group for group in (shifts[:cut], shifts[cut:-1], shifts[-1:]) if group]
     flat = col_blocks.reshape(requests)
     owners = flat // block_rows
@@ -514,10 +576,22 @@
         pack(off_blocks.reshape(requests, edge, edge), route + [counts], labels, sizes)
     )
 
-    line_omegas = []
-    for shift in shifts[:-1]:
-        steps = [(z, (z - shift) % layers) for z in range(layers)]
-        line_omegas.append(lax.ppermute(sketch, LINE, steps))
+    def planes_off(k):
+        return [(z, z - k) for z in range(k, layers)], [(z, z + k) for z in range(layers - k)]
+
+    down, up = planes_off(1)
+    above, below = lax.ppermute(sketch, LINE, down), lax.ppermute(sketch, LINE, up)
+    by_line = [(above, below)]
+    early_lines = [above, below]
+    if layers > 2:
+        by_line.append((lax.ppermute(above, LINE, down), lax.ppermute(below, LINE, up)))
+        both = lax.ppermute(sketch, LINE, sum(planes_off(3), []))
+        by_line.append((both, both))
+        early_lines.append(both)
+    line_omegas = [
+        (by_line[shift - 1][0], by_line[layers - shift - 1][1], (layer + shift < layers).astype(jnp.int32))
+        for shift in shifts[:-1]
+    ]
     chip, core = lax.axis_index(CHIPS), lax.axis_index(CORE)
     if [lax.axis_size(axis) for axis in PLANE] == [2, 2, 2]:
         swap = [(0, 1), (1, 0)]
@@ -537,8 +611,8 @@
     else:
         plane_omegas = [lax.all_gather(sketch, PLANE)]
         sources = jnp.arange(planes)
-    outgoing[1] = hold(outgoing[1], line_omegas[1:])
-    parts = [lax.all_to_all(part, PLANE, 0, 0, tiled=True) for part in outgoing]
+    outgoing[1] = hold(outgoing[1], early_lines)
+    parts = [lax.all_to_all(part, PLANE, 0, 0, tiled=True) for part in outgoing[:-1]]
     lines = sizes[0] * edge
     rows = parts[0][:, lines, :slots].astype(jnp.int32)
     cols = parts[0][:, lines + 1, :slots].astype(jnp.int32)
@@ -547,7 +621,6 @@
         part = sum(index * most >= end for end in ends)
         inside = index - (ends[part] - sizes[part]) // most
         shift = shifts[index]
-        kind = jnp.bfloat16 if shift else jnp.float32
         mirror = plane_sum(
             parts[part],
             plane_omegas,
@@ -558,69 +631,81 @@
             index * most,
             most,
             block_rows,
-            kind,
+            jnp.bfloat16,
             True,
             after,
         )
         steps = [(z, (z + shift) % layers) for z in range(layers)]
-        return lax.ppermute(mirror, LINE, steps) if shift else mirror, (mirror,)
-
-    pieces, latest = [], ()
-    for index in range(cut):
-        piece, latest = send_mirror(index, latest)
-        pieces.append(piece)
-
+        return lax.ppermute(mirror, LINE, steps), (mirror,)
+
+    first, latest = send_mirror(0, ())
+
+    home_rows = row_label.reshape(planes, slots)[:, -most:]
+    home_cols = col_label.reshape(planes, slots)[:, -most:]
     cores = lax.axis_size(CORE)
     chips = planes // cores
     away = (chip + jnp.arange(1, chips)) % chips
-    far = functools.partial(
-        far_sum,
-        parts=parts[:-1],
-        omegas=line_omegas,
-        rows=rows,
-        cols=cols,
-        most=most,
-        block_rows=block_rows,
-    )
-
-    def ask(chips_asked, after):
+    at_home = (home_rows, home_cols, outgoing[-1], sketch)
+    far = functools.partial(far_sum, rows=rows, cols=cols, most=most, block_rows=block_rows)
+    everything = dict(begin=0, parts=parts, omegas=line_omegas, home=at_home)
+    early = dict(begin=0, parts=parts[:1], omegas=line_omegas[:1], home=at_home)
+    late = dict(begin=sizes[0], parts=parts[1:], omegas=line_omegas[1:], home=None)
+
+    def ask(chips_asked, dtype, what, after):
         if cores == 1:
-            return None, after
+            return [], after
         count = chips_asked.shape[0]
         other = far(
-            chips_asked * cores + 1 - core, jnp.arange(count), count, dtype=jnp.float32, after=after
+            chips_asked * cores + 1 - core, jnp.arange(count), count, dtype=dtype, after=after, **what
         )
-        return lax.ppermute(other, CORE, [(0, 1), (1, 0)]), (other,)
-
-    other, latest = ask(away, latest)
-    late = []
-    for index in range(cut, layers - 1):
-        piece, latest = send_mirror(index, latest)
-        late.append(piece)
-    own_other, latest = ask(chip.reshape(1), latest)
-    sent = far(away * cores + core, away, chips, dtype=jnp.bfloat16, add=other, after=latest)
-    sent = hold(sent, parts[-1:])
-    received = lax.all_to_all(sent, CHIPS, 0, 0, tiled=True)
-    mirror, latest = send_mirror(layers - 1, (sent,))
+        return [lax.ppermute(other, CORE, [(0, 1), (1, 0)])], (other,)
+
+    other, latest = ask(away, jnp.float32, early, latest)
     home = plane_sum(
         outgoing[-1],
         plane_omegas,
         sources,
-        row_label.reshape(planes, slots),
-        col_label.reshape(planes, slots),
+        home_rows,
+        home_cols,
         0,
-        slots - most,
+        0,
         most,
         block_rows,
         jnp.float32,
         False,
         latest,
     )
+    begun = far(
+        away * cores + core,
+        jnp.arange(chips - 1),
+        chips - 1,
+        dtype=jnp.float32,
+        adds=other,
+        after=(home,),
+        **early,
+    )
+    other, latest = ask(away, jnp.bfloat16, late, (begun,))
+    second, latest = send_mirror(1, latest)
+    sent = far(
+        away * cores + core, away, chips, dtype=jnp.bfloat16, adds=[begun] + other, after=latest, **late
+    )
+    received = lax.all_to_all(sent, CHIPS, 0, 0, tiled=True)
+    pieces, latest = [second], (sent,)
+    for index in range(2, layers - 1):
+        piece, latest = send_mirror(index, latest)
+        pieces.append(piece)
+    other, _ = ask(chip.reshape(1), jnp.float32, everything, (sent,))
     own = far(
-        chip.reshape(1) * cores + core, jnp.arange(1), 1, dtype=jnp.float32, add=own_other, after=(home,)
-    )
-    base = base_sum(diag_blocks, sketch, [home, mirror, own.reshape(sketch.shape)] + pieces)
-    image, part = image_and_gram(base, chip, received, late, block_rows * edge * peers)
+        chip.reshape(1) * cores + core,
+        jnp.arange(1),
+        1,
+        dtype=jnp.float32,
+        adds=other,
+        after=latest,
+        **everything,
+    )
+    base = base_sum(diag_blocks, sketch, [home, own.reshape(sketch.shape), first])
+    image, part = image_and_gram(base, chip, received, pieces, block_rows * edge * peers)
     gram = sum_over_devices(part, peers)
     return factor_and_basis(gram, image)
 

time: 433 us -> 426 us (0.984)
  waiting for transfers between devices: 81.8 us -> 54.7 us
  Pallas kernels: 268 us -> 279 us
    all_to_all x3 -> x2, waiting for transfers between devices: 41.8 us -> 20 us  [on_device(): lax.all_to_all(part, PLANE, 0, 0, tiled=True)]
    pallas_call x4 -> x6, Pallas kernels: 25.1 us -> 41.9 us  [far_sum(): pl.pallas_call(functools.partial(far_kernel, most, begin, sizes, lines, l...]
    ppermute x8 -> x11, starting transfers between devices: 12.9 us -> 23.5 us  [the longest x1 5.56 us: on_device(): lax.ppermute(below, LINE, up)]
    pallas_call x5 -> x4, Pallas kernels: 32.4 us -> 25.8 us  [plane_sum(): pl.pallas_call(functools.partial(plane_kernel, inside, begin, most, count...]
    ppermute x2, waiting for transfers between devices: 4.7 us -> 0.01 us  [on_device(): by_x, by_y = (lax.ppermute(sketch, axis, swap) for axis in CHIPS)]
    ppermute x1, waiting for transfers between devices: 9.25 us -> 13.9 us  [on_device(): lax.ppermute(by_x[half:], CHIPS[1], swap)]
    all_to_all x3 -> x2, starting transfers between devices: 13.6 us -> 9.06 us  [on_device(): lax.all_to_all(part, PLANE, 0, 0, tiled=True)]
    ppermute x8 -> x11, waiting for transfers between devices: 10.3 us -> 12.2 us  [the longest x3 9.66 us: send_mirror(): return (lax.ppermute(mirror, LINE, steps), (mirror,))]
  transfers between devices with their start and end apart: 17 -> 19, of which waited for: 8 -> 7; matrix products, arithmetic and copies ran while one was open for 3% -> 3% of each run, Pallas kernels for 17% -> 20%
where the time goes in v6:
time: 426 us; the launch traced here: 425 us
  Pallas kernels  279 us (65%)
  waiting for transfers between devices  54.7 us (13%)
  starting transfers between devices  42.8 us (10%)
  blocking collectives  29 us (7%)
  local copies, waits for them, and re-layouts  12.1 us (3%)
  other arithmetic  6.47 us (2%)
    pallas_call x1, Pallas kernels, factor_and_basis(): pl.pallas_call(functools.partial(factor_kernel, rounds), out_shape=(jax.S...  190 us
    pallas_call x6, Pallas kernels, far_sum(): pl.pallas_call(functools.partial(far_kernel, most, begin, sizes, lines, l...  41.9 us
    pallas_call x4, Pallas kernels, plane_sum(): pl.pallas_call(functools.partial(plane_kernel, inside, begin, most, count...  25.8 us
    all_to_all x2, waiting for transfers between devices, on_device(): lax.all_to_all(part, PLANE, 0, 0, tiled=True)  20 us
    all_to_all x1, blocking collectives, sum_over_devices(): lax.all_to_all(part.reshape(peers, rows // peers, columns), ALL, 0, 0, ti...  16 us
    ppermute x1, waiting for transfers between devices, on_device(): lax.ppermute(by_x[half:], CHIPS[1], swap)  13.9 us
    all_to_all x1, blocking collectives, sum_over_devices(): return lax.all_to_all(mine, ALL, 0, 0, tiled=True).reshape(rows, columns)  13 us
    ppermute x3, waiting for transfers between devices, send_mirror(): return (lax.ppermute(mirror, LINE, steps), (mirror,))  9.66 us
  transfers between devices with their start and end apart: 19, of which 7 were waited for; matrix products, arithmetic and copies ran while one was open for 3% of the time, Pallas kernels for 20%

profile of v6, /device:TPU:0, one launch (start us, length us, event | category | flops | bytes accessed | tf_op | source)
XLA Modules:
  0.0 424.8 jit_solution(2025349893186715398)
XLA Ops:
  6.4 5.5 %collective-permute-start.7 = (bf16[2048,256]{1,0:T(8,128)(2,1)}, bf16[2048,256]{1,0:T(8,128)(2,1)}, u32[]{:S(2)}, u32[]{:S(2)}) collective-permute-start(bf16[2048,256]{1,0:T(8,128)(2,1)} %omega_ref.1), channel_id=1, source_target_pairs={{0,8},{8,16},{16,24},{1,9},{9,17},{17,25},{2,10},{10,18},{18,26},{... | collective-permute-start | bytes 3145736 | tf_op jit(solution)/shard_map/ppermute | solution.py:583
  17.8 7.1 %pack.1 = (bf16[8,1040,128]{2,1,0:T(8,128)(2,1)S(1)}, bf16[8,2048,128]{2,1,0:T(8,128)(2,1)}, bf16[8,1024,128]{2,1,0:T(8,128)(2,1)S(1)}) custom-call(s32[128]{0:T(128)S(1)} %get-tuple-element.14.entry_ref, s32[128]{0:T(128)S(1)} %get-tuple-element.13.plane_ref, s32[128]{0:T(128)S(1)} %get-tuple-element.12.slot_ref, s32[4]{0:T(128)S(1)} %convert_reduce_fusion.2.count_ref, ...), custom_call_target="tpu_custom_call" | custom-call | flops 999999995904 | bytes 99999997952 | tf_op jit(solution)/shard_map/pack/pallas_call | solution.py:72
  43.1 5.6 %collective-permute-start.8 = (bf16[2048,256]{1,0:T(8,128)(2,1)}, bf16[2048,256]{1,0:T(8,128)(2,1)}, u32[]{:S(2)}, u32[]{:S(2)}) collective-permute-start(bf16[2048,256]{1,0:T(8,128)(2,1)} %collective-permute-done.7.rest_1_.refs_11_.refs_14_), channel_id=1, source_target_pairs={{0,8},{8,16},{16,24},{1,9},{9,17},{17,25},{2,10},{10,18},{18,26},{... | collective-permute-start | bytes 3145736 | tf_op jit(solution)/shard_map/ppermute | solution.py:587
  49.7 13.9 %collective-permute-done.3.refs_4_ = bf16[1024,256]{1,0:T(8,128)(2,1)} collective-permute-done((bf16[1024,256]{1,0:T(8,128)(2,1)}, bf16[1024,256]{1,0:T(8,128)(2,1)}, u32[]{:S(2)}, u32[]{:S(2)}) %collective-permute-start.3) | collective-permute-done | bytes 524320 | tf_op jit(solution)/shard_map/ppermute | solution.py:602
  67.0 5.3 %all-to-all-done.rest_0_.refs_7_ = bf16[8,1040,128]{2,1,0:T(8,128)(2,1)} async-done(((bf16[8,1040,128]{2,1,0:T(8,128)(2,1)}), bf16[8,1040,128]{2,1,0:T(8,128)(2,1)}, u32[]{:S(2)}, u32[]{:S(2)}) %all-to-all-start) | async-done | bytes 2129952 | tf_op jit(solution)/shard_map/all_to_all | solution.py:615
  78.3 6.3 %mirror.3.refs_12_ = bf16[2048,256]{1,0:T(8,128)(2,1)} custom-call(s32[8]{0:T(128)} %pad_add_fusion.source_ref, s32[8,32]{1,0:T(8,128)} %bitcast.28, s32[8,32]{1,0:T(8,128)} %bitcast.17, bf16[8,1040,128]{2,1,0:T(8,128)(2,1)} %all-to-all-done.rest_0_.refs_7_, bf16[4,2048,256]{2,1,0:T(8,128)(2,1)} %bitcast.40, bf16[4,2048,256]{2,1,0:T(8,128)(2,1)} %bitcast.3.rest_2_), custom_call_target="tpu_custom_call" | custom-call | flops 999999995904 | bytes 99999997952 | tf_op jit(solution)/shard_map/mirror/pallas_call | solution.py:184
  85.2 6.1 %far.6.rest_3_ = f32[3,2048,256]{2,1,0:T(8,128)} custom-call(s32[3]{0:T(128)} %add_subtract_fusion.refs_0_, s32[3]{0:T(128)} %iota.37.refs_1_, s32[1]{0:T(128)} %bitcast.4.refs_2_, s32[8,32]{1,0:T(8,128)} %bitcast.29, s32[8,32]{1,0:T(8,128)} %bitcast.18, s32[8,8]{1,0:T(8,128)} %slice.26.refs_5_.row_ref, s32[8,8]{1,0:T(8,128)} %slice.27.refs_6_.col_ref, ...), custom_call_target="tpu_custom_call" | custom-call | flops 999999995904 | bytes 99999997952 | tf_op jit(solution)/shard_map/far/pallas_call | solution.py:304
  91.8 6.6 %home.1.refs_13_.rest_0_ = f32[2048,256]{1,0:T(8,128)} custom-call(s32[8]{0:T(128)} %pad_add_fusion.source_ref, s32[8,8]{1,0:T(8,128)} %slice.26.refs_5_.row_ref, s32[8,8]{1,0:T(8,128)} %slice.27.refs_6_.col_ref, bf16[8,1024,128]{2,1,0:T(8,128)(2,1)} %copy-done.4, bf16[4,2048,256]{2,1,0:T(8,128)(2,1)} %bitcast.41, bf16[4,2048,256]{2,1,0:T(8,128)(2,1)} %bitcast.3.rest_2_, ...), custom_call_target="tpu_custom_call" | custom-call | flops 999999995904 | bytes 99999997952 | tf_op jit(solution)/shard_map/home/pallas_call | solution.py:184
  102.5 7.8 %far.7.refs_12_ = f32[3,2048,256]{2,1,0:T(8,128)} custom-call(s32[3]{0:T(128)} %multiply_add_fusion.1.refs_0_, s32[3]{0:T(128)} %iota.38.refs_1_, s32[1]{0:T(128)} %bitcast.4.refs_2_, s32[8,32]{1,0:T(8,128)} %bitcast.30, s32[8,32]{1,0:T(8,128)} %bitcast.19, s32[8,8]{1,0:T(8,128)} %slice.26.refs_5_.row_ref, s32[8,8]{1,0:T(8,128)} %slice.27.refs_6_.col_ref, ...), custom_call_target="tpu_custom_call" | custom-call | flops 999999995904 | bytes 99999997952 | tf_op jit(solution)/shard_map/far/pallas_call | solution.py:304
  110.3 14.8 %all-to-all-done.1.refs_7_.rest_0_.refs_8_ = bf16[8,2048,128]{2,1,0:T(8,128)(2,1)} async-done(((bf16[8,2048,128]{2,1,0:T(8,128)(2,1)}), bf16[8,2048,128]{2,1,0:T(8,128)(2,1)}, u32[]{:S(2)}, u32[]{:S(2)}) %all-to-all-start.1) | async-done | bytes 4194336 | tf_op jit(solution)/shard_map/all_to_all | solution.py:615
  125.6 5.8 %far.8.rest_3_ = bf16[3,2048,256]{2,1,0:T(8,128)(2,1)} custom-call(s32[3]{0:T(128)} %add_subtract_fusion.refs_0_, s32[3]{0:T(128)} %iota.39.refs_1_, s32[2]{0:T(128)} %pad_add_fusion.2.refs_2_, s32[8,32]{1,0:T(8,128)} %bitcast.31, s32[8,32]{1,0:T(8,128)} %bitcast.20, s32[8,8]{1,0:T(8,128)} %bitcast.32, s32[8,8]{1,0:T(8,128)} %bitcast.21, ...), custom_call_target="tpu_custom_call" | custom-call | flops 999999995904 | bytes 99999997952 | tf_op jit(solution)/shard_map/far/pallas_call | solution.py:304
  131.5 6.4 %mirror.4.refs_14_ = bf16[2048,256]{1,0:T(8,128)(2,1)} custom-call(s32[8]{0:T(128)} %pad_add_fusion.source_ref, s32[8,32]{1,0:T(8,128)} %bitcast.33, s32[8,32]{1,0:T(8,128)} %bitcast.22, bf16[8,2048,128]{2,1,0:T(8,128)(2,1)} %all-to-all-done.1.refs_7_.rest_0_.refs_8_, bf16[4,2048,256]{2,1,0:T(8,128)(2,1)} %bitcast.42, bf16[4,2048,256]{2,1,0:T(8,128)(2,1)} %bitcast.3.rest_2_, ...), custom_call_target="tpu_custom_call" | custom-call | flops 999999995904 | bytes 99999997952 | tf_op jit(solution)/shard_map/mirror/pallas_call | solution.py:184
  138.0 9.2 %far.9.refs_17_.rest_3_ = bf16[4,2048,256]{2,1,0:T(8,128)(2,1)} custom-call(s32[3]{0:T(128)} %multiply_add_fusion.1.refs_0_, s32[3]{0:T(128)} %and_select_fusion.refs_1_, s32[2]{0:T(128)} %pad_add_fusion.2.refs_2_, s32[8,32]{1,0:T(8,128)} %bitcast.34, s32[8,32]{1,0:T(8,128)} %bitcast.23, s32[8,8]{1,0:T(8,128)} %bitcast.35, s32[8,8]{1,0:T(8,128)} %bitcast.24, ...), custom_call_target="tpu_custom_call" | custom-call | flops 999999995904 | bytes 99999997952 | tf_op jit(solution)/shard_map/far/pallas_call | solution.py:304
  147.2 4.9 %all-to-all-start.2 = ((bf16[4,2048,256]{2,1,0:T(8,128)(2,1)}), bf16[4,2048,256]{2,1,0:T(8,128)(2,1)}, u32[]{:S(2)}, u32[]{:S(2)}) async-start(bf16[4,2048,256]{2,1,0:T(8,128)(2,1)} %far.9.refs_17_.rest_3_), calls=%async_computation.2 | async-start | bytes 8388608 | tf_op jit(solution)/shard_map/all_to_all | solution.py:692
  152.1 6.0 %far.10 = f32[1,2048,256]{2,1,0:T(8,128)} custom-call(s32[1]{0:T(128)S(6)} %sub.74.refs_0_, s32[1]{0:T(128)} %constant.120.clone.1.refs_1_, s32[3]{0:T(128)} %pad_add_fusion.1.refs_2_, s32[8,32]{1,0:T(8,128)} %bitcast.36, s32[8,32]{1,0:T(8,128)} %bitcast.25, s32[8,8]{1,0:T(8,128)} %slice.26.refs_5_.row_ref, s32[8,8]{1,0:T(8,128)} %slice.27.refs_6_.col_ref, ...), custom_call_target="tpu_custom_call" | custom-call | flops 999999995904 | bytes 99999997952 | tf_op jit(solution)/shard_map/far/pallas_call | solution.py:304
  158.7 6.5 %mirror.5.refs_18_ = bf16[2048,256]{1,0:T(8,128)(2,1)} custom-call(s32[8]{0:T(128)} %pad_add_fusion.source_ref, s32[8,32]{1,0:T(8,128)} %bitcast.37, s32[8,32]{1,0:T(8,128)} %bitcast.26, bf16[8,2048,128]{2,1,0:T(8,128)(2,1)} %all-to-all-done.1.refs_7_.rest_0_.refs_8_, bf16[4,2048,256]{2,1,0:T(8,128)(2,1)} %bitcast.43, bf16[4,2048,256]{2,1,0:T(8,128)(2,1)} %bitcast.3.rest_2_, ...), custom_call_target="tpu_custom_call" | custom-call | flops 999999995904 | bytes 99999997952 | tf_op jit(solution)/shard_map/mirror/pallas_call | solution.py:184
  169.5 6.9 %far.11 = f32[1,2048,256]{2,1,0:T(8,128)} custom-call(s32[1]{0:T(128)S(6)} %add.313.refs_0_, s32[1]{0:T(128)} %constant.120.clone.1.refs_1_, s32[3]{0:T(128)} %pad_add_fusion.1.refs_2_, s32[8,32]{1,0:T(8,128)} %bitcast.38, s32[8,32]{1,0:T(8,128)} %bitcast.27, s32[8,8]{1,0:T(8,128)} %slice.26.refs_5_.row_ref, s32[8,8]{1,0:T(8,128)} %slice.27.refs_6_.col_ref, ...), custom_call_target="tpu_custom_call" | custom-call | flops 999999995904 | bytes 99999997952 | tf_op jit(solution)/shard_map/far/pallas_call | solution.py:304
  176.5 5.4 %base.1.base_ref = f32[2048,256]{1,0:T(8,128)S(1)} custom-call(bf16[16,128,128]{2,1,0:T(8,128)(2,1)S(1)} %copy-done.3, bf16[2048,256]{1,0:T(8,128)(2,1)S(1)} %copy-done.2, f32[2048,256]{1,0:T(8,128)} %home.1.refs_13_.rest_0_, f32[2048,256]{1,0:T(8,128)} %bitcast.44, bf16[2048,256]{1,0:T(8,128)(2,1)} %collective-permute-done.13.rest_2_), custom_call_target="tpu_custom_call" | custom-call | flops 999999995904 | bytes 99999997952 | tf_op jit(solution)/shard_map/base/pallas_call | solution.py:350
  183.2 9.7 %collective-permute-done.15.rest_1_ = bf16[2048,256]{1,0:T(8,128)(2,1)} collective-permute-done((bf16[2048,256]{1,0:T(8,128)(2,1)}, bf16[2048,256]{1,0:T(8,128)(2,1)}, u32[]{:S(2)}, u32[]{:S(2)}) %collective-permute-start.15) | collective-permute-done | bytes 1048608 | tf_op jit(solution)/shard_map/ppermute | solution.py:639
  192.8 7.6 %all-to-all-done.2.far_ref = bf16[4,2048,256]{2,1,0:T(8,128)(2,1)} async-done(((bf16[4,2048,256]{2,1,0:T(8,128)(2,1)}), bf16[4,2048,256]{2,1,0:T(8,128)(2,1)}, u32[]{:S(2)}, u32[]{:S(2)}) %all-to-all-start.2) | async-done | bytes 4194336 | tf_op jit(solution)/shard_map/all_to_all | solution.py:692
  200.4 5.6 %image.1 = (f32[2048,256]{1,0:T(8,128)}, f32[256,256]{1,0:T(8,128)}) custom-call(s32[1]{0:T(128)} %bitcast.chip_ref, f32[2048,256]{1,0:T(8,128)} %copy-done.5, bf16[4,2048,256]{2,1,0:T(8,128)(2,1)} %all-to-all-done.2.far_ref, bf16[2048,256]{1,0:T(8,128)(2,1)} %collective-permute-done.14.rest_0_, bf16[2048,256]{1,0:T(8,128)(2,1)} %collective-permute-done.15.rest_1_), custom_call_target="tpu_custom_call" | custom-call | flops 999999995904 | bytes 99999997952 | tf_op jit(solution)/shard_map/image/pallas_call | solution.py:407
  206.0 16.0 %all_to_all.25 = f32[32,8,256]{2,1,0:T(8,128)S(1)} all-to-all(f32[32,8,256]{2,1,0:T(8,128)} %bitcast.15), channel_id=1, replica_groups=mesh['z'=4,'x'=2,'y'=2,'c'=2] {'z','x','y','c'}, dimensions={0} | all-to-all | bytes 524288 | tf_op jit(solution)/shard_map/all_to_all | solution.py:523
  222.1 13.0 %all_to_all.26 = f32[32,8,256]{2,1,0:T(8,128)} all-to-all(f32[32,8,256]{2,1,0:T(8,128)S(1)} %broadcast_in_dim.86), channel_id=1, replica_groups=mesh['z'=4,'x'=2,'y'=2,'c'=2] {'z','x','y','c'}, dimensions={0} | all-to-all | bytes 524288 | tf_op jit(solution)/shard_map/all_to_all | solution.py:525
  235.1 189.5 %factor.1 = (f32[2048,256]{1,0:T(8,128)}, f32[256,256]{1,0:T(8,128)}) custom-call(f32[256,256]{1,0:T(8,128)} %bitcast.16, f32[2048,256]{1,0:T(8,128)} %get-tuple-element.11.image_ref), custom_call_target="tpu_custom_call" | custom-call | flops 999999995904 | bytes 99999997952 | tf_op jit(solution)/shard_map/factor/pallas_call | solution.py:505
  (83 shorter events, 52.3 us)
Async XLA Ops:
  0.6 32.0 %collective-permute-start = (bf16[2048,256]{1,0:T(8,128)(2,1)}, bf16[2048,256]{1,0:T(8,128)(2,1)}, u32[]{:S(2)}, u32[]{:S(2)}) collective-permute-start(bf16[2048,256]{1,0:T(8,128)(2,1)} %omega_ref.1), channel_id=1, source_target_pairs={{0,2},{2,0},{1,3},{3,1},{4,6},{6,4},{5,7},{7,5},{8,10},{10,8},{9,1... | collective-permute-start | bytes 3145736 | tf_op jit(solution)/shard_map/ppermute | solution.py:598
  3.7 31.4 %collective-permute-start.1 = (bf16[2048,256]{1,0:T(8,128)(2,1)}, bf16[2048,256]{1,0:T(8,128)(2,1)}, u32[]{:S(2)}, u32[]{:S(2)}) collective-permute-start(bf16[2048,256]{1,0:T(8,128)(2,1)} %omega_ref.1), channel_id=1, source_target_pairs={{0,4},{4,0},{1,5},{5,1},{2,6},{6,2},{3,7},{7,3},{8,12},{12,8},{9,1... | collective-permute-start | bytes 3145736 | tf_op jit(solution)/shard_map/ppermute | solution.py:598
  5.2 36.7 %collective-permute-start.5 = (bf16[2048,256]{1,0:T(8,128)(2,1)}, bf16[2048,256]{1,0:T(8,128)(2,1)}, u32[]{:S(2)}, u32[]{:S(2)}) collective-permute-start(bf16[2048,256]{1,0:T(8,128)(2,1)} %omega_ref.1), channel_id=1, source_target_pairs={{8,0},{16,8},{24,16},{9,1},{17,9},{25,17},{10,2},{18,10},{26,18},{... | collective-permute-start | bytes 3145736 | tf_op jit(solution)/shard_map/ppermute | solution.py:583
  6.4 36.7 %collective-permute-start.7 = (bf16[2048,256]{1,0:T(8,128)(2,1)}, bf16[2048,256]{1,0:T(8,128)(2,1)}, u32[]{:S(2)}, u32[]{:S(2)}) collective-permute-start(bf16[2048,256]{1,0:T(8,128)(2,1)} %omega_ref.1), channel_id=1, source_target_pairs={{0,8},{8,16},{16,24},{1,9},{9,17},{17,25},{2,10},{10,18},{18,26},{... | collective-permute-start | bytes 3145736 | tf_op jit(solution)/shard_map/ppermute | solution.py:583
  12.0 55.0 %collective-permute-start.9 = (bf16[2048,256]{1,0:T(8,128)(2,1)}, bf16[2048,256]{1,0:T(8,128)(2,1)}, u32[]{:S(2)}, u32[]{:S(2)}) collective-permute-start(bf16[2048,256]{1,0:T(8,128)(2,1)} %omega_ref.1), channel_id=1, source_target_pairs={{24,0},{0,24},{25,1},{1,25},{26,2},{2,26},{27,3},{3,27},{28,4},{4,... | collective-permute-start | bytes 3145736 | tf_op jit(solution)/shard_map/ppermute | solution.py:588
  17.8 9.8 %copy-start.7 = (s32[256]{0:T(256)S(1)}, s32[256]{0:T(256)}, u32[]{:S(2)}) copy-start(s32[256]{0:T(256)} %get-tuple-element.24) | copy-start | bytes 3076
  17.8 10.5 %copy-start.6 = (s32[256]{0:T(256)S(1)}, s32[256]{0:T(256)}, u32[]{:S(2)}) copy-start(s32[256]{0:T(256)} %get-tuple-element.32) | copy-start | bytes 3076
  34.6 15.1 %collective-permute-start.2 = (bf16[1024,256]{1,0:T(8,128)(2,1)}, bf16[1024,256]{1,0:T(8,128)(2,1)}, u32[]{:S(2)}, u32[]{:S(2)}) collective-permute-start(bf16[1024,256]{1,0:T(8,128)(2,1)} %slice.34), channel_id=1, source_target_pairs={{0,4},{4,0},{1,5},{5,1},{2,6},{6,2},{3,7},{7,3},{8,12},{12,8},{9,1... | collective-permute-start | bytes 1572872 | tf_op jit(solution)/shard_map/ppermute | solution.py:601
  37.0 26.6 %collective-permute-start.3 = (bf16[1024,256]{1,0:T(8,128)(2,1)}, bf16[1024,256]{1,0:T(8,128)(2,1)}, u32[]{:S(2)}, u32[]{:S(2)}) collective-permute-start(bf16[1024,256]{1,0:T(8,128)(2,1)} %slice.35), channel_id=1, source_target_pairs={{0,2},{2,0},{1,3},{3,1},{4,6},{6,4},{5,7},{7,5},{8,10},{10,8},{9,1... | collective-permute-start | bytes 1572872 | tf_op jit(solution)/shard_map/ppermute | solution.py:602
  37.3 26.3 %copy-start.1 = (bf16[2048,256]{1,0:T(8,128)(2,1)S(1)}, bf16[2048,256]{1,0:T(8,128)(2,1)}, u32[]{:S(2)}) copy-start(bf16[2048,256]{1,0:T(8,128)(2,1)} %omega_ref.1) | copy-start | bytes 3145732
  37.3 35.0 %all-to-all-start = ((bf16[8,1040,128]{2,1,0:T(8,128)(2,1)}), bf16[8,1040,128]{2,1,0:T(8,128)(2,1)}, u32[]{:S(2)}, u32[]{:S(2)}) async-start(bf16[8,1040,128]{2,1,0:T(8,128)(2,1)} %hold.2), calls=%async_computation | async-start | bytes 4259840 | tf_op jit(solution)/shard_map/all_to_all | solution.py:615
  41.8 42.8 %collective-permute-start.6 = (bf16[2048,256]{1,0:T(8,128)(2,1)}, bf16[2048,256]{1,0:T(8,128)(2,1)}, u32[]{:S(2)}, u32[]{:S(2)}) collective-permute-start(bf16[2048,256]{1,0:T(8,128)(2,1)} %collective-permute-done.5.rest_0_.refs_8_.refs_11_), channel_id=1, source_target_pairs={{8,0},{16,8},{24,16},{9,1},{17,9},{25,17},{10,2},{18,10},{26,18},{... | collective-permute-start | bytes 3145736 | tf_op jit(solution)/shard_map/ppermute | solution.py:587
  43.1 41.5 %collective-permute-start.8 = (bf16[2048,256]{1,0:T(8,128)(2,1)}, bf16[2048,256]{1,0:T(8,128)(2,1)}, u32[]{:S(2)}, u32[]{:S(2)}) collective-permute-start(bf16[2048,256]{1,0:T(8,128)(2,1)} %collective-permute-done.7.rest_1_.refs_11_.refs_14_), channel_id=1, source_target_pairs={{0,8},{8,16},{16,24},{1,9},{9,17},{17,25},{2,10},{10,18},{18,26},{... | collective-permute-start | bytes 3145736 | tf_op jit(solution)/shard_map/ppermute | solution.py:587
  66.9 11.4 %collective-permute-start.4 = (bf16[8192,256]{1,0:T(8,128)(2,1)}, bf16[8192,256]{1,0:T(8,128)(2,1)}, u32[]{:S(2)}, u32[]{:S(2)}) collective-permute-start(bf16[8192,256]{1,0:T(8,128)(2,1)} %join.1), channel_id=1, source_target_pairs={{0,1},{1,0},{2,3},{3,2},{4,5},{5,4},{6,7},{7,6},{8,9},{9,8},{10,11... | collective-permute-start | bytes 12582920 | tf_op jit(solution)/shard_map/ppermute | solution.py:607
  72.3 52.7 %all-to-all-start.1 = ((bf16[8,2048,128]{2,1,0:T(8,128)(2,1)}), bf16[8,2048,128]{2,1,0:T(8,128)(2,1)}, u32[]{:S(2)}, u32[]{:S(2)}) async-start(bf16[8,2048,128]{2,1,0:T(8,128)(2,1)} %hold.3), calls=%async_computation.1 | async-start | bytes 8388608 | tf_op jit(solution)/shard_map/all_to_all | solution.py:615
  91.4 10.6 %collective-permute-start.10 = (f32[3,2048,256]{2,1,0:T(8,128)}, f32[3,2048,256]{2,1,0:T(8,128)}, u32[]{:S(2)}, u32[]{:S(2)}) collective-permute-start(f32[3,2048,256]{2,1,0:T(8,128)} %far.6.rest_3_), channel_id=1, source_target_pairs={{0,1},{1,0},{2,3},{3,2},{4,5},{5,4},{6,7},{7,6},{8,9},{9,8},{10,11... | collective-permute-start | bytes 18874376 | tf_op jit(solution)/shard_map/ppermute | solution.py:661
  98.4 78.0 %collective-permute-start.13 = (bf16[2048,256]{1,0:T(8,128)(2,1)}, bf16[2048,256]{1,0:T(8,128)(2,1)}, u32[]{:S(2)}, u32[]{:S(2)}) collective-permute-start(bf16[2048,256]{1,0:T(8,128)(2,1)} %mirror.3.refs_12_), channel_id=1, source_target_pairs={{0,16},{8,24},{16,0},{24,8},{1,17},{9,25},{17,1},{25,9},{2,18},{10... | collective-permute-start | bytes 3145736 | tf_op jit(solution)/shard_map/ppermute | solution.py:639
  131.5 6.5 %collective-permute-start.11 = (bf16[3,2048,256]{2,1,0:T(8,128)(2,1)}, bf16[3,2048,256]{2,1,0:T(8,128)(2,1)}, u32[]{:S(2)}, u32[]{:S(2)}) collective-permute-start(bf16[3,2048,256]{2,1,0:T(8,128)(2,1)} %far.8.rest_3_), channel_id=1, source_target_pairs={{0,1},{1,0},{2,3},{3,2},{4,5},{5,4},{6,7},{7,6},{8,9},{9,8},{10,11... | collective-permute-start | bytes 9437192 | tf_op jit(solution)/shard_map/ppermute | solution.py:661
  137.9 45.3 %collective-permute-start.14 = (bf16[2048,256]{1,0:T(8,128)(2,1)}, bf16[2048,256]{1,0:T(8,128)(2,1)}, u32[]{:S(2)}, u32[]{:S(2)}) collective-permute-start(bf16[2048,256]{1,0:T(8,128)(2,1)} %mirror.4.refs_14_), channel_id=1, source_target_pairs={{0,8},{8,16},{16,24},{24,0},{1,9},{9,17},{17,25},{25,1},{2,10},{10... | collective-permute-start | bytes 3145736 | tf_op jit(solution)/shard_map/ppermute | solution.py:639
  147.2 53.2 %all-to-all-start.2 = ((bf16[4,2048,256]{2,1,0:T(8,128)(2,1)}), bf16[4,2048,256]{2,1,0:T(8,128)(2,1)}, u32[]{:S(2)}, u32[]{:S(2)}) async-start(bf16[4,2048,256]{2,1,0:T(8,128)(2,1)} %far.9.refs_17_.rest_3_), calls=%async_computation.2 | async-start | bytes 8388608 | tf_op jit(solution)/shard_map/all_to_all | solution.py:692
  158.1 11.4 %collective-permute-start.12 = (f32[1,2048,256]{2,1,0:T(8,128)}, f32[1,2048,256]{2,1,0:T(8,128)}, u32[]{:S(2)}, u32[]{:S(2)}) collective-permute-start(f32[1,2048,256]{2,1,0:T(8,128)} %far.10), channel_id=1, source_target_pairs={{0,1},{1,0},{2,3},{3,2},{4,5},{5,4},{6,7},{7,6},{8,9},{9,8},{10,11... | collective-permute-start | bytes 6291464 | tf_op jit(solution)/shard_map/ppermute | solution.py:661
  165.1 27.7 %collective-permute-start.15 = (bf16[2048,256]{1,0:T(8,128)(2,1)}, bf16[2048,256]{1,0:T(8,128)(2,1)}, u32[]{:S(2)}, u32[]{:S(2)}) collective-permute-start(bf16[2048,256]{1,0:T(8,128)(2,1)} %mirror.5.refs_18_), channel_id=1, source_target_pairs={{0,24},{8,0},{16,8},{24,16},{1,25},{9,1},{17,9},{25,17},{2,26},{10... | collective-permute-start | bytes 3145736 | tf_op jit(solution)/shard_map/ppermute | solution.py:639
  169.5 7.0 %copy-start.2 = (bf16[2048,256]{1,0:T(8,128)(2,1)S(1)}, bf16[2048,256]{1,0:T(8,128)(2,1)}, u32[]{:S(2)}) copy-start(bf16[2048,256]{1,0:T(8,128)(2,1)} %omega_ref.1) | copy-start | bytes 3145732
  169.5 7.0 %copy-start.3 = (bf16[16,128,128]{2,1,0:T(8,128)(2,1)S(1)}, bf16[16,128,128]{2,1,0:T(8,128)(2,1)}, u32[]{:S(2)}) copy-start(bf16[16,128,128]{2,1,0:T(8,128)(2,1)} %diag_ref.1) | copy-start | bytes 1572868
  (3 other events, 4.0 us)

commit v7 on v6

--- a/solution.py
+++ b/solution.py
@@ -79,7 +79,7 @@
             out_specs=[anywhere] * len(parts),
             scratch_shapes=[pltpu.SemaphoreType.DMA, pltpu.SemaphoreType.DMA],
         ),
-        compiler_params=params(),
+        compiler_params=params(VMEM_ALL),
         cost_estimate=COST,
         name="pack",
     )(*route, off, labels)
@@ -129,10 +129,44 @@
         in_specs=[anywhere] * len(arrays),
         out_specs=anywhere,
         scratch_shapes=[pltpu.VMEM(shape, arrays[0].dtype)] + [pltpu.SemaphoreType.DMA] * len(arrays),
-        compiler_params=params(),
+        compiler_params=params(VMEM_ALL),
         cost_estimate=COST,
         name="join",
     )(*arrays)
+
+
+def halves_kernel(y_ref, x_ref, first_ref, second_ref, held, sems):
+    half = first_ref.shape[0]
+    first = pltpu.make_async_copy(y_ref.at[pl.ds(0, half), :], held.at[0], sems.at[0])
+    second = pltpu.make_async_copy(x_ref.at[pl.ds(half, half), :], held.at[1], sems.at[1])
+    first.start()
+    second.start()
+    first.wait()
+    first = pltpu.make_async_copy(held.at[0], first_ref, sems.at[0])
+    first.start()
+    second.wait()
+    second = pltpu.make_async_copy(held.at[1], second_ref, sems.at[1])
+    second.start()
+    first.wait()
+    second.wait()
+
+
+def halves(by_y, by_x):
+    height, columns = by_y.shape
+    anywhere = pl.BlockSpec(memory_space=pl.ANY)
+    return pl.pallas_call(
+        halves_kernel,
+        out_shape=[jax.ShapeDtypeStruct((height // 2, columns), by_y.dtype)] * 2,
+        in_specs=[anywhere] * 2,
+        out_specs=[anywhere] * 2,
+        scratch_shapes=[
+            pltpu.VMEM((2, height // 2, columns), by_y.dtype),
+            pltpu.SemaphoreType.DMA((2,)),
+        ],
+        compiler_params=params(VMEM_ALL),
+        cost_estimate=COST,
+        name="halves",
+    )(by_y, by_x)
 
 
 def plane_kernel(inside, begin, most, counts, mirrored, source_ref, row_ref, col_ref, *rest):
@@ -354,7 +388,7 @@
         in_specs=[pl.BlockSpec((together, edge, edge), lambda b: (b, 0, 0)), rows]
         + [rows] * len(pieces),
         out_specs=rows,
-        compiler_params=params(),
+        compiler_params=params(VMEM_ALL),
         cost_estimate=COST,
         name="base",
     )(diag, sketch, *pieces)
@@ -588,35 +622,38 @@
         both = lax.ppermute(sketch, LINE, sum(planes_off(3), []))
         by_line.append((both, both))
         early_lines.append(both)
-    line_omegas = [
-        (by_line[shift - 1][0], by_line[layers - shift - 1][1], (layer + shift < layers).astype(jnp.int32))
-        for shift in shifts[:-1]
-    ]
     chip, core = lax.axis_index(CHIPS), lax.axis_index(CORE)
     if [lax.axis_size(axis) for axis in PLANE] == [2, 2, 2]:
         swap = [(0, 1), (1, 0)]
         by_x, by_y = (lax.ppermute(sketch, axis, swap) for axis in CHIPS)
-        half = sketch.shape[0] // 2
-        across = [
-            lax.ppermute(by_y[:half], CHIPS[0], swap),
-            lax.ppermute(by_x[half:], CHIPS[1], swap),
-        ]
+        upper, lower = halves(by_y, by_x)
+        across = [lax.ppermute(upper, CHIPS[0], swap), lax.ppermute(lower, CHIPS[1], swap)]
         outgoing[0] = hold(outgoing[0], [by_x, by_y])
         mine = join([sketch, by_y, by_x] + across)
         plane_omegas = [
             array.reshape((4,) + sketch.shape) for array in (mine, lax.ppermute(mine, CORE, swap))
         ]
-        near_chips = (chip ^ jnp.arange(4)) * 2
-        sources = jnp.concatenate([near_chips + core, near_chips + 1 - core])
+        relative = True
     else:
         plane_omegas = [lax.all_gather(sketch, PLANE)]
-        sources = jnp.arange(planes)
+        relative = False
     outgoing[1] = hold(outgoing[1], early_lines)
     parts = [lax.all_to_all(part, PLANE, 0, 0, tiled=True) for part in outgoing[:-1]]
     lines = sizes[0] * edge
     rows = parts[0][:, lines, :slots].astype(jnp.int32)
     cols = parts[0][:, lines + 1, :slots].astype(jnp.int32)
 
+    layer, chip, core, row_label, col_label, rows, cols = lax.optimization_barrier(
+        (layer, chip, core, row_label, col_label, rows, cols)
+    )
+    line_omegas = [
+        (by_line[shift - 1][0], by_line[layers - shift - 1][1], (layer + shift < layers).astype(jnp.int32))
+        for shift in shifts[:-1]
+    ]
+    sources = jnp.arange(planes)
+    if relative:
+        near_chips = (chip ^ jnp.arange(4)) * 2
+        sources = jnp.concatenate([near_chips + core, near_chips + 1 - core])
     def send_mirror(index, after):
         part = sum(index * most >= end for end in ends)
         inside = index - (ends[part] - sizes[part]) // most

time: 426 us -> 421 us (0.988)
  local copies, waits for them, and re-layouts: 12.1 us -> 4.26 us
    ppermute x2, waiting for transfers between devices: 14.9 us -> 2.26 us  [the longest x1 1.87 us: on_device(): lax.ppermute(upper, CHIPS[0], swap)]
    ppermute x1, waiting for transfers between devices: 0.01 us -> 8.44 us  [on_device(): both = lax.ppermute(sketch, LINE, sum(planes_off(3), []))]
  transfers between devices with their start and end apart: 19 -> 19, of which waited for: 7 -> 10; matrix products, arithmetic and copies ran while one was open for 3% -> 3% of each run, Pallas kernels for 20% -> 20%
where the time goes in v7:
time: 421 us; the launch traced here: 419 us
  Pallas kernels  280 us (67%)
  waiting for transfers between devices  52.4 us (12%)
  starting transfers between devices  45.7 us (11%)
  blocking collectives  28.1 us (7%)
  other arithmetic  8.12 us (2%)
  local copies, waits for them, and re-layouts  4.26 us (1%)
    pallas_call x1, Pallas kernels, factor_and_basis(): pl.pallas_call(functools.partial(factor_kernel, rounds), out_shape=(jax.S...  190 us
    pallas_call x6, Pallas kernels, far_sum(): pl.pallas_call(functools.partial(far_kernel, most, begin, sizes, lines, l...  41.7 us
    pallas_call x4, Pallas kernels, plane_sum(): pl.pallas_call(functools.partial(plane_kernel, inside, begin, most, count...  25.7 us
    all_to_all x2, waiting for transfers between devices, on_device(): lax.all_to_all(part, PLANE, 0, 0, tiled=True)  18.4 us
    all_to_all x1, blocking collectives, sum_over_devices(): lax.all_to_all(part.reshape(peers, rows // peers, columns), ALL, 0, 0, ti...  15.1 us
    ppermute x3, waiting for transfers between devices, send_mirror(): return (lax.ppermute(mirror, LINE, steps), (mirror,))  13.9 us
    all_to_all x1, blocking collectives, sum_over_devices(): return lax.all_to_all(mine, ALL, 0, 0, tiled=True).reshape(rows, columns)  13 us
    all_to_all x2, starting transfers between devices, on_device(): lax.all_to_all(part, PLANE, 0, 0, tiled=True)  8.94 us
  transfers between devices with their start and end apart: 19, of which 10 were waited for; matrix products, arithmetic and copies ran while one was open for 3% of the time, Pallas kernels for 20%

profile of v7, /device:TPU:0, one launch (start us, length us, event | category | flops | bytes accessed | tf_op | source)
XLA Modules:
  0.0 419.5 jit_solution(6114483331279196484)
XLA Ops:
  6.4 5.6 %collective-permute-start.7 = (bf16[2048,256]{1,0:T(8,128)(2,1)}, bf16[2048,256]{1,0:T(8,128)(2,1)}, u32[]{:S(2)}, u32[]{:S(2)}) collective-permute-start(bf16[2048,256]{1,0:T(8,128)(2,1)} %omega_ref.1), channel_id=1, source_target_pairs={{0,8},{8,16},{16,24},{1,9},{9,17},{17,25},{2,10},{10,18},{18,26},{... | collective-permute-start | bytes 3145736 | tf_op jit(solution)/shard_map/ppermute | solution.py:617
  19.4 5.0 %pack.1 = (bf16[8,1040,128]{2,1,0:T(8,128)(2,1)}, bf16[8,2048,128]{2,1,0:T(8,128)(2,1)}, bf16[8,1024,128]{2,1,0:T(8,128)(2,1)}) custom-call(s32[128]{0:T(128)} %get-tuple-element.32.entry_ref, s32[128]{0:T(128)} %get-tuple-element.31.plane_ref, s32[128]{0:T(128)} %get-tuple-element.30.slot_ref, s32[4]{0:T(128)} %convert_reduce_fusion.2.count_ref, ...), custom_call_target="tpu_custom_call" | custom-call | flops 999999995904 | bytes 99999997952 | tf_op jit(solution)/shard_map/pack/pallas_call | solution.py:72
  38.4 5.6 %collective-permute-start.8 = (bf16[2048,256]{1,0:T(8,128)(2,1)}, bf16[2048,256]{1,0:T(8,128)(2,1)}, u32[]{:S(2)}, u32[]{:S(2)}) collective-permute-start(bf16[2048,256]{1,0:T(8,128)(2,1)} %collective-permute-done.7.rest_1_.refs_11_.refs_14_), channel_id=1, source_target_pairs={{0,8},{8,16},{16,24},{1,9},{9,17},{17,25},{2,10},{10,18},{18,26},{... | collective-permute-start | bytes 3145736 | tf_op jit(solution)/shard_map/ppermute | solution.py:621
  49.6 8.4 %collective-permute-done.9.rest_2_.refs_9_.refs_10_.refs_12_.refs_13_ = bf16[2048,256]{1,0:T(8,128)(2,1)} collective-permute-done((bf16[2048,256]{1,0:T(8,128)(2,1)}, bf16[2048,256]{1,0:T(8,128)(2,1)}, u32[]{:S(2)}, u32[]{:S(2)}) %collective-permute-start.9) | collective-permute-done | bytes 1048608 | tf_op jit(solution)/shard_map/ppermute | solution.py:622
  58.0 8.7 %all-to-all-done.rest_0_.refs_7_ = bf16[8,1040,128]{2,1,0:T(8,128)(2,1)} async-done(((bf16[8,1040,128]{2,1,0:T(8,128)(2,1)}), bf16[8,1040,128]{2,1,0:T(8,128)(2,1)}, u32[]{:S(2)}, u32[]{:S(2)}) %all-to-all-start) | async-done | bytes 2129952 | tf_op jit(solution)/shard_map/all_to_all | solution.py:641
  66.7 4.6 %all-to-all-start.1 = ((bf16[8,2048,128]{2,1,0:T(8,128)(2,1)}), bf16[8,2048,128]{2,1,0:T(8,128)(2,1)}, u32[]{:S(2)}, u32[]{:S(2)}) async-start(bf16[8,2048,128]{2,1,0:T(8,128)(2,1)} %hold.3), calls=%async_computation.1 | async-start | bytes 8388608 | tf_op jit(solution)/shard_map/all_to_all | solution.py:641
  77.8 6.3 %mirror.3.refs_12_ = bf16[2048,256]{1,0:T(8,128)(2,1)} custom-call(s32[8]{0:T(128)} %pad_add_fusion.source_ref, s32[8,32]{1,0:T(8,128)} %bitcast.28, s32[8,32]{1,0:T(8,128)} %bitcast.17, bf16[8,1040,128]{2,1,0:T(8,128)(2,1)} %all-to-all-done.rest_0_.refs_7_, bf16[4,2048,256]{2,1,0:T(8,128)(2,1)} %bitcast.40, bf16[4,2048,256]{2,1,0:T(8,128)(2,1)} %bitcast.5.rest_2_), custom_call_target="tpu_custom_call" | custom-call | flops 999999995904 | bytes 99999997952 | tf_op jit(solution)/shard_map/mirror/pallas_call | solution.py:218
  84.8 6.1 %far.6.rest_3_ = f32[3,2048,256]{2,1,0:T(8,128)} custom-call(s32[3]{0:T(128)} %add_subtract_fusion.refs_0_, s32[3]{0:T(128)} %iota.37.refs_1_, s32[1]{0:T(128)} %bitcast.6.refs_2_, s32[8,32]{1,0:T(8,128)} %bitcast.29, s32[8,32]{1,0:T(8,128)} %bitcast.18, s32[8,8]{1,0:T(8,128)} %slice.22.refs_5_.row_ref, s32[8,8]{1,0:T(8,128)} %slice.23.refs_6_.col_ref, ...), custom_call_target="tpu_custom_call" | custom-call | flops 999999995904 | bytes 99999997952 | tf_op jit(solution)/shard_map/far/pallas_call | solution.py:338
  91.3 6.6 %home.1.refs_13_.rest_0_ = f32[2048,256]{1,0:T(8,128)} custom-call(s32[8]{0:T(128)} %pad_add_fusion.source_ref, s32[8,8]{1,0:T(8,128)} %slice.22.refs_5_.row_ref, s32[8,8]{1,0:T(8,128)} %slice.23.refs_6_.col_ref, bf16[8,1024,128]{2,1,0:T(8,128)(2,1)} %get-tuple-element.21.refs_10_.rest_0_.refs_15_, bf16[4,2048,256]{2,1,0:T(8,128)(2,1)} %bitcast.41, ...), custom_call_target="tpu_custom_call" | custom-call | flops 999999995904 | bytes 99999997952 | tf_op jit(solution)/shard_map/home/pallas_call | solution.py:218
  102.0 7.8 %far.7.refs_12_ = f32[3,2048,256]{2,1,0:T(8,128)} custom-call(s32[3]{0:T(128)} %multiply_add_fusion.1.refs_0_, s32[3]{0:T(128)} %iota.38.refs_1_, s32[1]{0:T(128)} %bitcast.6.refs_2_, s32[8,32]{1,0:T(8,128)} %bitcast.30, s32[8,32]{1,0:T(8,128)} %bitcast.19, s32[8,8]{1,0:T(8,128)} %slice.22.refs_5_.row_ref, s32[8,8]{1,0:T(8,128)} %slice.23.refs_6_.col_ref, ...), custom_call_target="tpu_custom_call" | custom-call | flops 999999995904 | bytes 99999997952 | tf_op jit(solution)/shard_map/far/pallas_call | solution.py:338
  109.8 9.7 %all-to-all-done.1.refs_7_.rest_0_.refs_8_ = bf16[8,2048,128]{2,1,0:T(8,128)(2,1)} async-done(((bf16[8,2048,128]{2,1,0:T(8,128)(2,1)}), bf16[8,2048,128]{2,1,0:T(8,128)(2,1)}, u32[]{:S(2)}, u32[]{:S(2)}) %all-to-all-start.1) | async-done | bytes 4194336 | tf_op jit(solution)/shard_map/all_to_all | solution.py:641
  120.1 5.8 %far.8.rest_3_ = bf16[3,2048,256]{2,1,0:T(8,128)(2,1)} custom-call(s32[3]{0:T(128)} %add_subtract_fusion.refs_0_, s32[3]{0:T(128)} %iota.39.refs_1_, s32[2]{0:T(128)} %pad_add_fusion.2.refs_2_, s32[8,32]{1,0:T(8,128)} %bitcast.31, s32[8,32]{1,0:T(8,128)} %bitcast.20, s32[8,8]{1,0:T(8,128)} %bitcast.32, s32[8,8]{1,0:T(8,128)} %bitcast.21, ...), custom_call_target="tpu_custom_call" | custom-call | flops 999999995904 | bytes 99999997952 | tf_op jit(solution)/shard_map/far/pallas_call | solution.py:338
  126.0 6.4 %mirror.4.refs_14_ = bf16[2048,256]{1,0:T(8,128)(2,1)} custom-call(s32[8]{0:T(128)} %pad_add_fusion.source_ref, s32[8,32]{1,0:T(8,128)} %bitcast.33, s32[8,32]{1,0:T(8,128)} %bitcast.22, bf16[8,2048,128]{2,1,0:T(8,128)(2,1)} %all-to-all-done.1.refs_7_.rest_0_.refs_8_, bf16[4,2048,256]{2,1,0:T(8,128)(2,1)} %bitcast.42, bf16[4,2048,256]{2,1,0:T(8,128)(2,1)} %bitcast.5.rest_2_, ...), custom_call_target="tpu_custom_call" | custom-call | flops 999999995904 | bytes 99999997952 | tf_op jit(solution)/shard_map/mirror/pallas_call | solution.py:218
  133.9 9.2 %far.9.refs_17_.rest_3_ = bf16[4,2048,256]{2,1,0:T(8,128)(2,1)} custom-call(s32[3]{0:T(128)} %multiply_add_fusion.1.refs_0_, s32[3]{0:T(128)} %and_select_fusion.refs_1_, s32[2]{0:T(128)} %pad_add_fusion.2.refs_2_, s32[8,32]{1,0:T(8,128)} %bitcast.34, s32[8,32]{1,0:T(8,128)} %bitcast.23, s32[8,8]{1,0:T(8,128)} %bitcast.35, s32[8,8]{1,0:T(8,128)} %bitcast.24, ...), custom_call_target="tpu_custom_call" | custom-call | flops 999999995904 | bytes 99999997952 | tf_op jit(solution)/shard_map/far/pallas_call | solution.py:338
  143.1 4.8 %all-to-all-start.2 = ((bf16[4,2048,256]{2,1,0:T(8,128)(2,1)}), bf16[4,2048,256]{2,1,0:T(8,128)(2,1)}, u32[]{:S(2)}, u32[]{:S(2)}) async-start(bf16[4,2048,256]{2,1,0:T(8,128)(2,1)} %far.9.refs_17_.rest_3_), calls=%async_computation.2 | async-start | bytes 8388608 | tf_op jit(solution)/shard_map/all_to_all | solution.py:729
  148.0 6.0 %far.10 = f32[1,2048,256]{2,1,0:T(8,128)} custom-call(s32[1]{0:T(128)S(6)} %sub.74.refs_0_, s32[1]{0:T(128)} %constant.120.clone.1.refs_1_, s32[3]{0:T(128)} %pad_add_fusion.1.refs_2_, s32[8,32]{1,0:T(8,128)} %bitcast.36, s32[8,32]{1,0:T(8,128)} %bitcast.25, s32[8,8]{1,0:T(8,128)} %slice.22.refs_5_.row_ref, s32[8,8]{1,0:T(8,128)} %slice.23.refs_6_.col_ref, ...), custom_call_target="tpu_custom_call" | custom-call | flops 999999995904 | bytes 99999997952 | tf_op jit(solution)/shard_map/far/pallas_call | solution.py:338
  154.3 6.4 %mirror.5.refs_18_ = bf16[2048,256]{1,0:T(8,128)(2,1)} custom-call(s32[8]{0:T(128)} %pad_add_fusion.source_ref, s32[8,32]{1,0:T(8,128)} %bitcast.37, s32[8,32]{1,0:T(8,128)} %bitcast.26, bf16[8,2048,128]{2,1,0:T(8,128)(2,1)} %all-to-all-done.1.refs_7_.rest_0_.refs_8_, bf16[4,2048,256]{2,1,0:T(8,128)(2,1)} %bitcast.43, bf16[4,2048,256]{2,1,0:T(8,128)(2,1)} %bitcast.5.rest_2_, ...), custom_call_target="tpu_custom_call" | custom-call | flops 999999995904 | bytes 99999997952 | tf_op jit(solution)/shard_map/mirror/pallas_call | solution.py:218
  164.0 6.8 %far.11 = f32[1,2048,256]{2,1,0:T(8,128)} custom-call(s32[1]{0:T(128)S(6)} %add.303.refs_0_, s32[1]{0:T(128)} %constant.120.clone.1.refs_1_, s32[3]{0:T(128)} %pad_add_fusion.1.refs_2_, s32[8,32]{1,0:T(8,128)} %bitcast.38, s32[8,32]{1,0:T(8,128)} %bitcast.27, s32[8,8]{1,0:T(8,128)} %slice.22.refs_5_.row_ref, s32[8,8]{1,0:T(8,128)} %slice.23.refs_6_.col_ref, ...), custom_call_target="tpu_custom_call" | custom-call | flops 999999995904 | bytes 99999997952 | tf_op jit(solution)/shard_map/far/pallas_call | solution.py:338
  170.8 7.1 %base.1.base_ref = f32[2048,256]{1,0:T(8,128)} custom-call(bf16[16,128,128]{2,1,0:T(8,128)(2,1)} %diag_ref.1, bf16[2048,256]{1,0:T(8,128)(2,1)} %omega_ref.1, f32[2048,256]{1,0:T(8,128)} %home.1.refs_13_.rest_0_, f32[2048,256]{1,0:T(8,128)} %bitcast.44, bf16[2048,256]{1,0:T(8,128)(2,1)} %collective-permute-done.13.rest_2_), custom_call_target="tpu_custom_call" | custom-call | flops 999999995904 | bytes 99999997952 | tf_op jit(solution)/shard_map/base/pallas_call | solution.py:384
  177.9 13.9 %collective-permute-done.15.rest_1_ = bf16[2048,256]{1,0:T(8,128)(2,1)} collective-permute-done((bf16[2048,256]{1,0:T(8,128)(2,1)}, bf16[2048,256]{1,0:T(8,128)(2,1)}, u32[]{:S(2)}, u32[]{:S(2)}) %collective-permute-start.15) | collective-permute-done | bytes 1048608 | tf_op jit(solution)/shard_map/ppermute | solution.py:676
  196.1 5.6 %image.1 = (f32[2048,256]{1,0:T(8,128)}, f32[256,256]{1,0:T(8,128)}) custom-call(s32[1]{0:T(128)} %bitcast.3.chip_ref, f32[2048,256]{1,0:T(8,128)} %base.1.base_ref, bf16[4,2048,256]{2,1,0:T(8,128)(2,1)} %all-to-all-done.2.far_ref, bf16[2048,256]{1,0:T(8,128)(2,1)} %collective-permute-done.14.rest_0_, bf16[2048,256]{1,0:T(8,128)(2,1)} %collective-permute-done.15.rest_1_), custom_call_target="tpu_custom_call" | custom-call | flops 999999995904 | bytes 99999997952 | tf_op jit(solution)/shard_map/image/pallas_call | solution.py:441
  201.6 15.1 %all_to_all.25 = f32[32,8,256]{2,1,0:T(8,128)S(1)} all-to-all(f32[32,8,256]{2,1,0:T(8,128)} %bitcast.15), channel_id=1, replica_groups=mesh['z'=4,'x'=2,'y'=2,'c'=2] {'z','x','y','c'}, dimensions={0} | all-to-all | bytes 524288 | tf_op jit(solution)/shard_map/all_to_all | solution.py:557
  216.8 13.0 %all_to_all.26 = f32[32,8,256]{2,1,0:T(8,128)} all-to-all(f32[32,8,256]{2,1,0:T(8,128)S(1)} %broadcast_in_dim.86), channel_id=1, replica_groups=mesh['z'=4,'x'=2,'y'=2,'c'=2] {'z','x','y','c'}, dimensions={0} | all-to-all | bytes 524288 | tf_op jit(solution)/shard_map/all_to_all | solution.py:559
  229.8 189.5 %factor.1 = (f32[2048,256]{1,0:T(8,128)}, f32[256,256]{1,0:T(8,128)}) custom-call(f32[256,256]{1,0:T(8,128)} %bitcast.16, f32[2048,256]{1,0:T(8,128)} %get-tuple-element.29.image_ref), custom_call_target="tpu_custom_call" | custom-call | flops 999999995904 | bytes 99999997952 | tf_op jit(solution)/shard_map/factor/pallas_call | solution.py:539
  (71 shorter events, 54.3 us)
Async XLA Ops:
  0.6 26.5 %collective-permute-start = (bf16[2048,256]{1,0:T(8,128)(2,1)}, bf16[2048,256]{1,0:T(8,128)(2,1)}, u32[]{:S(2)}, u32[]{:S(2)}) collective-permute-start(bf16[2048,256]{1,0:T(8,128)(2,1)} %omega_ref.1), channel_id=1, source_target_pairs={{0,4},{4,0},{1,5},{5,1},{2,6},{6,2},{3,7},{7,3},{8,12},{12,8},{9,1... | collective-permute-start | bytes 3145736 | tf_op jit(solution)/shard_map/ppermute | solution.py:628
  3.6 24.9 %collective-permute-start.1 = (bf16[2048,256]{1,0:T(8,128)(2,1)}, bf16[2048,256]{1,0:T(8,128)(2,1)}, u32[]{:S(2)}, u32[]{:S(2)}) collective-permute-start(bf16[2048,256]{1,0:T(8,128)(2,1)} %omega_ref.1), channel_id=1, source_target_pairs={{0,2},{2,0},{1,3},{3,1},{4,6},{6,4},{5,7},{7,5},{8,10},{10,8},{9,1... | collective-permute-start | bytes 3145736 | tf_op jit(solution)/shard_map/ppermute | solution.py:628
  5.2 32.0 %collective-permute-start.5 = (bf16[2048,256]{1,0:T(8,128)(2,1)}, bf16[2048,256]{1,0:T(8,128)(2,1)}, u32[]{:S(2)}, u32[]{:S(2)}) collective-permute-start(bf16[2048,256]{1,0:T(8,128)(2,1)} %omega_ref.1), channel_id=1, source_target_pairs={{8,0},{16,8},{24,16},{9,1},{17,9},{25,17},{10,2},{18,10},{26,18},{... | collective-permute-start | bytes 3145736 | tf_op jit(solution)/shard_map/ppermute | solution.py:617
  6.4 32.0 %collective-permute-start.7 = (bf16[2048,256]{1,0:T(8,128)(2,1)}, bf16[2048,256]{1,0:T(8,128)(2,1)}, u32[]{:S(2)}, u32[]{:S(2)}) collective-permute-start(bf16[2048,256]{1,0:T(8,128)(2,1)} %omega_ref.1), channel_id=1, source_target_pairs={{0,8},{8,16},{16,24},{1,9},{9,17},{17,25},{2,10},{10,18},{18,26},{... | collective-permute-start | bytes 3145736 | tf_op jit(solution)/shard_map/ppermute | solution.py:617
  12.0 46.0 %collective-permute-start.9 = (bf16[2048,256]{1,0:T(8,128)(2,1)}, bf16[2048,256]{1,0:T(8,128)(2,1)}, u32[]{:S(2)}, u32[]{:S(2)}) collective-permute-start(bf16[2048,256]{1,0:T(8,128)(2,1)} %omega_ref.1), channel_id=1, source_target_pairs={{24,0},{0,24},{25,1},{1,25},{26,2},{2,26},{27,3},{3,27},{28,4},{4,... | collective-permute-start | bytes 3145736 | tf_op jit(solution)/shard_map/ppermute | solution.py:622
  30.6 15.2 %collective-permute-start.2 = (bf16[1024,256]{1,0:T(8,128)(2,1)}, bf16[1024,256]{1,0:T(8,128)(2,1)}, u32[]{:S(2)}, u32[]{:S(2)}) collective-permute-start(bf16[1024,256]{1,0:T(8,128)(2,1)} %get-tuple-element.22), channel_id=1, source_target_pairs={{0,4},{4,0},{1,5},{5,1},{2,6},{6,2},{3,7},{7,3},{8,12},{12,8},{9,1... | collective-permute-start | bytes 1572872 | tf_op jit(solution)/shard_map/ppermute | solution.py:630
  31.1 15.2 %collective-permute-start.3 = (bf16[1024,256]{1,0:T(8,128)(2,1)}, bf16[1024,256]{1,0:T(8,128)(2,1)}, u32[]{:S(2)}, u32[]{:S(2)}) collective-permute-start(bf16[1024,256]{1,0:T(8,128)(2,1)} %get-tuple-element.23), channel_id=1, source_target_pairs={{0,2},{2,0},{1,3},{3,1},{4,6},{6,4},{5,7},{7,5},{8,10},{10,8},{9,1... | collective-permute-start | bytes 1572872 | tf_op jit(solution)/shard_map/ppermute | solution.py:630
  32.8 34.0 %all-to-all-start = ((bf16[8,1040,128]{2,1,0:T(8,128)(2,1)}), bf16[8,1040,128]{2,1,0:T(8,128)(2,1)}, u32[]{:S(2)}, u32[]{:S(2)}) async-start(bf16[8,1040,128]{2,1,0:T(8,128)(2,1)} %hold.2), calls=%async_computation | async-start | bytes 4259840 | tf_op jit(solution)/shard_map/all_to_all | solution.py:641
  37.1 47.0 %collective-permute-start.6 = (bf16[2048,256]{1,0:T(8,128)(2,1)}, bf16[2048,256]{1,0:T(8,128)(2,1)}, u32[]{:S(2)}, u32[]{:S(2)}) collective-permute-start(bf16[2048,256]{1,0:T(8,128)(2,1)} %collective-permute-done.5.rest_0_.refs_8_.refs_11_), channel_id=1, source_target_pairs={{8,0},{16,8},{24,16},{9,1},{17,9},{25,17},{10,2},{18,10},{26,18},{... | collective-permute-start | bytes 3145736 | tf_op jit(solution)/shard_map/ppermute | solution.py:621
  38.4 45.7 %collective-permute-start.8 = (bf16[2048,256]{1,0:T(8,128)(2,1)}, bf16[2048,256]{1,0:T(8,128)(2,1)}, u32[]{:S(2)}, u32[]{:S(2)}) collective-permute-start(bf16[2048,256]{1,0:T(8,128)(2,1)} %collective-permute-done.7.rest_1_.refs_11_.refs_14_), channel_id=1, source_target_pairs={{0,8},{8,16},{16,24},{1,9},{9,17},{17,25},{2,10},{10,18},{18,26},{... | collective-permute-start | bytes 3145736 | tf_op jit(solution)/shard_map/ppermute | solution.py:621
  49.5 28.3 %collective-permute-start.4 = (bf16[8192,256]{1,0:T(8,128)(2,1)}, bf16[8192,256]{1,0:T(8,128)(2,1)}, u32[]{:S(2)}, u32[]{:S(2)}) collective-permute-start(bf16[8192,256]{1,0:T(8,128)(2,1)} %join.1), channel_id=1, source_target_pairs={{0,1},{1,0},{2,3},{3,2},{4,5},{5,4},{6,7},{7,6},{8,9},{9,8},{10,11... | collective-permute-start | bytes 12582920 | tf_op jit(solution)/shard_map/ppermute | solution.py:634
  58.0 14.7 %copy-start.1 = (s32[256]{0:T(256)S(1)}, s32[256]{0:T(256)}, u32[]{:S(2)}) copy-start(s32[256]{0:T(256)} %get-tuple-element.19) | copy-start | bytes 3076
  58.0 15.5 %copy-start = (s32[256]{0:T(256)S(1)}, s32[256]{0:T(256)}, u32[]{:S(2)}) copy-start(s32[256]{0:T(256)} %get-tuple-element.20) | copy-start | bytes 3076
  66.7 52.8 %all-to-all-start.1 = ((bf16[8,2048,128]{2,1,0:T(8,128)(2,1)}), bf16[8,2048,128]{2,1,0:T(8,128)(2,1)}, u32[]{:S(2)}, u32[]{:S(2)}) async-start(bf16[8,2048,128]{2,1,0:T(8,128)(2,1)} %hold.3), calls=%async_computation.1 | async-start | bytes 8388608 | tf_op jit(solution)/shard_map/all_to_all | solution.py:641
  90.9 10.6 %collective-permute-start.10 = (f32[3,2048,256]{2,1,0:T(8,128)}, f32[3,2048,256]{2,1,0:T(8,128)}, u32[]{:S(2)}, u32[]{:S(2)}) collective-permute-start(f32[3,2048,256]{2,1,0:T(8,128)} %far.6.rest_3_), channel_id=1, source_target_pairs={{0,1},{1,0},{2,3},{3,2},{4,5},{5,4},{6,7},{7,6},{8,9},{9,8},{10,11... | collective-permute-start | bytes 18874376 | tf_op jit(solution)/shard_map/ppermute | solution.py:698
  97.9 72.8 %collective-permute-start.13 = (bf16[2048,256]{1,0:T(8,128)(2,1)}, bf16[2048,256]{1,0:T(8,128)(2,1)}, u32[]{:S(2)}, u32[]{:S(2)}) collective-permute-start(bf16[2048,256]{1,0:T(8,128)(2,1)} %mirror.3.refs_12_), channel_id=1, source_target_pairs={{0,16},{8,24},{16,0},{24,8},{1,17},{9,25},{17,1},{25,9},{2,18},{10... | collective-permute-start | bytes 3145736 | tf_op jit(solution)/shard_map/ppermute | solution.py:676
  125.9 8.0 %collective-permute-start.11 = (bf16[3,2048,256]{2,1,0:T(8,128)(2,1)}, bf16[3,2048,256]{2,1,0:T(8,128)(2,1)}, u32[]{:S(2)}, u32[]{:S(2)}) collective-permute-start(bf16[3,2048,256]{2,1,0:T(8,128)(2,1)} %far.8.rest_3_), channel_id=1, source_target_pairs={{0,1},{1,0},{2,3},{3,2},{4,5},{5,4},{6,7},{7,6},{8,9},{9,8},{10,11... | collective-permute-start | bytes 9437192 | tf_op jit(solution)/shard_map/ppermute | solution.py:698
  132.3 45.6 %collective-permute-start.14 = (bf16[2048,256]{1,0:T(8,128)(2,1)}, bf16[2048,256]{1,0:T(8,128)(2,1)}, u32[]{:S(2)}, u32[]{:S(2)}) collective-permute-start(bf16[2048,256]{1,0:T(8,128)(2,1)} %mirror.4.refs_14_), channel_id=1, source_target_pairs={{0,8},{8,16},{16,24},{24,0},{1,9},{9,17},{17,25},{25,1},{2,10},{10... | collective-permute-start | bytes 3145736 | tf_op jit(solution)/shard_map/ppermute | solution.py:676
  143.1 52.9 %all-to-all-start.2 = ((bf16[4,2048,256]{2,1,0:T(8,128)(2,1)}), bf16[4,2048,256]{2,1,0:T(8,128)(2,1)}, u32[]{:S(2)}, u32[]{:S(2)}) async-start(bf16[4,2048,256]{2,1,0:T(8,128)(2,1)} %far.9.refs_17_.rest_3_), calls=%async_computation.2 | async-start | bytes 8388608 | tf_op jit(solution)/shard_map/all_to_all | solution.py:729
  154.0 10.0 %collective-permute-start.12 = (f32[1,2048,256]{2,1,0:T(8,128)}, f32[1,2048,256]{2,1,0:T(8,128)}, u32[]{:S(2)}, u32[]{:S(2)}) collective-permute-start(f32[1,2048,256]{2,1,0:T(8,128)} %far.10), channel_id=1, source_target_pairs={{0,1},{1,0},{2,3},{3,2},{4,5},{5,4},{6,7},{7,6},{8,9},{9,8},{10,11... | collective-permute-start | bytes 6291464 | tf_op jit(solution)/shard_map/ppermute | solution.py:698
  160.7 31.1 %collective-permute-start.15 = (bf16[2048,256]{1,0:T(8,128)(2,1)}, bf16[2048,256]{1,0:T(8,128)(2,1)}, u32[]{:S(2)}, u32[]{:S(2)}) collective-permute-start(bf16[2048,256]{1,0:T(8,128)(2,1)} %mirror.5.refs_18_), channel_id=1, source_target_pairs={{0,24},{8,0},{16,8},{24,16},{1,25},{9,1},{17,9},{25,17},{2,26},{10... | collective-permute-start | bytes 3145736 | tf_op jit(solution)/shard_map/ppermute | solution.py:676

commit v8 on v7

--- a/solution.py
+++ b/solution.py
@@ -495,7 +495,7 @@
     factor_ref[...] = jnp.where(row <= col, dot3(split(guess), split(gram)), 0.0)
     size = jnp.sum(error * error)
 
-    @pl.when(jnp.logical_not(size < 1e-6))
+    @pl.when(jnp.logical_not(size < 1e-4))
     def _():
         exact = lax.Precision.HIGHEST
         work[...] = gram
@@ -530,7 +530,7 @@
         move.wait()
 
 
-def factor_and_basis(gram, image, rounds=3):
+def factor_and_basis(gram, image, rounds=2):
     height, n = image.shape
     tile = math.gcd(height, 256)
     tiles = height // tile
@@ -552,11 +552,17 @@
     )(gram, image)
 
 
-def sum_over_devices(part, peers):
+def sum_over_devices(part):
     rows, columns = part.shape
-    pieces = lax.all_to_all(part.reshape(peers, rows // peers, columns), ALL, 0, 0, tiled=True)
-    mine = jnp.broadcast_to(jnp.sum(pieces, axis=0), pieces.shape)
-    return lax.all_to_all(mine, ALL, 0, 0, tiled=True).reshape(rows, columns)
+    planes, layers = lax.axis_size(PLANE), lax.axis_size(LINE)
+    pieces = lax.all_to_all(part.reshape(planes, rows // planes, columns), PLANE, 0, 0, tiled=True)
+    mine = jnp.sum(pieces, axis=0)
+    step = 1
+    while step < layers:
+        mine += lax.ppermute(mine, LINE, [(z, z ^ step) for z in range(layers)])
+        step *= 2
+    mine = jnp.broadcast_to(mine, pieces.shape)
+    return lax.all_to_all(mine, PLANE, 0, 0, tiled=True).reshape(rows, columns)
 
 
 def on_device(diag_blocks, off_blocks, col_blocks, sketch):
@@ -743,7 +749,7 @@
     )
     base = base_sum(diag_blocks, sketch, [home, own.reshape(sketch.shape), first])
     image, part = image_and_gram(base, chip, received, pieces, block_rows * edge * peers)
-    gram = sum_over_devices(part, peers)
+    gram = sum_over_devices(part)
     return factor_and_basis(gram, image)
 
 

time: 421 us -> 419 us (level)
  blocking collectives: 28.1 us -> 18.5 us
  starting transfers between devices: 45.7 us -> 50.9 us
    all_to_all x2, blocking collectives: 28.1 us -> 18.5 us  [the longest x1 9.38 us: sum_over_devices(): lax.all_to_all(part.reshape(planes, rows // planes, columns), PLANE, 0, 0...]
    ppermute x0 -> x2, starting transfers between devices: none -> 5.27 us  [sum_over_devices(): mine += lax.ppermute(mine, LINE, [(z, z ^ step) for z in range(layers)])]
  transfers between devices with their start and end apart: 19 -> 21, of which waited for: 10 -> 12; matrix products, arithmetic and copies ran while one was open for 3% -> 3% of each run, Pallas kernels for 20% -> 20%
where the time goes in v8:
time: 419 us; the launch traced here: 418 us
  Pallas kernels  279 us (67%)
  waiting for transfers between devices  56.2 us (13%)
  starting transfers between devices  50.9 us (12%)
  blocking collectives  18.5 us (4%)
  other arithmetic  8.09 us (2%)
  local copies, waits for them, and re-layouts  4.27 us (1%)
    pallas_call x1, Pallas kernels, factor_and_basis(): pl.pallas_call(functools.partial(factor_kernel, rounds), out_shape=(jax.S...  189 us
    pallas_call x6, Pallas kernels, far_sum(): pl.pallas_call(functools.partial(far_kernel, most, begin, sizes, lines, l...  41.7 us
    pallas_call x4, Pallas kernels, plane_sum(): pl.pallas_call(functools.partial(plane_kernel, inside, begin, most, count...  25.7 us
    all_to_all x2, waiting for transfers between devices, on_device(): lax.all_to_all(part, PLANE, 0, 0, tiled=True)  18.4 us
    ppermute x3, waiting for transfers between devices, send_mirror(): return (lax.ppermute(mirror, LINE, steps), (mirror,))  13.9 us
    all_to_all x1, blocking collectives, sum_over_devices(): lax.all_to_all(part.reshape(planes, rows // planes, columns), PLANE, 0, 0...  9.38 us
    all_to_all x1, blocking collectives, sum_over_devices(): return lax.all_to_all(mine, PLANE, 0, 0, tiled=True).reshape(rows, columns)  9.12 us
    all_to_all x2, starting transfers between devices, on_device(): lax.all_to_all(part, PLANE, 0, 0, tiled=True)  8.92 us
  transfers between devices with their start and end apart: 21, of which 12 were waited for; matrix products, arithmetic and copies ran while one was open for 3% of the time, Pallas kernels for 20%

profile of v8, /device:TPU:0, one launch (start us, length us, event | category | flops | bytes accessed | tf_op | source)
XLA Modules:
  0.0 418.1 jit_solution(8170712036396841319)
XLA Ops:
  6.4 5.6 %collective-permute-start.7 = (bf16[2048,256]{1,0:T(8,128)(2,1)}, bf16[2048,256]{1,0:T(8,128)(2,1)}, u32[]{:S(2)}, u32[]{:S(2)}) collective-permute-start(bf16[2048,256]{1,0:T(8,128)(2,1)} %omega_ref.1), channel_id=1, source_target_pairs={{0,8},{8,16},{16,24},{1,9},{9,17},{17,25},{2,10},{10,18},{18,26},{... | collective-permute-start | bytes 3145736 | tf_op jit(solution)/shard_map/ppermute | solution.py:623
  19.4 5.0 %pack.1 = (bf16[8,1040,128]{2,1,0:T(8,128)(2,1)}, bf16[8,2048,128]{2,1,0:T(8,128)(2,1)}, bf16[8,1024,128]{2,1,0:T(8,128)(2,1)}) custom-call(s32[128]{0:T(128)} %get-tuple-element.32.entry_ref, s32[128]{0:T(128)} %get-tuple-element.31.plane_ref, s32[128]{0:T(128)} %get-tuple-element.30.slot_ref, s32[4]{0:T(128)} %convert_reduce_fusion.2.count_ref, ...), custom_call_target="tpu_custom_call" | custom-call | flops 999999995904 | bytes 99999997952 | tf_op jit(solution)/shard_map/pack/pallas_call | solution.py:72
  38.4 5.5 %collective-permute-start.8 = (bf16[2048,256]{1,0:T(8,128)(2,1)}, bf16[2048,256]{1,0:T(8,128)(2,1)}, u32[]{:S(2)}, u32[]{:S(2)}) collective-permute-start(bf16[2048,256]{1,0:T(8,128)(2,1)} %collective-permute-done.7.rest_1_.refs_11_.refs_14_), channel_id=1, source_target_pairs={{0,8},{8,16},{16,24},{1,9},{9,17},{17,25},{2,10},{10,18},{18,26},{... | collective-permute-start | bytes 3145736 | tf_op jit(solution)/shard_map/ppermute | solution.py:627
  49.5 8.4 %collective-permute-done.9.rest_2_.refs_9_.refs_10_.refs_12_.refs_13_ = bf16[2048,256]{1,0:T(8,128)(2,1)} collective-permute-done((bf16[2048,256]{1,0:T(8,128)(2,1)}, bf16[2048,256]{1,0:T(8,128)(2,1)}, u32[]{:S(2)}, u32[]{:S(2)}) %collective-permute-start.9) | collective-permute-done | bytes 1048608 | tf_op jit(solution)/shard_map/ppermute | solution.py:628
  58.0 8.7 %all-to-all-done.rest_0_.refs_7_ = bf16[8,1040,128]{2,1,0:T(8,128)(2,1)} async-done(((bf16[8,1040,128]{2,1,0:T(8,128)(2,1)}), bf16[8,1040,128]{2,1,0:T(8,128)(2,1)}, u32[]{:S(2)}, u32[]{:S(2)}) %all-to-all-start) | async-done | bytes 2129952 | tf_op jit(solution)/shard_map/all_to_all | solution.py:647
  66.7 4.6 %all-to-all-start.1 = ((bf16[8,2048,128]{2,1,0:T(8,128)(2,1)}), bf16[8,2048,128]{2,1,0:T(8,128)(2,1)}, u32[]{:S(2)}, u32[]{:S(2)}) async-start(bf16[8,2048,128]{2,1,0:T(8,128)(2,1)} %hold.3), calls=%async_computation.1 | async-start | bytes 8388608 | tf_op jit(solution)/shard_map/all_to_all | solution.py:647
  77.8 6.3 %mirror.3.refs_12_ = bf16[2048,256]{1,0:T(8,128)(2,1)} custom-call(s32[8]{0:T(128)} %pad_add_fusion.source_ref, s32[8,32]{1,0:T(8,128)} %bitcast.28, s32[8,32]{1,0:T(8,128)} %bitcast.17, bf16[8,1040,128]{2,1,0:T(8,128)(2,1)} %all-to-all-done.rest_0_.refs_7_, bf16[4,2048,256]{2,1,0:T(8,128)(2,1)} %bitcast.40, bf16[4,2048,256]{2,1,0:T(8,128)(2,1)} %bitcast.5.rest_2_), custom_call_target="tpu_custom_call" | custom-call | flops 999999995904 | bytes 99999997952 | tf_op jit(solution)/shard_map/mirror/pallas_call | solution.py:218
  84.8 6.1 %far.6.rest_3_ = f32[3,2048,256]{2,1,0:T(8,128)} custom-call(s32[3]{0:T(128)} %add_subtract_fusion.refs_0_, s32[3]{0:T(128)} %iota.37.refs_1_, s32[1]{0:T(128)} %bitcast.6.refs_2_, s32[8,32]{1,0:T(8,128)} %bitcast.29, s32[8,32]{1,0:T(8,128)} %bitcast.18, s32[8,8]{1,0:T(8,128)} %slice.22.refs_5_.row_ref, s32[8,8]{1,0:T(8,128)} %slice.23.refs_6_.col_ref, ...), custom_call_target="tpu_custom_call" | custom-call | flops 999999995904 | bytes 99999997952 | tf_op jit(solution)/shard_map/far/pallas_call | solution.py:338
  91.3 6.6 %home.1.refs_13_.rest_0_ = f32[2048,256]{1,0:T(8,128)} custom-call(s32[8]{0:T(128)} %pad_add_fusion.source_ref, s32[8,8]{1,0:T(8,128)} %slice.22.refs_5_.row_ref, s32[8,8]{1,0:T(8,128)} %slice.23.refs_6_.col_ref, bf16[8,1024,128]{2,1,0:T(8,128)(2,1)} %get-tuple-element.21.refs_10_.rest_0_.refs_15_, bf16[4,2048,256]{2,1,0:T(8,128)(2,1)} %bitcast.41, ...), custom_call_target="tpu_custom_call" | custom-call | flops 999999995904 | bytes 99999997952 | tf_op jit(solution)/shard_map/home/pallas_call | solution.py:218
  102.0 7.7 %far.7.refs_12_ = f32[3,2048,256]{2,1,0:T(8,128)} custom-call(s32[3]{0:T(128)} %multiply_add_fusion.1.refs_0_, s32[3]{0:T(128)} %iota.38.refs_1_, s32[1]{0:T(128)} %bitcast.6.refs_2_, s32[8,32]{1,0:T(8,128)} %bitcast.30, s32[8,32]{1,0:T(8,128)} %bitcast.19, s32[8,8]{1,0:T(8,128)} %slice.22.refs_5_.row_ref, s32[8,8]{1,0:T(8,128)} %slice.23.refs_6_.col_ref, ...), custom_call_target="tpu_custom_call" | custom-call | flops 999999995904 | bytes 99999997952 | tf_op jit(solution)/shard_map/far/pallas_call | solution.py:338
  109.8 9.7 %all-to-all-done.1.refs_7_.rest_0_.refs_8_ = bf16[8,2048,128]{2,1,0:T(8,128)(2,1)} async-done(((bf16[8,2048,128]{2,1,0:T(8,128)(2,1)}), bf16[8,2048,128]{2,1,0:T(8,128)(2,1)}, u32[]{:S(2)}, u32[]{:S(2)}) %all-to-all-start.1) | async-done | bytes 4194336 | tf_op jit(solution)/shard_map/all_to_all | solution.py:647
  120.1 5.8 %far.8.rest_3_ = bf16[3,2048,256]{2,1,0:T(8,128)(2,1)} custom-call(s32[3]{0:T(128)} %add_subtract_fusion.refs_0_, s32[3]{0:T(128)} %iota.39.refs_1_, s32[2]{0:T(128)} %pad_add_fusion.2.refs_2_, s32[8,32]{1,0:T(8,128)} %bitcast.31, s32[8,32]{1,0:T(8,128)} %bitcast.20, s32[8,8]{1,0:T(8,128)} %bitcast.32, s32[8,8]{1,0:T(8,128)} %bitcast.21, ...), custom_call_target="tpu_custom_call" | custom-call | flops 999999995904 | bytes 99999997952 | tf_op jit(solution)/shard_map/far/pallas_call | solution.py:338
  126.0 6.4 %mirror.4.refs_14_ = bf16[2048,256]{1,0:T(8,128)(2,1)} custom-call(s32[8]{0:T(128)} %pad_add_fusion.source_ref, s32[8,32]{1,0:T(8,128)} %bitcast.33, s32[8,32]{1,0:T(8,128)} %bitcast.22, bf16[8,2048,128]{2,1,0:T(8,128)(2,1)} %all-to-all-done.1.refs_7_.rest_0_.refs_8_, bf16[4,2048,256]{2,1,0:T(8,128)(2,1)} %bitcast.42, bf16[4,2048,256]{2,1,0:T(8,128)(2,1)} %bitcast.5.rest_2_, ...), custom_call_target="tpu_custom_call" | custom-call | flops 999999995904 | bytes 99999997952 | tf_op jit(solution)/shard_map/mirror/pallas_call | solution.py:218
  133.9 9.2 %far.9.refs_17_.rest_3_ = bf16[4,2048,256]{2,1,0:T(8,128)(2,1)} custom-call(s32[3]{0:T(128)} %multiply_add_fusion.1.refs_0_, s32[3]{0:T(128)} %and_select_fusion.refs_1_, s32[2]{0:T(128)} %pad_add_fusion.2.refs_2_, s32[8,32]{1,0:T(8,128)} %bitcast.34, s32[8,32]{1,0:T(8,128)} %bitcast.23, s32[8,8]{1,0:T(8,128)} %bitcast.35, s32[8,8]{1,0:T(8,128)} %bitcast.24, ...), custom_call_target="tpu_custom_call" | custom-call | flops 999999995904 | bytes 99999997952 | tf_op jit(solution)/shard_map/far/pallas_call | solution.py:338
  143.1 4.8 %all-to-all-start.2 = ((bf16[4,2048,256]{2,1,0:T(8,128)(2,1)}), bf16[4,2048,256]{2,1,0:T(8,128)(2,1)}, u32[]{:S(2)}, u32[]{:S(2)}) async-start(bf16[4,2048,256]{2,1,0:T(8,128)(2,1)} %far.9.refs_17_.rest_3_), calls=%async_computation.2 | async-start | bytes 8388608 | tf_op jit(solution)/shard_map/all_to_all | solution.py:735
  148.0 6.0 %far.10 = f32[1,2048,256]{2,1,0:T(8,128)} custom-call(s32[1]{0:T(128)S(6)} %sub.74.refs_0_, s32[1]{0:T(128)} %constant.120.clone.1.refs_1_, s32[3]{0:T(128)} %pad_add_fusion.1.refs_2_, s32[8,32]{1,0:T(8,128)} %bitcast.36, s32[8,32]{1,0:T(8,128)} %bitcast.25, s32[8,8]{1,0:T(8,128)} %slice.22.refs_5_.row_ref, s32[8,8]{1,0:T(8,128)} %slice.23.refs_6_.col_ref, ...), custom_call_target="tpu_custom_call" | custom-call | flops 999999995904 | bytes 99999997952 | tf_op jit(solution)/shard_map/far/pallas_call | solution.py:338
  154.3 6.4 %mirror.5.refs_18_ = bf16[2048,256]{1,0:T(8,128)(2,1)} custom-call(s32[8]{0:T(128)} %pad_add_fusion.source_ref, s32[8,32]{1,0:T(8,128)} %bitcast.37, s32[8,32]{1,0:T(8,128)} %bitcast.26, bf16[8,2048,128]{2,1,0:T(8,128)(2,1)} %all-to-all-done.1.refs_7_.rest_0_.refs_8_, bf16[4,2048,256]{2,1,0:T(8,128)(2,1)} %bitcast.43, bf16[4,2048,256]{2,1,0:T(8,128)(2,1)} %bitcast.5.rest_2_, ...), custom_call_target="tpu_custom_call" | custom-call | flops 999999995904 | bytes 99999997952 | tf_op jit(solution)/shard_map/mirror/pallas_call | solution.py:218
  164.0 6.8 %far.11 = f32[1,2048,256]{2,1,0:T(8,128)} custom-call(s32[1]{0:T(128)S(6)} %add.309.refs_0_, s32[1]{0:T(128)} %constant.120.clone.1.refs_1_, s32[3]{0:T(128)} %pad_add_fusion.1.refs_2_, s32[8,32]{1,0:T(8,128)} %bitcast.38, s32[8,32]{1,0:T(8,128)} %bitcast.27, s32[8,8]{1,0:T(8,128)} %slice.22.refs_5_.row_ref, s32[8,8]{1,0:T(8,128)} %slice.23.refs_6_.col_ref, ...), custom_call_target="tpu_custom_call" | custom-call | flops 999999995904 | bytes 99999997952 | tf_op jit(solution)/shard_map/far/pallas_call | solution.py:338
  170.8 7.1 %base.1.base_ref = f32[2048,256]{1,0:T(8,128)} custom-call(bf16[16,128,128]{2,1,0:T(8,128)(2,1)} %diag_ref.1, bf16[2048,256]{1,0:T(8,128)(2,1)} %omega_ref.1, f32[2048,256]{1,0:T(8,128)} %home.1.refs_13_.rest_0_, f32[2048,256]{1,0:T(8,128)} %bitcast.44, bf16[2048,256]{1,0:T(8,128)(2,1)} %collective-permute-done.13.rest_2_), custom_call_target="tpu_custom_call" | custom-call | flops 999999995904 | bytes 99999997952 | tf_op jit(solution)/shard_map/base/pallas_call | solution.py:384
  177.9 13.9 %collective-permute-done.15.rest_1_ = bf16[2048,256]{1,0:T(8,128)(2,1)} collective-permute-done((bf16[2048,256]{1,0:T(8,128)(2,1)}, bf16[2048,256]{1,0:T(8,128)(2,1)}, u32[]{:S(2)}, u32[]{:S(2)}) %collective-permute-start.15) | collective-permute-done | bytes 1048608 | tf_op jit(solution)/shard_map/ppermute | solution.py:682
  196.0 5.6 %image.1 = (f32[2048,256]{1,0:T(8,128)}, f32[256,256]{1,0:T(8,128)}) custom-call(s32[1]{0:T(128)} %bitcast.3.chip_ref, f32[2048,256]{1,0:T(8,128)} %base.1.base_ref, bf16[4,2048,256]{2,1,0:T(8,128)(2,1)} %all-to-all-done.2.far_ref, bf16[2048,256]{1,0:T(8,128)(2,1)} %collective-permute-done.14.rest_0_, bf16[2048,256]{1,0:T(8,128)(2,1)} %collective-permute-done.15.rest_1_), custom_call_target="tpu_custom_call" | custom-call | flops 999999995904 | bytes 99999997952 | tf_op jit(solution)/shard_map/image/pallas_call | solution.py:441
  201.6 9.4 %all_to_all.25 = f32[8,32,256]{2,1,0:T(8,128)S(1)} all-to-all(f32[8,32,256]{2,1,0:T(8,128)} %bitcast.15), channel_id=1, replica_groups=mesh['z'=4,'x'=2,'y'=2,'c'=2] {'x','y','c'}, dimensions={0} | all-to-all | bytes 524288 | tf_op jit(solution)/shard_map/all_to_all | solution.py:558
  220.1 9.1 %all_to_all.26 = f32[8,32,256]{2,1,0:T(8,128)} all-to-all(f32[8,32,256]{2,1,0:T(8,128)S(1)} %broadcast_in_dim.86), channel_id=1, replica_groups=mesh['z'=4,'x'=2,'y'=2,'c'=2] {'x','y','c'}, dimensions={0} | all-to-all | bytes 524288 | tf_op jit(solution)/shard_map/all_to_all | solution.py:565
  229.3 188.7 %factor.1 = (f32[2048,256]{1,0:T(8,128)}, f32[256,256]{1,0:T(8,128)}) custom-call(f32[256,256]{1,0:T(8,128)} %bitcast.16, f32[2048,256]{1,0:T(8,128)} %get-tuple-element.29.image_ref), custom_call_target="tpu_custom_call" | custom-call | flops 999999995904 | bytes 99999997952 | tf_op jit(solution)/shard_map/factor/pallas_call | solution.py:539
  (77 shorter events, 63.5 us)
Async XLA Ops:
  0.6 26.5 %collective-permute-start = (bf16[2048,256]{1,0:T(8,128)(2,1)}, bf16[2048,256]{1,0:T(8,128)(2,1)}, u32[]{:S(2)}, u32[]{:S(2)}) collective-permute-start(bf16[2048,256]{1,0:T(8,128)(2,1)} %omega_ref.1), channel_id=1, source_target_pairs={{0,4},{4,0},{1,5},{5,1},{2,6},{6,2},{3,7},{7,3},{8,12},{12,8},{9,1... | collective-permute-start | bytes 3145736 | tf_op jit(solution)/shard_map/ppermute | solution.py:634
  3.6 24.9 %collective-permute-start.1 = (bf16[2048,256]{1,0:T(8,128)(2,1)}, bf16[2048,256]{1,0:T(8,128)(2,1)}, u32[]{:S(2)}, u32[]{:S(2)}) collective-permute-start(bf16[2048,256]{1,0:T(8,128)(2,1)} %omega_ref.1), channel_id=1, source_target_pairs={{0,2},{2,0},{1,3},{3,1},{4,6},{6,4},{5,7},{7,5},{8,10},{10,8},{9,1... | collective-permute-start | bytes 3145736 | tf_op jit(solution)/shard_map/ppermute | solution.py:634
  5.2 32.0 %collective-permute-start.5 = (bf16[2048,256]{1,0:T(8,128)(2,1)}, bf16[2048,256]{1,0:T(8,128)(2,1)}, u32[]{:S(2)}, u32[]{:S(2)}) collective-permute-start(bf16[2048,256]{1,0:T(8,128)(2,1)} %omega_ref.1), channel_id=1, source_target_pairs={{8,0},{16,8},{24,16},{9,1},{17,9},{25,17},{10,2},{18,10},{26,18},{... | collective-permute-start | bytes 3145736 | tf_op jit(solution)/shard_map/ppermute | solution.py:623
  6.4 32.0 %collective-permute-start.7 = (bf16[2048,256]{1,0:T(8,128)(2,1)}, bf16[2048,256]{1,0:T(8,128)(2,1)}, u32[]{:S(2)}, u32[]{:S(2)}) collective-permute-start(bf16[2048,256]{1,0:T(8,128)(2,1)} %omega_ref.1), channel_id=1, source_target_pairs={{0,8},{8,16},{16,24},{1,9},{9,17},{17,25},{2,10},{10,18},{18,26},{... | collective-permute-start | bytes 3145736 | tf_op jit(solution)/shard_map/ppermute | solution.py:623
  12.0 46.0 %collective-permute-start.9 = (bf16[2048,256]{1,0:T(8,128)(2,1)}, bf16[2048,256]{1,0:T(8,128)(2,1)}, u32[]{:S(2)}, u32[]{:S(2)}) collective-permute-start(bf16[2048,256]{1,0:T(8,128)(2,1)} %omega_ref.1), channel_id=1, source_target_pairs={{24,0},{0,24},{25,1},{1,25},{26,2},{2,26},{27,3},{3,27},{28,4},{4,... | collective-permute-start | bytes 3145736 | tf_op jit(solution)/shard_map/ppermute | solution.py:628
  30.6 15.2 %collective-permute-start.2 = (bf16[1024,256]{1,0:T(8,128)(2,1)}, bf16[1024,256]{1,0:T(8,128)(2,1)}, u32[]{:S(2)}, u32[]{:S(2)}) collective-permute-start(bf16[1024,256]{1,0:T(8,128)(2,1)} %get-tuple-element.22), channel_id=1, source_target_pairs={{0,4},{4,0},{1,5},{5,1},{2,6},{6,2},{3,7},{7,3},{8,12},{12,8},{9,1... | collective-permute-start | bytes 1572872 | tf_op jit(solution)/shard_map/ppermute | solution.py:636
  31.1 15.2 %collective-permute-start.3 = (bf16[1024,256]{1,0:T(8,128)(2,1)}, bf16[1024,256]{1,0:T(8,128)(2,1)}, u32[]{:S(2)}, u32[]{:S(2)}) collective-permute-start(bf16[1024,256]{1,0:T(8,128)(2,1)} %get-tuple-element.23), channel_id=1, source_target_pairs={{0,2},{2,0},{1,3},{3,1},{4,6},{6,4},{5,7},{7,5},{8,10},{10,8},{9,1... | collective-permute-start | bytes 1572872 | tf_op jit(solution)/shard_map/ppermute | solution.py:636
  32.7 34.0 %all-to-all-start = ((bf16[8,1040,128]{2,1,0:T(8,128)(2,1)}), bf16[8,1040,128]{2,1,0:T(8,128)(2,1)}, u32[]{:S(2)}, u32[]{:S(2)}) async-start(bf16[8,1040,128]{2,1,0:T(8,128)(2,1)} %hold.2), calls=%async_computation | async-start | bytes 4259840 | tf_op jit(solution)/shard_map/all_to_all | solution.py:647
  37.1 47.1 %collective-permute-start.6 = (bf16[2048,256]{1,0:T(8,128)(2,1)}, bf16[2048,256]{1,0:T(8,128)(2,1)}, u32[]{:S(2)}, u32[]{:S(2)}) collective-permute-start(bf16[2048,256]{1,0:T(8,128)(2,1)} %collective-permute-done.5.rest_0_.refs_8_.refs_11_), channel_id=1, source_target_pairs={{8,0},{16,8},{24,16},{9,1},{17,9},{25,17},{10,2},{18,10},{26,18},{... | collective-permute-start | bytes 3145736 | tf_op jit(solution)/shard_map/ppermute | solution.py:627
  38.4 45.8 %collective-permute-start.8 = (bf16[2048,256]{1,0:T(8,128)(2,1)}, bf16[2048,256]{1,0:T(8,128)(2,1)}, u32[]{:S(2)}, u32[]{:S(2)}) collective-permute-start(bf16[2048,256]{1,0:T(8,128)(2,1)} %collective-permute-done.7.rest_1_.refs_11_.refs_14_), channel_id=1, source_target_pairs={{0,8},{8,16},{16,24},{1,9},{9,17},{17,25},{2,10},{10,18},{18,26},{... | collective-permute-start | bytes 3145736 | tf_op jit(solution)/shard_map/ppermute | solution.py:627
  49.5 28.4 %collective-permute-start.4 = (bf16[8192,256]{1,0:T(8,128)(2,1)}, bf16[8192,256]{1,0:T(8,128)(2,1)}, u32[]{:S(2)}, u32[]{:S(2)}) collective-permute-start(bf16[8192,256]{1,0:T(8,128)(2,1)} %join.1), channel_id=1, source_target_pairs={{0,1},{1,0},{2,3},{3,2},{4,5},{5,4},{6,7},{7,6},{8,9},{9,8},{10,11... | collective-permute-start | bytes 12582920 | tf_op jit(solution)/shard_map/ppermute | solution.py:640
  58.0 14.7 %copy-start.1 = (s32[256]{0:T(256)S(1)}, s32[256]{0:T(256)}, u32[]{:S(2)}) copy-start(s32[256]{0:T(256)} %get-tuple-element.19) | copy-start | bytes 3076
  58.0 15.5 %copy-start = (s32[256]{0:T(256)S(1)}, s32[256]{0:T(256)}, u32[]{:S(2)}) copy-start(s32[256]{0:T(256)} %get-tuple-element.20) | copy-start | bytes 3076
  66.7 52.7 %all-to-all-start.1 = ((bf16[8,2048,128]{2,1,0:T(8,128)(2,1)}), bf16[8,2048,128]{2,1,0:T(8,128)(2,1)}, u32[]{:S(2)}, u32[]{:S(2)}) async-start(bf16[8,2048,128]{2,1,0:T(8,128)(2,1)} %hold.3), calls=%async_computation.1 | async-start | bytes 8388608 | tf_op jit(solution)/shard_map/all_to_all | solution.py:647
  90.9 10.6 %collective-permute-start.10 = (f32[3,2048,256]{2,1,0:T(8,128)}, f32[3,2048,256]{2,1,0:T(8,128)}, u32[]{:S(2)}, u32[]{:S(2)}) collective-permute-start(f32[3,2048,256]{2,1,0:T(8,128)} %far.6.rest_3_), channel_id=1, source_target_pairs={{0,1},{1,0},{2,3},{3,2},{4,5},{5,4},{6,7},{7,6},{8,9},{9,8},{10,11... | collective-permute-start | bytes 18874376 | tf_op jit(solution)/shard_map/ppermute | solution.py:704
  97.9 72.8 %collective-permute-start.13 = (bf16[2048,256]{1,0:T(8,128)(2,1)}, bf16[2048,256]{1,0:T(8,128)(2,1)}, u32[]{:S(2)}, u32[]{:S(2)}) collective-permute-start(bf16[2048,256]{1,0:T(8,128)(2,1)} %mirror.3.refs_12_), channel_id=1, source_target_pairs={{0,16},{8,24},{16,0},{24,8},{1,17},{9,25},{17,1},{25,9},{2,18},{10... | collective-permute-start | bytes 3145736 | tf_op jit(solution)/shard_map/ppermute | solution.py:682
  125.9 8.0 %collective-permute-start.11 = (bf16[3,2048,256]{2,1,0:T(8,128)(2,1)}, bf16[3,2048,256]{2,1,0:T(8,128)(2,1)}, u32[]{:S(2)}, u32[]{:S(2)}) collective-permute-start(bf16[3,2048,256]{2,1,0:T(8,128)(2,1)} %far.8.rest_3_), channel_id=1, source_target_pairs={{0,1},{1,0},{2,3},{3,2},{4,5},{5,4},{6,7},{7,6},{8,9},{9,8},{10,11... | collective-permute-start | bytes 9437192 | tf_op jit(solution)/shard_map/ppermute | solution.py:704
  132.3 45.6 %collective-permute-start.14 = (bf16[2048,256]{1,0:T(8,128)(2,1)}, bf16[2048,256]{1,0:T(8,128)(2,1)}, u32[]{:S(2)}, u32[]{:S(2)}) collective-permute-start(bf16[2048,256]{1,0:T(8,128)(2,1)} %mirror.4.refs_14_), channel_id=1, source_target_pairs={{0,8},{8,16},{16,24},{24,0},{1,9},{9,17},{17,25},{25,1},{2,10},{10... | collective-permute-start | bytes 3145736 | tf_op jit(solution)/shard_map/ppermute | solution.py:682
  143.1 52.9 %all-to-all-start.2 = ((bf16[4,2048,256]{2,1,0:T(8,128)(2,1)}), bf16[4,2048,256]{2,1,0:T(8,128)(2,1)}, u32[]{:S(2)}, u32[]{:S(2)}) async-start(bf16[4,2048,256]{2,1,0:T(8,128)(2,1)} %far.9.refs_17_.rest_3_), calls=%async_computation.2 | async-start | bytes 8388608 | tf_op jit(solution)/shard_map/all_to_all | solution.py:735
  154.0 10.0 %collective-permute-start.12 = (f32[1,2048,256]{2,1,0:T(8,128)}, f32[1,2048,256]{2,1,0:T(8,128)}, u32[]{:S(2)}, u32[]{:S(2)}) collective-permute-start(f32[1,2048,256]{2,1,0:T(8,128)} %far.10), channel_id=1, source_target_pairs={{0,1},{1,0},{2,3},{3,2},{4,5},{5,4},{6,7},{7,6},{8,9},{9,8},{10,11... | collective-permute-start | bytes 6291464 | tf_op jit(solution)/shard_map/ppermute | solution.py:704
  160.7 31.1 %collective-permute-start.15 = (bf16[2048,256]{1,0:T(8,128)(2,1)}, bf16[2048,256]{1,0:T(8,128)(2,1)}, u32[]{:S(2)}, u32[]{:S(2)}) collective-permute-start(bf16[2048,256]{1,0:T(8,128)(2,1)} %mirror.5.refs_18_), channel_id=1, source_target_pairs={{0,24},{8,0},{16,8},{24,16},{1,25},{9,1},{17,9},{25,17},{2,26},{10... | collective-permute-start | bytes 3145736 | tf_op jit(solution)/shard_map/ppermute | solution.py:682
  211.0 4.1 collective-permute-start.16
  215.2 4.9 %collective-permute-start.17 = (f32[32,256]{1,0:T(8,128)S(1)}, f32[32,256]{1,0:T(8,128)S(1)}, u32[]{:S(2)}, u32[]{:S(2)}) collective-permute-start(f32[32,256]{1,0:T(8,128)S(1)} %add.314), channel_id=1, source_target_pairs={{0,16},{8,24},{16,0},{24,8},{1,17},{9,25},{17,1},{25,9},{2,18},{10... | collective-permute-start | bytes 98312 | tf_op jit(solution)/shard_map/ppermute | solution.py:562

commit v9 on v8

--- a/solution.py
+++ b/solution.py
@@ -274,8 +274,9 @@
     ]
     if at_home:
         own = pltpu.make_async_copy(home_refs[1], homes[1], omega_sem.at[lines])
-    for k in range(min(depth, count)):
-        for move in arrive(k):
+    ahead = [arrive(k) for k in range(min(depth, count))]
+    for k, moves in enumerate(ahead):
+        for move in moves[: len(moves) - added]:
             move.start()
         if k == 0:
             if at_home:
@@ -283,9 +284,13 @@
             for index, (above, below) in enumerate(lead):
                 pl.when(above_ref[index] == 1)(above.start)
                 pl.when(above_ref[index] == 0)(below.start)
+    for moves in ahead:
+        for move in moves[len(moves) - added :]:
+            move.start()
     for k in range(count):
         slot, source = k % depth, source_ref[k]
-        for move in arrive(k):
+        moves = arrive(k)
+        for move in moves[: len(moves) - added]:
             move.wait()
         total[...] = jnp.zeros_like(total)
         if at_home:
@@ -310,6 +315,8 @@
                 index += 1
         if k >= depth:
             leave(k - depth).wait()
+        for move in moves[len(moves) - added :]:
+            move.wait()
         result = total[:spare].reshape(outs.shape[1:])
         for add in adds:
             result += add[slot].astype(jnp.float32)

time: 419 us -> 419 us (level)
  transfers between devices with their start and end apart: 21 -> 21, of which waited for: 12 -> 13; matrix products, arithmetic and copies ran while one was open for 3% -> 3% of each run, Pallas kernels for 20% -> 20%
where the time goes in v9:
time: 419 us; the launch traced here: 417 us
  Pallas kernels  278 us (66%)
  waiting for transfers between devices  58.5 us (14%)
  starting transfers between devices  49.1 us (12%)
  blocking collectives  18.5 us (4%)
  other arithmetic  8.09 us (2%)
  local copies, waits for them, and re-layouts  4.27 us (1%)
    pallas_call x1, Pallas kernels, factor_and_basis(): pl.pallas_call(functools.partial(factor_kernel, rounds), out_shape=(jax.S...  189 us
    pallas_call x6, Pallas kernels, far_sum(): pl.pallas_call(functools.partial(far_kernel, most, begin, sizes, lines, l...  40.4 us
    pallas_call x4, Pallas kernels, plane_sum(): pl.pallas_call(functools.partial(plane_kernel, inside, begin, most, count...  25.7 us
    all_to_all x2, waiting for transfers between devices, on_device(): lax.all_to_all(part, PLANE, 0, 0, tiled=True)  18.4 us
    ppermute x3, waiting for transfers between devices, send_mirror(): return (lax.ppermute(mirror, LINE, steps), (mirror,))  16 us
    all_to_all x1, blocking collectives, sum_over_devices(): lax.all_to_all(part.reshape(planes, rows // planes, columns), PLANE, 0, 0...  9.38 us
    all_to_all x1, blocking collectives, sum_over_devices(): return lax.all_to_all(mine, PLANE, 0, 0, tiled=True).reshape(rows, columns)  9.12 us
    all_to_all x2, starting transfers between devices, on_device(): lax.all_to_all(part, PLANE, 0, 0, tiled=True)  8.92 us
  transfers between devices with their start and end apart: 21, of which 13 were waited for; matrix products, arithmetic and copies ran while one was open for 3% of the time, Pallas kernels for 20%

profile of v9, /device:TPU:0, one launch (start us, length us, event | category | flops | bytes accessed | tf_op | source)
XLA Modules:
  0.0 417.3 jit_solution(17647491169506435788)
XLA Ops:
  6.4 5.6 %collective-permute-start.7 = (bf16[2048,256]{1,0:T(8,128)(2,1)}, bf16[2048,256]{1,0:T(8,128)(2,1)}, u32[]{:S(2)}, u32[]{:S(2)}) collective-permute-start(bf16[2048,256]{1,0:T(8,128)(2,1)} %omega_ref.1), channel_id=1, source_target_pairs={{0,8},{8,16},{16,24},{1,9},{9,17},{17,25},{2,10},{10,18},{18,26},{... | collective-permute-start | bytes 3145736 | tf_op jit(solution)/shard_map/ppermute | solution.py:630
  19.4 5.0 %pack.1 = (bf16[8,1040,128]{2,1,0:T(8,128)(2,1)}, bf16[8,2048,128]{2,1,0:T(8,128)(2,1)}, bf16[8,1024,128]{2,1,0:T(8,128)(2,1)}) custom-call(s32[128]{0:T(128)} %get-tuple-element.32.entry_ref, s32[128]{0:T(128)} %get-tuple-element.31.plane_ref, s32[128]{0:T(128)} %get-tuple-element.30.slot_ref, s32[4]{0:T(128)} %convert_reduce_fusion.2.count_ref, ...), custom_call_target="tpu_custom_call" | custom-call | flops 999999995904 | bytes 99999997952 | tf_op jit(solution)/shard_map/pack/pallas_call | solution.py:72
  38.4 5.5 %collective-permute-start.8 = (bf16[2048,256]{1,0:T(8,128)(2,1)}, bf16[2048,256]{1,0:T(8,128)(2,1)}, u32[]{:S(2)}, u32[]{:S(2)}) collective-permute-start(bf16[2048,256]{1,0:T(8,128)(2,1)} %collective-permute-done.7.rest_1_.refs_11_.refs_14_), channel_id=1, source_target_pairs={{0,8},{8,16},{16,24},{1,9},{9,17},{17,25},{2,10},{10,18},{18,26},{... | collective-permute-start | bytes 3145736 | tf_op jit(solution)/shard_map/ppermute | solution.py:634
  49.5 8.4 %collective-permute-done.9.rest_2_.refs_9_.refs_10_.refs_12_.refs_13_ = bf16[2048,256]{1,0:T(8,128)(2,1)} collective-permute-done((bf16[2048,256]{1,0:T(8,128)(2,1)}, bf16[2048,256]{1,0:T(8,128)(2,1)}, u32[]{:S(2)}, u32[]{:S(2)}) %collective-permute-start.9) | collective-permute-done | bytes 1048608 | tf_op jit(solution)/shard_map/ppermute | solution.py:635
  58.0 8.7 %all-to-all-done.rest_0_.refs_7_ = bf16[8,1040,128]{2,1,0:T(8,128)(2,1)} async-done(((bf16[8,1040,128]{2,1,0:T(8,128)(2,1)}), bf16[8,1040,128]{2,1,0:T(8,128)(2,1)}, u32[]{:S(2)}, u32[]{:S(2)}) %all-to-all-start) | async-done | bytes 2129952 | tf_op jit(solution)/shard_map/all_to_all | solution.py:654
  66.7 4.6 %all-to-all-start.1 = ((bf16[8,2048,128]{2,1,0:T(8,128)(2,1)}), bf16[8,2048,128]{2,1,0:T(8,128)(2,1)}, u32[]{:S(2)}, u32[]{:S(2)}) async-start(bf16[8,2048,128]{2,1,0:T(8,128)(2,1)} %hold.3), calls=%async_computation.1 | async-start | bytes 8388608 | tf_op jit(solution)/shard_map/all_to_all | solution.py:654
  77.8 6.3 %mirror.3.refs_12_ = bf16[2048,256]{1,0:T(8,128)(2,1)} custom-call(s32[8]{0:T(128)} %pad_add_fusion.source_ref, s32[8,32]{1,0:T(8,128)} %bitcast.28, s32[8,32]{1,0:T(8,128)} %bitcast.17, bf16[8,1040,128]{2,1,0:T(8,128)(2,1)} %all-to-all-done.rest_0_.refs_7_, bf16[4,2048,256]{2,1,0:T(8,128)(2,1)} %bitcast.40, bf16[4,2048,256]{2,1,0:T(8,128)(2,1)} %bitcast.5.rest_2_), custom_call_target="tpu_custom_call" | custom-call | flops 999999995904 | bytes 99999997952 | tf_op jit(solution)/shard_map/mirror/pallas_call | solution.py:218
  84.8 6.1 %far.6.rest_3_ = f32[3,2048,256]{2,1,0:T(8,128)} custom-call(s32[3]{0:T(128)} %add_subtract_fusion.refs_0_, s32[3]{0:T(128)} %iota.37.refs_1_, s32[1]{0:T(128)} %bitcast.6.refs_2_, s32[8,32]{1,0:T(8,128)} %bitcast.29, s32[8,32]{1,0:T(8,128)} %bitcast.18, s32[8,8]{1,0:T(8,128)} %slice.22.refs_5_.row_ref, s32[8,8]{1,0:T(8,128)} %slice.23.refs_6_.col_ref, ...), custom_call_target="tpu_custom_call" | custom-call | flops 999999995904 | bytes 99999997952 | tf_op jit(solution)/shard_map/far/pallas_call | solution.py:345
  91.3 6.6 %home.1.refs_13_.rest_0_ = f32[2048,256]{1,0:T(8,128)} custom-call(s32[8]{0:T(128)} %pad_add_fusion.source_ref, s32[8,8]{1,0:T(8,128)} %slice.22.refs_5_.row_ref, s32[8,8]{1,0:T(8,128)} %slice.23.refs_6_.col_ref, bf16[8,1024,128]{2,1,0:T(8,128)(2,1)} %get-tuple-element.21.refs_10_.rest_0_.refs_15_, bf16[4,2048,256]{2,1,0:T(8,128)(2,1)} %bitcast.41, ...), custom_call_target="tpu_custom_call" | custom-call | flops 999999995904 | bytes 99999997952 | tf_op jit(solution)/shard_map/home/pallas_call | solution.py:218
  102.0 7.8 %far.7.refs_12_ = f32[3,2048,256]{2,1,0:T(8,128)} custom-call(s32[3]{0:T(128)} %multiply_add_fusion.1.refs_0_, s32[3]{0:T(128)} %iota.38.refs_1_, s32[1]{0:T(128)} %bitcast.6.refs_2_, s32[8,32]{1,0:T(8,128)} %bitcast.30, s32[8,32]{1,0:T(8,128)} %bitcast.19, s32[8,8]{1,0:T(8,128)} %slice.22.refs_5_.row_ref, s32[8,8]{1,0:T(8,128)} %slice.23.refs_6_.col_ref, ...), custom_call_target="tpu_custom_call" | custom-call | flops 999999995904 | bytes 99999997952 | tf_op jit(solution)/shard_map/far/pallas_call | solution.py:345
  109.8 9.7 %all-to-all-done.1.refs_7_.rest_0_.refs_8_ = bf16[8,2048,128]{2,1,0:T(8,128)(2,1)} async-done(((bf16[8,2048,128]{2,1,0:T(8,128)(2,1)}), bf16[8,2048,128]{2,1,0:T(8,128)(2,1)}, u32[]{:S(2)}, u32[]{:S(2)}) %all-to-all-start.1) | async-done | bytes 4194336 | tf_op jit(solution)/shard_map/all_to_all | solution.py:654
  120.1 5.8 %far.8.rest_3_ = bf16[3,2048,256]{2,1,0:T(8,128)(2,1)} custom-call(s32[3]{0:T(128)} %add_subtract_fusion.refs_0_, s32[3]{0:T(128)} %iota.39.refs_1_, s32[2]{0:T(128)} %pad_add_fusion.2.refs_2_, s32[8,32]{1,0:T(8,128)} %bitcast.31, s32[8,32]{1,0:T(8,128)} %bitcast.20, s32[8,8]{1,0:T(8,128)} %bitcast.32, s32[8,8]{1,0:T(8,128)} %bitcast.21, ...), custom_call_target="tpu_custom_call" | custom-call | flops 999999995904 | bytes 99999997952 | tf_op jit(solution)/shard_map/far/pallas_call | solution.py:345
  126.0 6.4 %mirror.4.refs_14_ = bf16[2048,256]{1,0:T(8,128)(2,1)} custom-call(s32[8]{0:T(128)} %pad_add_fusion.source_ref, s32[8,32]{1,0:T(8,128)} %bitcast.33, s32[8,32]{1,0:T(8,128)} %bitcast.22, bf16[8,2048,128]{2,1,0:T(8,128)(2,1)} %all-to-all-done.1.refs_7_.rest_0_.refs_8_, bf16[4,2048,256]{2,1,0:T(8,128)(2,1)} %bitcast.42, bf16[4,2048,256]{2,1,0:T(8,128)(2,1)} %bitcast.5.rest_2_, ...), custom_call_target="tpu_custom_call" | custom-call | flops 999999995904 | bytes 99999997952 | tf_op jit(solution)/shard_map/mirror/pallas_call | solution.py:218
  133.9 8.7 %far.9.refs_17_.rest_3_ = bf16[4,2048,256]{2,1,0:T(8,128)(2,1)} custom-call(s32[3]{0:T(128)} %multiply_add_fusion.1.refs_0_, s32[3]{0:T(128)} %and_select_fusion.refs_1_, s32[2]{0:T(128)} %pad_add_fusion.2.refs_2_, s32[8,32]{1,0:T(8,128)} %bitcast.34, s32[8,32]{1,0:T(8,128)} %bitcast.23, s32[8,8]{1,0:T(8,128)} %bitcast.35, s32[8,8]{1,0:T(8,128)} %bitcast.24, ...), custom_call_target="tpu_custom_call" | custom-call | flops 999999995904 | bytes 99999997952 | tf_op jit(solution)/shard_map/far/pallas_call | solution.py:345
  142.6 4.8 %all-to-all-start.2 = ((bf16[4,2048,256]{2,1,0:T(8,128)(2,1)}), bf16[4,2048,256]{2,1,0:T(8,128)(2,1)}, u32[]{:S(2)}, u32[]{:S(2)}) async-start(bf16[4,2048,256]{2,1,0:T(8,128)(2,1)} %far.9.refs_17_.rest_3_), calls=%async_computation.2 | async-start | bytes 8388608 | tf_op jit(solution)/shard_map/all_to_all | solution.py:742
  147.4 6.0 %far.10 = f32[1,2048,256]{2,1,0:T(8,128)} custom-call(s32[1]{0:T(128)S(6)} %sub.74.refs_0_, s32[1]{0:T(128)} %constant.120.clone.1.refs_1_, s32[3]{0:T(128)} %pad_add_fusion.1.refs_2_, s32[8,32]{1,0:T(8,128)} %bitcast.36, s32[8,32]{1,0:T(8,128)} %bitcast.25, s32[8,8]{1,0:T(8,128)} %slice.22.refs_5_.row_ref, s32[8,8]{1,0:T(8,128)} %slice.23.refs_6_.col_ref, ...), custom_call_target="tpu_custom_call" | custom-call | flops 999999995904 | bytes 99999997952 | tf_op jit(solution)/shard_map/far/pallas_call | solution.py:345
  153.7 6.4 %mirror.5.refs_18_ = bf16[2048,256]{1,0:T(8,128)(2,1)} custom-call(s32[8]{0:T(128)} %pad_add_fusion.source_ref, s32[8,32]{1,0:T(8,128)} %bitcast.37, s32[8,32]{1,0:T(8,128)} %bitcast.26, bf16[8,2048,128]{2,1,0:T(8,128)(2,1)} %all-to-all-done.1.refs_7_.rest_0_.refs_8_, bf16[4,2048,256]{2,1,0:T(8,128)(2,1)} %bitcast.43, bf16[4,2048,256]{2,1,0:T(8,128)(2,1)} %bitcast.5.rest_2_, ...), custom_call_target="tpu_custom_call" | custom-call | flops 999999995904 | bytes 99999997952 | tf_op jit(solution)/shard_map/mirror/pallas_call | solution.py:218
  162.6 6.1 %far.11 = f32[1,2048,256]{2,1,0:T(8,128)} custom-call(s32[1]{0:T(128)S(6)} %add.309.refs_0_, s32[1]{0:T(128)} %constant.120.clone.1.refs_1_, s32[3]{0:T(128)} %pad_add_fusion.1.refs_2_, s32[8,32]{1,0:T(8,128)} %bitcast.38, s32[8,32]{1,0:T(8,128)} %bitcast.27, s32[8,8]{1,0:T(8,128)} %slice.22.refs_5_.row_ref, s32[8,8]{1,0:T(8,128)} %slice.23.refs_6_.col_ref, ...), custom_call_target="tpu_custom_call" | custom-call | flops 999999995904 | bytes 99999997952 | tf_op jit(solution)/shard_map/far/pallas_call | solution.py:345
  170.2 7.1 %base.1.base_ref = f32[2048,256]{1,0:T(8,128)} custom-call(bf16[16,128,128]{2,1,0:T(8,128)(2,1)} %diag_ref.1, bf16[2048,256]{1,0:T(8,128)(2,1)} %omega_ref.1, f32[2048,256]{1,0:T(8,128)} %home.1.refs_13_.rest_0_, f32[2048,256]{1,0:T(8,128)} %bitcast.44, bf16[2048,256]{1,0:T(8,128)(2,1)} %collective-permute-done.13.rest_2_), custom_call_target="tpu_custom_call" | custom-call | flops 999999995904 | bytes 99999997952 | tf_op jit(solution)/shard_map/base/pallas_call | solution.py:391
  177.3 14.5 %collective-permute-done.15.rest_1_ = bf16[2048,256]{1,0:T(8,128)(2,1)} collective-permute-done((bf16[2048,256]{1,0:T(8,128)(2,1)}, bf16[2048,256]{1,0:T(8,128)(2,1)}, u32[]{:S(2)}, u32[]{:S(2)}) %collective-permute-start.15) | collective-permute-done | bytes 1048608 | tf_op jit(solution)/shard_map/ppermute | solution.py:689
  195.5 5.6 %image.1 = (f32[2048,256]{1,0:T(8,128)}, f32[256,256]{1,0:T(8,128)}) custom-call(s32[1]{0:T(128)} %bitcast.3.chip_ref, f32[2048,256]{1,0:T(8,128)} %base.1.base_ref, bf16[4,2048,256]{2,1,0:T(8,128)(2,1)} %all-to-all-done.2.far_ref, bf16[2048,256]{1,0:T(8,128)(2,1)} %collective-permute-done.14.rest_0_, bf16[2048,256]{1,0:T(8,128)(2,1)} %collective-permute-done.15.rest_1_), custom_call_target="tpu_custom_call" | custom-call | flops 999999995904 | bytes 99999997952 | tf_op jit(solution)/shard_map/image/pallas_call | solution.py:448
  201.1 9.4 %all_to_all.25 = f32[8,32,256]{2,1,0:T(8,128)S(1)} all-to-all(f32[8,32,256]{2,1,0:T(8,128)} %bitcast.15), channel_id=1, replica_groups=mesh['z'=4,'x'=2,'y'=2,'c'=2] {'x','y','c'}, dimensions={0} | all-to-all | bytes 524288 | tf_op jit(solution)/shard_map/all_to_all | solution.py:565
  219.3 9.1 %all_to_all.26 = f32[8,32,256]{2,1,0:T(8,128)} all-to-all(f32[8,32,256]{2,1,0:T(8,128)S(1)} %broadcast_in_dim.86), channel_id=1, replica_groups=mesh['z'=4,'x'=2,'y'=2,'c'=2] {'x','y','c'}, dimensions={0} | all-to-all | bytes 524288 | tf_op jit(solution)/shard_map/all_to_all | solution.py:572
  228.4 188.7 %factor.1 = (f32[2048,256]{1,0:T(8,128)}, f32[256,256]{1,0:T(8,128)}) custom-call(f32[256,256]{1,0:T(8,128)} %bitcast.16, f32[2048,256]{1,0:T(8,128)} %get-tuple-element.29.image_ref), custom_call_target="tpu_custom_call" | custom-call | flops 999999995904 | bytes 99999997952 | tf_op jit(solution)/shard_map/factor/pallas_call | solution.py:546
  (77 shorter events, 63.3 us)
Async XLA Ops:
  0.6 26.5 %collective-permute-start = (bf16[2048,256]{1,0:T(8,128)(2,1)}, bf16[2048,256]{1,0:T(8,128)(2,1)}, u32[]{:S(2)}, u32[]{:S(2)}) collective-permute-start(bf16[2048,256]{1,0:T(8,128)(2,1)} %omega_ref.1), channel_id=1, source_target_pairs={{0,4},{4,0},{1,5},{5,1},{2,6},{6,2},{3,7},{7,3},{8,12},{12,8},{9,1... | collective-permute-start | bytes 3145736 | tf_op jit(solution)/shard_map/ppermute | solution.py:641
  3.6 24.9 %collective-permute-start.1 = (bf16[2048,256]{1,0:T(8,128)(2,1)}, bf16[2048,256]{1,0:T(8,128)(2,1)}, u32[]{:S(2)}, u32[]{:S(2)}) collective-permute-start(bf16[2048,256]{1,0:T(8,128)(2,1)} %omega_ref.1), channel_id=1, source_target_pairs={{0,2},{2,0},{1,3},{3,1},{4,6},{6,4},{5,7},{7,5},{8,10},{10,8},{9,1... | collective-permute-start | bytes 3145736 | tf_op jit(solution)/shard_map/ppermute | solution.py:641
  5.2 32.0 %collective-permute-start.5 = (bf16[2048,256]{1,0:T(8,128)(2,1)}, bf16[2048,256]{1,0:T(8,128)(2,1)}, u32[]{:S(2)}, u32[]{:S(2)}) collective-permute-start(bf16[2048,256]{1,0:T(8,128)(2,1)} %omega_ref.1), channel_id=1, source_target_pairs={{8,0},{16,8},{24,16},{9,1},{17,9},{25,17},{10,2},{18,10},{26,18},{... | collective-permute-start | bytes 3145736 | tf_op jit(solution)/shard_map/ppermute | solution.py:630
  6.4 32.0 %collective-permute-start.7 = (bf16[2048,256]{1,0:T(8,128)(2,1)}, bf16[2048,256]{1,0:T(8,128)(2,1)}, u32[]{:S(2)}, u32[]{:S(2)}) collective-permute-start(bf16[2048,256]{1,0:T(8,128)(2,1)} %omega_ref.1), channel_id=1, source_target_pairs={{0,8},{8,16},{16,24},{1,9},{9,17},{17,25},{2,10},{10,18},{18,26},{... | collective-permute-start | bytes 3145736 | tf_op jit(solution)/shard_map/ppermute | solution.py:630
  12.0 46.0 %collective-permute-start.9 = (bf16[2048,256]{1,0:T(8,128)(2,1)}, bf16[2048,256]{1,0:T(8,128)(2,1)}, u32[]{:S(2)}, u32[]{:S(2)}) collective-permute-start(bf16[2048,256]{1,0:T(8,128)(2,1)} %omega_ref.1), channel_id=1, source_target_pairs={{24,0},{0,24},{25,1},{1,25},{26,2},{2,26},{27,3},{3,27},{28,4},{4,... | collective-permute-start | bytes 3145736 | tf_op jit(solution)/shard_map/ppermute | solution.py:635
  30.6 15.2 %collective-permute-start.2 = (bf16[1024,256]{1,0:T(8,128)(2,1)}, bf16[1024,256]{1,0:T(8,128)(2,1)}, u32[]{:S(2)}, u32[]{:S(2)}) collective-permute-start(bf16[1024,256]{1,0:T(8,128)(2,1)} %get-tuple-element.22), channel_id=1, source_target_pairs={{0,4},{4,0},{1,5},{5,1},{2,6},{6,2},{3,7},{7,3},{8,12},{12,8},{9,1... | collective-permute-start | bytes 1572872 | tf_op jit(solution)/shard_map/ppermute | solution.py:643
  31.1 15.2 %collective-permute-start.3 = (bf16[1024,256]{1,0:T(8,128)(2,1)}, bf16[1024,256]{1,0:T(8,128)(2,1)}, u32[]{:S(2)}, u32[]{:S(2)}) collective-permute-start(bf16[1024,256]{1,0:T(8,128)(2,1)} %get-tuple-element.23), channel_id=1, source_target_pairs={{0,2},{2,0},{1,3},{3,1},{4,6},{6,4},{5,7},{7,5},{8,10},{10,8},{9,1... | collective-permute-start | bytes 1572872 | tf_op jit(solution)/shard_map/ppermute | solution.py:643
  32.7 34.0 %all-to-all-start = ((bf16[8,1040,128]{2,1,0:T(8,128)(2,1)}), bf16[8,1040,128]{2,1,0:T(8,128)(2,1)}, u32[]{:S(2)}, u32[]{:S(2)}) async-start(bf16[8,1040,128]{2,1,0:T(8,128)(2,1)} %hold.2), calls=%async_computation | async-start | bytes 4259840 | tf_op jit(solution)/shard_map/all_to_all | solution.py:654
  37.1 47.1 %collective-permute-start.6 = (bf16[2048,256]{1,0:T(8,128)(2,1)}, bf16[2048,256]{1,0:T(8,128)(2,1)}, u32[]{:S(2)}, u32[]{:S(2)}) collective-permute-start(bf16[2048,256]{1,0:T(8,128)(2,1)} %collective-permute-done.5.rest_0_.refs_8_.refs_11_), channel_id=1, source_target_pairs={{8,0},{16,8},{24,16},{9,1},{17,9},{25,17},{10,2},{18,10},{26,18},{... | collective-permute-start | bytes 3145736 | tf_op jit(solution)/shard_map/ppermute | solution.py:634
  38.4 45.8 %collective-permute-start.8 = (bf16[2048,256]{1,0:T(8,128)(2,1)}, bf16[2048,256]{1,0:T(8,128)(2,1)}, u32[]{:S(2)}, u32[]{:S(2)}) collective-permute-start(bf16[2048,256]{1,0:T(8,128)(2,1)} %collective-permute-done.7.rest_1_.refs_11_.refs_14_), channel_id=1, source_target_pairs={{0,8},{8,16},{16,24},{1,9},{9,17},{17,25},{2,10},{10,18},{18,26},{... | collective-permute-start | bytes 3145736 | tf_op jit(solution)/shard_map/ppermute | solution.py:634
  49.5 28.4 %collective-permute-start.4 = (bf16[8192,256]{1,0:T(8,128)(2,1)}, bf16[8192,256]{1,0:T(8,128)(2,1)}, u32[]{:S(2)}, u32[]{:S(2)}) collective-permute-start(bf16[8192,256]{1,0:T(8,128)(2,1)} %join.1), channel_id=1, source_target_pairs={{0,1},{1,0},{2,3},{3,2},{4,5},{5,4},{6,7},{7,6},{8,9},{9,8},{10,11... | collective-permute-start | bytes 12582920 | tf_op jit(solution)/shard_map/ppermute | solution.py:647
  58.0 14.7 %copy-start.1 = (s32[256]{0:T(256)S(1)}, s32[256]{0:T(256)}, u32[]{:S(2)}) copy-start(s32[256]{0:T(256)} %get-tuple-element.19) | copy-start | bytes 3076
  58.0 15.5 %copy-start = (s32[256]{0:T(256)S(1)}, s32[256]{0:T(256)}, u32[]{:S(2)}) copy-start(s32[256]{0:T(256)} %get-tuple-element.20) | copy-start | bytes 3076
  66.7 52.7 %all-to-all-start.1 = ((bf16[8,2048,128]{2,1,0:T(8,128)(2,1)}), bf16[8,2048,128]{2,1,0:T(8,128)(2,1)}, u32[]{:S(2)}, u32[]{:S(2)}) async-start(bf16[8,2048,128]{2,1,0:T(8,128)(2,1)} %hold.3), calls=%async_computation.1 | async-start | bytes 8388608 | tf_op jit(solution)/shard_map/all_to_all | solution.py:654
  90.9 10.6 %collective-permute-start.10 = (f32[3,2048,256]{2,1,0:T(8,128)}, f32[3,2048,256]{2,1,0:T(8,128)}, u32[]{:S(2)}, u32[]{:S(2)}) collective-permute-start(f32[3,2048,256]{2,1,0:T(8,128)} %far.6.rest_3_), channel_id=1, source_target_pairs={{0,1},{1,0},{2,3},{3,2},{4,5},{5,4},{6,7},{7,6},{8,9},{9,8},{10,11... | collective-permute-start | bytes 18874376 | tf_op jit(solution)/shard_map/ppermute | solution.py:711
  97.9 72.3 %collective-permute-start.13 = (bf16[2048,256]{1,0:T(8,128)(2,1)}, bf16[2048,256]{1,0:T(8,128)(2,1)}, u32[]{:S(2)}, u32[]{:S(2)}) collective-permute-start(bf16[2048,256]{1,0:T(8,128)(2,1)} %mirror.3.refs_12_), channel_id=1, source_target_pairs={{0,16},{8,24},{16,0},{24,8},{1,17},{9,25},{17,1},{25,9},{2,18},{10... | collective-permute-start | bytes 3145736 | tf_op jit(solution)/shard_map/ppermute | solution.py:689
  125.9 8.0 %collective-permute-start.11 = (bf16[3,2048,256]{2,1,0:T(8,128)(2,1)}, bf16[3,2048,256]{2,1,0:T(8,128)(2,1)}, u32[]{:S(2)}, u32[]{:S(2)}) collective-permute-start(bf16[3,2048,256]{2,1,0:T(8,128)(2,1)} %far.8.rest_3_), channel_id=1, source_target_pairs={{0,1},{1,0},{2,3},{3,2},{4,5},{5,4},{6,7},{7,6},{8,9},{9,8},{10,11... | collective-permute-start | bytes 9437192 | tf_op jit(solution)/shard_map/ppermute | solution.py:711
  132.3 45.0 %collective-permute-start.14 = (bf16[2048,256]{1,0:T(8,128)(2,1)}, bf16[2048,256]{1,0:T(8,128)(2,1)}, u32[]{:S(2)}, u32[]{:S(2)}) collective-permute-start(bf16[2048,256]{1,0:T(8,128)(2,1)} %mirror.4.refs_14_), channel_id=1, source_target_pairs={{0,8},{8,16},{16,24},{24,0},{1,9},{9,17},{17,25},{25,1},{2,10},{10... | collective-permute-start | bytes 3145736 | tf_op jit(solution)/shard_map/ppermute | solution.py:689
  142.6 52.9 %all-to-all-start.2 = ((bf16[4,2048,256]{2,1,0:T(8,128)(2,1)}), bf16[4,2048,256]{2,1,0:T(8,128)(2,1)}, u32[]{:S(2)}, u32[]{:S(2)}) async-start(bf16[4,2048,256]{2,1,0:T(8,128)(2,1)} %far.9.refs_17_.rest_3_), calls=%async_computation.2 | async-start | bytes 8388608 | tf_op jit(solution)/shard_map/all_to_all | solution.py:742
  153.4 9.2 %collective-permute-start.12 = (f32[1,2048,256]{2,1,0:T(8,128)}, f32[1,2048,256]{2,1,0:T(8,128)}, u32[]{:S(2)}, u32[]{:S(2)}) collective-permute-start(f32[1,2048,256]{2,1,0:T(8,128)} %far.10), channel_id=1, source_target_pairs={{0,1},{1,0},{2,3},{3,2},{4,5},{5,4},{6,7},{7,6},{8,9},{9,8},{10,11... | collective-permute-start | bytes 6291464 | tf_op jit(solution)/shard_map/ppermute | solution.py:711
  160.1 31.7 %collective-permute-start.15 = (bf16[2048,256]{1,0:T(8,128)(2,1)}, bf16[2048,256]{1,0:T(8,128)(2,1)}, u32[]{:S(2)}, u32[]{:S(2)}) collective-permute-start(bf16[2048,256]{1,0:T(8,128)(2,1)} %mirror.5.refs_18_), channel_id=1, source_target_pairs={{0,24},{8,0},{16,8},{24,16},{1,25},{9,1},{17,9},{25,17},{2,26},{10... | collective-permute-start | bytes 3145736 | tf_op jit(solution)/shard_map/ppermute | solution.py:689
  210.5 4.0 collective-permute-start.16
  214.4 4.8 %collective-permute-start.17 = (f32[32,256]{1,0:T(8,128)S(1)}, f32[32,256]{1,0:T(8,128)S(1)}, u32[]{:S(2)}, u32[]{:S(2)}) collective-permute-start(f32[32,256]{1,0:T(8,128)S(1)} %add.314), channel_id=1, source_target_pairs={{0,16},{8,24},{16,0},{24,8},{1,17},{9,25},{17,1},{25,9},{2,18},{10... | collective-permute-start | bytes 98312 | tf_op jit(solution)/shard_map/ppermute | solution.py:569
